TPU v7x, 32 devices: a whole 2x2x4 slice. The times are simulated.
32 devices in a mesh: groups: 2 (over y), chan: 4 (over z), tm: 2 (over x), sub: 2 (over core).
Axes of the slice: x: 2, y: 2, z: 4, core: 2. Of those that a mesh axis runs over, the one named last changes fastest.
Arguments:
- traces: float32 [2048, 8192], P(('groups', 'chan', 'sub'), 'tm'), parts along dimension 0, may hold values from -6 to 6
- filters: float32 [2048, 65], P(('groups', 'chan', 'sub')), parts along dimension 0, may hold values from -0.75 to 0.75
- sources: int32 [256], P('groups'), parts along dimension 0, may hold values from 0 to 1023, as said below
Outputs:
- corr: float32 [128, 129, 2048], P('tm', None, ('groups', 'chan', 'sub')), parts along dimension 2
There are 2 independent parts, one for each index of `groups`. A program takes and returns all parts, laid end to end along the dimension named above; each array names one. Nothing has to cross between parts.
Inputs may be any that keep to these rules, and one draw needn't show every extreme that they name: `sources`: the 128 partner channels are distinct. No block of 128 consecutive channels starting at a multiple of 128 holds more than 16 of them, and some block holds exactly 16.
All inputs are finite; a program needn't handle non-finite values.
Results may differ from a plain program's by a relative error of at most 0.0033.
Values may be sent and summed in bfloat16 or wider, within the bound.
No kernel may reach another device: no remote copies, remote signals or barrier semaphores. Data moves between devices by JAX's collectives and lax.ppermute only.
A program may use at most 64 MiB of HBM per device.

v0:
```python
import math

import jax
import jax.numpy as jnp
from jax import lax
from jax.sharding import PartitionSpec as P

LAGS = 129


def padded_2(block, sides, width):
    for axis, dim in sides:
        count = lax.axis_size(axis)
        forward = [(i, i + 1) for i in range(count - 1)]
        backward = [(target, source) for source, target in forward]
        low = lax.ppermute(
            lax.slice_in_dim(block, block.shape[dim] - width, None, axis=dim), axis, forward
        )
        high = lax.ppermute(lax.slice_in_dim(block, 0, width, axis=dim), axis, backward)
        block = jnp.concatenate([low, block, high], axis=dim)
    return block


def whiten(extended, filters, out_len):
    running = jnp.zeros((extended.shape[0], out_len), jnp.float32)
    for k in range(filters.shape[1]):
        running = running + filters[:, k : k + 1] * extended[:, k : k + out_len]
    return running


def correlate(padded_seg, part_rows):
    seg_len = part_rows.shape[1]
    block_len = min(512, seg_len)
    block_count = seg_len // block_len

    def advance(block_index, summed):
        offset = block_index * block_len
        window = lax.dynamic_slice_in_dim(padded_seg, offset, block_len + LAGS - 1, 1)
        rows_here = lax.dynamic_slice_in_dim(part_rows, offset, block_len, 1)
        term = lax.conv_general_dilated(
            window[:, None, :],
            rows_here[:, None, :],
            (1,),
            "VALID",
            dimension_numbers=("NCH", "OIH", "NCH"),
            preferred_element_type=jnp.float32,
        )
        return summed + term

    start_sum = jnp.zeros((padded_seg.shape[0], part_rows.shape[0], LAGS), jnp.float32)
    return lax.fori_loop(0, block_count, advance, start_sum)


def on_device(traces, filters, sources):
    chan_dev, seg_len = traces.shape
    taps = filters.shape[1]
    half_taps = (taps - 1) // 2
    half_lags = (LAGS - 1) // 2
    partner_count = sources.shape[0]
    time_devs = lax.axis_size("tm")
    extended = padded_2(traces, (("tm", 1),), half_taps + half_lags)
    whitened_ext = whiten(extended, filters, seg_len + 2 * half_lags)
    position = (
        lax.axis_index("tm") * seg_len
        - half_lags
        + jnp.arange(seg_len + 2 * half_lags, dtype=jnp.int32)
    )
    inside = (position >= 0) & (position < seg_len * time_devs)
    padded = jnp.where(inside[None, :], whitened_ext, 0.0).astype(jnp.bfloat16)
    whitened = padded[:, half_lags : half_lags + seg_len]
    my_block = lax.axis_index(("chan", "sub"))
    owners = sources // chan_dev
    within = sources % chan_dev
    is_mine = owners == my_block
    chan_ids = jnp.arange(chan_dev, dtype=jnp.int32)
    slot_most = min(chan_dev, partner_count // 8)
    order_ids = jnp.arange(partner_count, dtype=jnp.int32)
    same_owner = owners[:, None] == owners[None, :]
    earlier = order_ids[None, :] < order_ids[:, None]
    rank_in = jnp.sum((same_owner & earlier).astype(jnp.int32), axis=1)
    choose = (
        (rank_in[None, :] == jnp.arange(slot_most, dtype=jnp.int32)[:, None]) & is_mine[None, :]
    ).astype(jnp.bfloat16)
    onehot = (within[:, None] == chan_ids[None, :]).astype(jnp.bfloat16)
    picker = jnp.dot(choose, onehot, preferred_element_type=jnp.float32).astype(jnp.bfloat16)
    slot_rows = jnp.dot(picker, whitened, preferred_element_type=jnp.float32).astype(jnp.bfloat16)
    slot_id = owners * slot_most + rank_in
    segment = lax.all_gather(slot_rows, ("chan", "sub"), axis=0, tiled=True)
    row_count = segment.shape[0]
    select = (slot_id[:, None] == jnp.arange(row_count, dtype=jnp.int32)[None, :]).astype(
        jnp.bfloat16
    )
    partners = jnp.dot(select, segment, preferred_element_type=jnp.float32).astype(jnp.bfloat16)
    norm_scale = 1.0 / math.sqrt(seg_len * time_devs)
    summed = correlate(padded, partners)
    return lax.psum_scatter(
        jnp.transpose(summed[:, :, ::-1], (1, 2, 0)) * norm_scale,
        "tm",
        scatter_dimension=0,
        tiled=True,
    )


def solution(mesh):
    return jax.shard_map(
        on_device,
        mesh=mesh,
        in_specs=(
            P(("groups", "chan", "sub"), "tm"),
            P(("groups", "chan", "sub"), None),
            P("groups"),
        ),
        out_specs=P("tm", None, ("groups", "chan", "sub")),
        check_vma=False,
    )
```

profile of v0, /device:TPU:0, one launch (start us, length us, event | category | flops | bytes accessed | tf_op | source)
XLA Modules:
  0.0 404.1 jit_solution(17135391241325937660)
XLA Ops:
  6.5 1.0 fusion.81
  7.5 1.3 collective-permute-start.1
  8.8 4.8 %collective-permute-start = (f32[128,96]{1,0:T(8,128)S(1)}, f32[128,96]{1,0:T(8,128)S(1)}, u32[]{:S(2)}, u32[]{:S(2)}) collective-permute-start(f32[128,96]{1,0:T(8,128)S(1)} %get-tuple-element.115), channel_id=1, source_target_pairs={{0,2},{1,3},{4,6},{5,7},{8,10},{9,11},{12,14},{13,15},{16,18},{17,... | collective-permute-start | bytes 147464 | tf_op jit(solution)/shard_map/ppermute | solution.py:16
  14.5 1.0 slice_bitcast_fusion.63
  15.5 1.0 slice_bitcast_fusion.64
  16.5 1.0 slice_bitcast_fusion.62
  19.1 2.9 concatenate.3
  22.1 42.9 %fusion.2 = bf16[128,4224]{1,0:T(8,128)(2,1)} fusion(f32[128,4288]{1,0:T(8,128)S(1)} %concatenate.3, f32[128]{0:T(128)S(1)} %get-tuple-element.179, f32[128]{0:T(128)S(1)} %get-tuple-element.180, f32[128]{0:T(128)S(1)} %get-tuple-element.117, f32[128]{0:T(128)S(1)} %get-tuple-element.118, f32[128]{0:T(128)S(1)} %get-tuple-element.119, ...), kind=kLoop, calls=%fused_computation.9 | loop fusion | flops 70828032 | bytes 141693568 | tf_op jit(solution)/shard_map/convert_element_type | solution.py:69
  65.0 2.4 convolution_convert_fusion.1
  67.6 23.5 %all-gather.2.cloned.1.call-done = bf16[128,4096]{1,0:T(8,128)(2,1)} async-done(((bf16[16,4096]{1,0:T(8,128)(2,1)}), bf16[128,4096]{1,0:T(8,128)(2,1)}) %all-gather.2.cloned.1.call-update) | async-done | bytes 1048592 | tf_op jit(solution)/shard_map/all_gather | solution.py:88
  91.1 2.8 convolution_convert_fusion
  93.9 186.1 %while.14 = (s32[]{:T(128)}, f32[128,128,129]{1,0,2:T(8,128)}, bf16[128,4224]{1,0:T(8,128)(2,1)}, bf16[128,4096]{1,0:T(8,128)(2,1)}, s32[]{:T(128)}, /*index=5*/s32[]{:T(128)}, s32[]{:T(128)}, s32[]{:T(128)}, s32[]{:T(128)}) while((s32[]{:T(128)}, f32[128,128,129]{1,0,2:T(8,128)}, bf16[128,4224]{1,0:T(8,128)(2,1)}, ...), condition=%wide.region_2.3_spmd.clone, body=%wide.region_1.2_spmd.clone.sunk | while | flops 2168487936 | bytes 18383036 | solution.py:51
  95.0 0.9 dynamic-slice_bitcast_fusion.4
  96.1 19.1 %select_add_fusion.2 = f32[128,128,129]{1,0,2:T(8,128)} fusion(f32[128,128,129]{1,0,2:T(8,128)} %get-tuple-element.216, pred[]{:T(512)S(6)} %compare.6, bf16[128,1,640]{0,1,2:T(2,128)(2,1)S(1)} %copy.17, bf16[128,1,512]{0,1,2:T(2,128)(2,1)S(1)} %copy.18), kind=kOutput, calls=%fused_computation.clone.1 | convolution fusion | flops 2168487936 | bytes 17203200 | tf_op jit(solution)/shard_map/while/body/eval_jaxpr/conv_general_dilated | solution.py:40
  117.5 21.3 %select_add_fusion.2 = f32[128,128,129]{1,0,2:T(8,128)} fusion(f32[128,128,129]{1,0,2:T(8,128)} %get-tuple-element.216, pred[]{:T(512)S(6)} %compare.6, bf16[128,1,640]{0,1,2:T(2,128)(2,1)S(1)} %copy.17, bf16[128,1,512]{0,1,2:T(2,128)(2,1)S(1)} %copy.18), kind=kOutput, calls=%fused_computation.clone.1 | convolution fusion | flops 2168487936 | bytes 17203200 | tf_op jit(solution)/shard_map/while/body/eval_jaxpr/conv_general_dilated | solution.py:40
  141.0 21.3 %select_add_fusion.2 = f32[128,128,129]{1,0,2:T(8,128)} fusion(f32[128,128,129]{1,0,2:T(8,128)} %get-tuple-element.216, pred[]{:T(512)S(6)} %compare.6, bf16[128,1,640]{0,1,2:T(2,128)(2,1)S(1)} %copy.17, bf16[128,1,512]{0,1,2:T(2,128)(2,1)S(1)} %copy.18), kind=kOutput, calls=%fused_computation.clone.1 | convolution fusion | flops 2168487936 | bytes 17203200 | tf_op jit(solution)/shard_map/while/body/eval_jaxpr/conv_general_dilated | solution.py:40
  164.6 21.3 %select_add_fusion.2 = f32[128,128,129]{1,0,2:T(8,128)} fusion(f32[128,128,129]{1,0,2:T(8,128)} %get-tuple-element.216, pred[]{:T(512)S(6)} %compare.6, bf16[128,1,640]{0,1,2:T(2,128)(2,1)S(1)} %copy.17, bf16[128,1,512]{0,1,2:T(2,128)(2,1)S(1)} %copy.18), kind=kOutput, calls=%fused_computation.clone.1 | convolution fusion | flops 2168487936 | bytes 17203200 | tf_op jit(solution)/shard_map/while/body/eval_jaxpr/conv_general_dilated | solution.py:40
  188.1 21.3 %select_add_fusion.2 = f32[128,128,129]{1,0,2:T(8,128)} fusion(f32[128,128,129]{1,0,2:T(8,128)} %get-tuple-element.216, pred[]{:T(512)S(6)} %compare.6, bf16[128,1,640]{0,1,2:T(2,128)(2,1)S(1)} %copy.17, bf16[128,1,512]{0,1,2:T(2,128)(2,1)S(1)} %copy.18), kind=kOutput, calls=%fused_computation.clone.1 | convolution fusion | flops 2168487936 | bytes 17203200 | tf_op jit(solution)/shard_map/while/body/eval_jaxpr/conv_general_dilated | solution.py:40
  211.6 21.3 %select_add_fusion.2 = f32[128,128,129]{1,0,2:T(8,128)} fusion(f32[128,128,129]{1,0,2:T(8,128)} %get-tuple-element.216, pred[]{:T(512)S(6)} %compare.6, bf16[128,1,640]{0,1,2:T(2,128)(2,1)S(1)} %copy.17, bf16[128,1,512]{0,1,2:T(2,128)(2,1)S(1)} %copy.18), kind=kOutput, calls=%fused_computation.clone.1 | convolution fusion | flops 2168487936 | bytes 17203200 | tf_op jit(solution)/shard_map/while/body/eval_jaxpr/conv_general_dilated | solution.py:40
  235.2 21.3 %select_add_fusion.2 = f32[128,128,129]{1,0,2:T(8,128)} fusion(f32[128,128,129]{1,0,2:T(8,128)} %get-tuple-element.216, pred[]{:T(512)S(6)} %compare.6, bf16[128,1,640]{0,1,2:T(2,128)(2,1)S(1)} %copy.17, bf16[128,1,512]{0,1,2:T(2,128)(2,1)S(1)} %copy.18), kind=kOutput, calls=%fused_computation.clone.1 | convolution fusion | flops 2168487936 | bytes 17203200 | tf_op jit(solution)/shard_map/while/body/eval_jaxpr/conv_general_dilated | solution.py:40
  258.7 21.3 %select_add_fusion.2 = f32[128,128,129]{1,0,2:T(8,128)} fusion(f32[128,128,129]{1,0,2:T(8,128)} %get-tuple-element.216, pred[]{:T(512)S(6)} %compare.6, bf16[128,1,640]{0,1,2:T(2,128)(2,1)S(1)} %copy.17, bf16[128,1,512]{0,1,2:T(2,128)(2,1)S(1)} %copy.18), kind=kOutput, calls=%fused_computation.clone.1 | convolution fusion | flops 2168487936 | bytes 17203200 | tf_op jit(solution)/shard_map/while/body/eval_jaxpr/conv_general_dilated | solution.py:40
  280.0 9.0 %copy.14 = f32[128,128,129]{0,1,2:T(8,128)} copy(f32[128,128,129]{1,0,2:T(8,128)} %get-tuple-element.84) | data formatting | bytes 16908288 | tf_op jit(solution)/shard_map/while | solution.py:51
  289.0 8.5 %multiply_bitcast_fusion = f32[128,129,128]{2,0,1:T(8,128)} fusion(f32[128,128,129]{0,1,2:T(8,128)} %copy.14), kind=kLoop, calls=%fused_computation.3 | loop fusion | flops 2113536 | bytes 16908288 | tf_op jit(solution)/shard_map/mul | solution.py:97
  297.5 99.7 %reduce-scatter.2.cloned.1.call-done = f32[64,129,128]{2,0,1:T(8,128)} async-done(((f32[128,129,128]{2,0,1:T(8,128)}), f32[64,129,128]{2,0,1:T(8,128)}) %reduce-scatter.2.cloned.1.call-update) | async-done | bytes 4227088 | tf_op jit(solution)/shard_map/reduce_scatter | solution.py:96
  (44 shorter events, 19.5 us)
Async XLA Ops:
  6.5 84.6 %all-gather.2.cloned.1.call-start = ((), (), s32[]{:S(2)}) async-start(), calls=%async_computation.1 | async-start | bytes 1179648 | tf_op jit(solution)/shard_map/all_gather | solution.py:88
  7.5 11.6 %collective-permute-start.1 = (f32[128,96]{1,0:T(8,128)S(1)}, f32[128,96]{1,0:T(8,128)S(1)}, u32[]{:S(2)}, u32[]{:S(2)}) collective-permute-start(f32[128,96]{1,0:T(8,128)S(1)} %get-tuple-element.114), channel_id=1, source_target_pairs={{2,0},{3,1},{6,4},{7,5},{10,8},{11,9},{14,12},{15,13},{18,16},{19,... | collective-permute-start | bytes 147464 | tf_op jit(solution)/shard_map/ppermute | solution.py:19
  8.8 10.3 %collective-permute-start = (f32[128,96]{1,0:T(8,128)S(1)}, f32[128,96]{1,0:T(8,128)S(1)}, u32[]{:S(2)}, u32[]{:S(2)}) collective-permute-start(f32[128,96]{1,0:T(8,128)S(1)} %get-tuple-element.115), channel_id=1, source_target_pairs={{0,2},{1,3},{4,6},{5,7},{8,10},{9,11},{12,14},{13,15},{16,18},{17,... | collective-permute-start | bytes 147464 | tf_op jit(solution)/shard_map/ppermute | solution.py:16
  67.4 329.9 %reduce-scatter.2.cloned.1.call-start = ((), (), s32[]{:S(2)}) async-start(), calls=%async_computation.2 | async-start | bytes 12681216 | tf_op jit(solution)/shard_map/reduce_scatter | solution.py:96
Sparse Core Ops, SparseCore 0:
  67.5 23.5 all-gather.1
  297.7 99.5 reduce-scatter.1
where the time goes:
time: 405 us; the launch traced here: 404 us
  matrix products  173 us (43%)
  waiting for transfers between devices  123 us (30%)
  other arithmetic  52.9 us (13%)
  local copies, waits for them, and re-layouts  34.5 us (9%)
  between operations  13.5 us (3%)
  starting transfers between devices  6.36 us (2%)
    conv_general_dilated x8, matrix products, advance(): lax.conv_general_dilated(window[:, None, :], rows_here[:, None, :], (1,),...  168 us
    reduce_scatter x1, waiting for transfers between devices, on_device(): lax.psum_scatter(jnp.transpose(summed[:, :, ::-1], (1, 2, 0)) * norm_scal...  99.7 us
    convert_element_type x1, other arithmetic, on_device(): padded = jnp.where(inside[None, :], whitened_ext, 0.0).astype(jnp.bfloat16)  42.9 us
    all_gather x1, waiting for transfers between devices, on_device(): segment = lax.all_gather(slot_rows, ('chan', 'sub'), axis=0, tiled=True)  23.5 us
    broadcast_in_dim x16, local copies, waits for them, and re-layouts, advance(): window[:, None, :]  9.16 us
    while x1, local copies, waits for them, and re-layouts, correlate(): return lax.fori_loop(0, block_count, advance, start_sum)  9 us
    broadcast_in_dim x16, local copies, waits for them, and re-layouts, advance(): rows_here[:, None, :]  8.59 us
    mul x1, other arithmetic, on_device(): jnp.transpose(summed[:, :, ::-1], (1, 2, 0)) * norm_scale  8.51 us
  transfers between devices with their start and end apart: 4, of which 2 were waited for; matrix products, arithmetic and copies ran while one was open for 1% of the time, Pallas kernels for 0%

commit v1 on v0

v1 whole, which is shorter than its diff:
```python
import functools
import math

import jax
import jax.numpy as jnp
from jax import lax
from jax.experimental import pallas as pl
from jax.experimental.pallas import tpu as pltpu
from jax.sharding import PartitionSpec as P

LAGS = 129
MOST = 16
TILE = 128
FINE = 16
F32 = jnp.float32
BF16 = jnp.bfloat16
VMEM_BYTES = 56 * 2**20


def vmem(count):
    return [pl.BlockSpec(memory_space=pltpu.VMEM)] * count


SMEM = pl.BlockSpec(memory_space=pltpu.SMEM)
ANY = pl.BlockSpec(memory_space=pl.ANY)


def params():
    return pltpu.CompilerParams(vmem_limit_bytes=VMEM_BYTES)


def cost(flops, moved):
    return pl.CostEstimate(flops=int(flops), bytes_accessed=int(moved), transcendentals=0)


def fir(samples, taps_ref, taps, base, rows):
    total = None
    for first in range(8):
        later = [j for j in range((taps + 7) // 8) if first + 8 * j < taps]
        window = samples[pl.ds(base + first, rows + 8 * later[-1]), :]
        for j in later:
            k = first + 8 * j
            term = taps_ref[k : k + 1, :] * window[8 * j : 8 * j + rows]
            total = term if total is None else total + term
    return total


def slots_kernel(taps, sources, info, x, low, high, filters, out, rows, wide, tall, chan_taps, lane_taps):
    chans, length = x.shape
    slots = out.shape[0]
    segs = TILE // slots
    seg_len = length // segs
    half = (taps - 1) // 2
    for s in range(slots):
        rows[s] = 0

    def find(p, count):
        local = sources[p] - info[0] * chans
        mine = (local >= 0) & (local < chans)
        rows[jnp.where(mine, count, slots)] = local
        return count + mine.astype(jnp.int32)

    lax.fori_loop(0, sources.shape[0], find, 0, unroll=8)
    lane_taps[0:taps, :chans] = filters[...]
    chan_taps[...] = lane_taps[:, :chans].T
    keep_low = (info[1] > 0).astype(F32)
    keep_high = (info[2] > 0).astype(F32)
    for s in range(slots):
        row = rows[s]
        group = pl.multiple_of((row >> 3) << 3, 8)
        turn = (s - row) & 7

        def pick(ref):
            return pltpu.roll(ref[pl.ds(group, 8), :], turn, 0)[s % 8 : s % 8 + 1, :]

        wide[s : s + 1, 0:TILE] = pick(low) * keep_low
        wide[s : s + 1, TILE : TILE + length] = pick(x)
        wide[s : s + 1, TILE + length :] = pick(high) * keep_high
        lane_taps[s : s + 1, :] = pick(chan_taps)
    picked = lane_taps[0:slots, :]
    lane_taps[...] = jnp.concatenate([picked] * segs, 0).T
    for t in range(seg_len // TILE + 2):
        cols = [wide[:, g * seg_len + t * TILE : g * seg_len + (t + 1) * TILE] for g in range(segs)]
        tall[t * TILE : (t + 1) * TILE, :] = jnp.concatenate(cols, 0).T
    for t in range(seg_len // TILE):
        done = fir(tall, lane_taps, taps, (t + 1) * TILE - half, TILE).T
        for g in range(segs):
            start = g * seg_len + t * TILE
            out[:, start : start + TILE] = done[g * slots : (g + 1) * slots].astype(BF16)


def whiten_slots(sources, info, traces, low, high, filters, slots):
    chans, length = traces.shape
    taps = filters.shape[0]
    seg_len = length * slots // TILE
    return pl.pallas_call(
        functools.partial(slots_kernel, taps),
        out_shape=jax.ShapeDtypeStruct((slots, length), BF16),
        in_specs=[SMEM, SMEM] + vmem(4),
        out_specs=vmem(1)[0],
        scratch_shapes=[
            pltpu.SMEM((slots + 1,), jnp.int32),
            pltpu.VMEM((slots, length + 2 * TILE), F32),
            pltpu.VMEM((seg_len + 2 * TILE, TILE), F32),
            pltpu.VMEM((chans, TILE), F32),
            pltpu.VMEM((TILE, TILE), F32),
        ],
        compiler_params=params(),
        cost_estimate=cost(2 * slots * length * taps, 4 * chans * length),
        name="whiten_slots",
    )(sources, info, traces, low, high, filters)


def whiten_kernel(taps, rows, info, x, low, high, filters, out, tall):
    length = x.shape[1]
    half = (taps - 1) // 2
    tall[0:TILE, :] = jnp.where(info[1] > 0, low[...], 0.0).T
    tall[TILE + length :, :] = jnp.where(info[2] > 0, high[...], 0.0).T

    def turn(t, carry):
        start = pl.multiple_of(t * TILE, TILE)
        tall[pl.ds(start + TILE, TILE), :] = x[:, pl.ds(start, TILE)].T
        return carry

    lax.fori_loop(0, length // TILE, turn, 0, unroll=4)

    def block(i, carry):
        start = pl.multiple_of(i * rows, rows)
        out[pl.ds(start, rows), :] = fir(tall, filters, taps, start + TILE - half, rows).astype(BF16)
        return carry

    lax.fori_loop(0, length // rows, block, 0)


def whiten(info, traces, low, high, filters):
    chans, length = traces.shape
    taps = filters.shape[0]
    return pl.pallas_call(
        functools.partial(whiten_kernel, taps, 2 * TILE),
        out_shape=jax.ShapeDtypeStruct((length, chans), BF16),
        in_specs=[SMEM] + vmem(4),
        out_specs=vmem(1)[0],
        scratch_shapes=[pltpu.VMEM((length + 2 * TILE, chans), F32)],
        compiler_params=params(),
        cost_estimate=cost(2 * chans * length * taps, 6 * chans * length),
        name="whiten",
    )(info, traces, low, high, filters)


def order_kernel(chans, sizes, ring, count, lead, send_rows, info, sources, *refs):
    parts, outs = refs[:count], refs[count : -2]
    slots_ref, choose = refs[-2:]
    partners = sources.shape[1]
    chan_devs, sub_devs = sizes
    slots = parts[0].shape[0] if ring else MOST
    own_row = jnp.broadcast_to(sources[...].astype(F32), (partners, partners))
    owner_row = jnp.floor((own_row + 0.5) * (1.0 / chans))
    owner_col = owner_row.T
    lane = lax.broadcasted_iota(jnp.int32, (partners, partners), 1)
    line = lax.broadcasted_iota(jnp.int32, (partners, partners), 0)
    earlier = (owner_row == owner_col) & (lane < line)
    rank = jnp.sum(earlier.astype(F32), axis=1, keepdims=True)
    owner = owner_col[:, 0:1]
    if ring:
        owner_chan = jnp.floor((owner + 0.5) * (1.0 / sub_devs))
        owner_sub = owner - sub_devs * owner_chan
        my_chan = info[3].astype(F32)
        my_sub = info[4].astype(F32)
        behind = my_chan - owner_chan
        behind = jnp.where(behind < 0, behind + chan_devs, behind)
        place = jnp.where(owner_sub == my_sub, 0.0, 1.0) * chan_devs + behind
    else:
        place = owner
    row = place * slots + rank
    total = slots_ref.shape[0]
    at = lax.broadcasted_iota(jnp.int32, (partners, total), 1).astype(F32)
    choose[...] = (row == at).astype(F32)
    step = total // count
    for i, part in enumerate(parts):
        slots_ref[i * step : (i + 1) * step, :] = part[...]
    if not ring:
        outs[0][...] = jnp.dot(choose[...].astype(BF16), slots_ref[...], preferred_element_type=F32).astype(BF16)
        return
    own, send = outs
    half = own.shape[0]
    mine = choose[pl.ds(pl.multiple_of(info[5] * half, half), half), :]
    other = (1 - info[5]) * half + info[4] * send_rows
    theirs = choose[pl.ds(pl.multiple_of(other, send_rows), send_rows), :]
    wanted = jnp.concatenate([mine, theirs], 0).astype(BF16)
    length = send.shape[1]
    got = jnp.dot(wanted, slots_ref[...], preferred_element_type=F32).astype(BF16)
    own[:, 0:lead] = jnp.zeros((half, lead), BF16)
    own[:, lead + length :] = jnp.zeros((half, lead), BF16)
    own[:, lead : lead + length] = got[:half]
    send[...] = got[half:]


def order(info, sources, parts, chans, sizes, ring):
    partners = sources.shape[0]
    length = parts[0].shape[1]
    total = sum(part.shape[0] for part in parts)
    if ring:
        half, send_rows = partners // 2, partners // 4
        out_shape = (
            jax.ShapeDtypeStruct((half, length + 2 * TILE), BF16),
            jax.ShapeDtypeStruct((send_rows, length), BF16),
        )
        out_specs = tuple(vmem(2))
    else:
        send_rows = 0
        out_shape = jax.ShapeDtypeStruct((partners, length), BF16)
        out_specs = vmem(1)[0]
    return pl.pallas_call(
        functools.partial(order_kernel, chans, sizes, ring, len(parts), TILE, send_rows),
        out_shape=out_shape,
        in_specs=[SMEM] + vmem(1 + len(parts)),
        out_specs=out_specs,
        scratch_shapes=[pltpu.VMEM((total, length), BF16), pltpu.VMEM((partners, total), F32)],
        compiler_params=params(),
        cost_estimate=cost(2 * partners * total * length, 4 * total * length),
        name="order_partners",
    )(info, sources.reshape(1, partners), *parts)


def lay_out(part, out, start, width):
    rows = part.shape[0]
    lane = lax.broadcasted_iota(jnp.int32, (rows, TILE), 1)
    tiles = [part[:, pl.ds(start + TILE * i, TILE)] for i in range(width // TILE + 1)]
    half = (LAGS - 1) // 2
    for b in range(FINE + 1):
        turned = [pltpu.roll(tile, half - b, 1) for tile in tiles]
        for i in range(width // TILE):
            piece = jnp.where(lane < half - b, turned[i], turned[i + 1])
            out[b * rows : (b + 1) * rows, TILE * i : TILE * i + TILE] = piece


def add_lags(shifted, chan, total, start, width, rows):
    chans = chan.shape[1]
    coarse = (LAGS - 1) // FINE
    pair = 2 if chans % TILE == 0 else 1
    for a in range(0, coarse, pair):
        cols = [chan[pl.ds(start + TILE - FINE * (a + i), width), :] for i in range(pair)]
        last = a + pair == coarse
        used = rows * (FINE + 1 if last else FINE)
        block = cols[0] if pair == 1 else jnp.concatenate(cols, 1)
        term = jnp.dot(shifted[:used, :], block, preferred_element_type=F32)
        for i in range(pair):
            size = used if i == pair - 1 else rows * FINE
            place = (a + i) * FINE * rows
            total[place : place + size, :] += term[:size, i * chans : (i + 1) * chans]


def correlate_all(part, chan, total, spare, start, width, chunk, rows):
    first, second, rest = spare
    whole = width // (2 * chunk) * (2 * chunk)
    lay_out(part, first, start, chunk)

    def advance(i, carry):
        now = pl.multiple_of(start + 2 * chunk * i, TILE)
        lay_out(part, second, now + chunk, chunk)
        add_lags(first, chan, total, now, chunk, rows)
        after = pl.multiple_of(jnp.minimum(now + 2 * chunk, start + whole - chunk), TILE)
        lay_out(part, first, after, chunk)
        add_lags(second, chan, total, now + chunk, chunk, rows)
        return carry

    lax.fori_loop(0, whole // (2 * chunk), advance, 0)
    if width > whole:
        lay_out(part, rest, start + whole, width - whole)
        add_lags(rest, chan, total, start + whole, width - whole, rows)


def first_kernel(chunk, info, part, chan_hbm, total, chan, a, b, c, sem):
    length = chan_hbm.shape[0]
    rows = part.shape[0]
    copy = pltpu.make_async_copy(chan_hbm, chan.at[pl.ds(TILE, length), :], sem)
    copy.start()
    edge = jnp.zeros((TILE, chan.shape[1]), BF16)
    chan[0:TILE, :] = edge
    chan[TILE + length :, :] = edge
    total[...] = jnp.zeros_like(total)
    copy.wait()
    start = pl.multiple_of(info[5] * TILE, TILE)
    correlate_all(part, chan, total, (a, b, c), start, length, chunk, rows)


def second_kernel(chunk, scale, info, own_part, parts_hbm, own_chan, chan_hbm, before, total, part, chan, a, b, c, sems):
    length = chan_hbm.shape[0]
    rows = part.shape[0]
    few = parts_hbm[0].shape[0]
    copies = [
        pltpu.make_async_copy(parts_hbm[0], part.at[pl.ds(pl.multiple_of(info[6], few), few), pl.ds(TILE, length)], sems.at[0]),
        pltpu.make_async_copy(parts_hbm[1], part.at[pl.ds(pl.multiple_of(info[7], few), few), pl.ds(TILE, length)], sems.at[1]),
        pltpu.make_async_copy(chan_hbm, chan.at[pl.ds(TILE, length), :], sems.at[2]),
        pltpu.make_async_copy(before, total, sems.at[3]),
    ]
    for copy in copies:
        copy.start()
    later = info[5] > 0
    part[:, 0:TILE] = jnp.where(later, 0, own_part[:, length : length + TILE]).astype(BF16)
    part[:, TILE + length :] = jnp.where(later, own_part[:, TILE : 2 * TILE], 0).astype(BF16)
    chan[0:TILE, :] = jnp.where(later, 0, own_chan[length - TILE :, :]).astype(BF16)
    chan[TILE + length :, :] = jnp.where(later, own_chan[0:TILE, :], 0).astype(BF16)
    for copy in copies:
        copy.wait()
    correlate_all(part, chan, total, (a, b, c), 0, length + TILE, chunk, rows)
    total[...] = total[...] * scale


def split_second(chunk, scale, info, own_part, low_part, high_part, own_chan, chan_hbm, before, *rest):
    second_kernel(chunk, scale, info, own_part, (low_part, high_part), own_chan, chan_hbm, before, *rest)


def whole_kernel(chunk, scale, part_in, chan_in, total, part, chan, a, b, c):
    length = chan_in.shape[0]
    rows = part.shape[0]
    part[:, 0:TILE] = jnp.zeros((rows, TILE), BF16)
    part[:, TILE + length :] = jnp.zeros((rows, TILE), BF16)
    part[:, TILE : TILE + length] = part_in[...]
    edge = jnp.zeros((TILE, chan.shape[1]), BF16)
    chan[0:TILE, :] = edge
    chan[TILE + length :, :] = edge
    chan[TILE : TILE + length, :] = chan_in[...]
    total[...] = jnp.zeros_like(total)
    correlate_all(part, chan, total, (a, b, c), 0, length + TILE, chunk, rows)
    total[...] = total[...] * scale


def spare(rows, chunk):
    return [pltpu.VMEM((rows * (FINE + 1), width), BF16) for width in (chunk, chunk, TILE)]


def shifted(array, axis, step):
    count = lax.axis_size(axis)
    return lax.ppermute(array, axis, [(i, (i + step) % count) for i in range(count)])


def on_device(traces, filters, sources):
    chans, length = traces.shape
    partners = sources.shape[0]
    time_devs, chan_devs, sub_devs = (lax.axis_size(axis) for axis in ("tm", "chan", "sub"))
    here_tm, here_chan, here_sub = (lax.axis_index(axis) for axis in ("tm", "chan", "sub"))
    slots = min(chans, MOST)
    rows = partners // time_devs
    few = rows // sub_devs
    scale = 1.0 / math.sqrt(length * time_devs)
    chunk = 4 * TILE
    info = jnp.stack(
        [
            here_chan * sub_devs + here_sub,
            (here_tm > 0).astype(jnp.int32),
            (here_tm < time_devs - 1).astype(jnp.int32),
            here_chan,
            here_sub,
            here_tm,
            here_sub * few,
            (1 - here_sub) * few,
        ]
    ).astype(jnp.int32)
    taps = filters.T
    ring = time_devs == 2 and sub_devs == 2 and chan_devs <= 4
    flops = 2 * rows * LAGS * chans * length
    out_shape = jax.ShapeDtypeStruct((LAGS * rows, chans), F32)
    if ring:
        edge = lax.dynamic_slice_in_dim(traces, jnp.where(here_tm == 0, length - TILE, 0), TILE, 1)
        low = high = shifted(edge, "tm", 1)
    else:
        low = lax.ppermute(traces[:, length - TILE :], "tm", [(i, i + 1) for i in range(time_devs - 1)])
        high = lax.ppermute(traces[:, :TILE], "tm", [(i + 1, i) for i in range(time_devs - 1)])
    picked = whiten_slots(sources, info, traces, low, high, taps, slots)
    whitened = whiten(info, traces, low, high, taps)
    sizes = (chan_devs, sub_devs)
    if ring:
        near = [picked] + [shifted(picked, "chan", step) for step in range(1, chan_devs)]
        far = [shifted(part, "sub", 1) for part in near]
        own_part, send = order(info, sources, near + far, chans, sizes, True)
        other_chan = shifted(whitened, "tm", 1)
        low_part = shifted(send, "tm", 1)
        high_part = shifted(low_part, "sub", 1)
        before = pl.pallas_call(
            functools.partial(first_kernel, chunk),
            out_shape=out_shape,
            in_specs=[SMEM] + vmem(1) + [ANY],
            out_specs=vmem(1)[0],
            scratch_shapes=[pltpu.VMEM((length + 2 * TILE, chans), BF16)]
            + spare(rows, chunk)
            + [pltpu.SemaphoreType.DMA],
            compiler_params=params(),
            cost_estimate=cost(flops, 8 * rows * LAGS * chans),
            name="correlate_own",
        )(info, own_part, whitened)
        total = pl.pallas_call(
            functools.partial(split_second, chunk, scale),
            out_shape=out_shape,
            in_specs=[SMEM] + vmem(1) + [ANY, ANY] + vmem(1) + [ANY, ANY],
            out_specs=vmem(1)[0],
            scratch_shapes=[
                pltpu.VMEM((rows, length + 2 * TILE), BF16),
                pltpu.VMEM((length + 2 * TILE, chans), BF16),
            ]
            + spare(rows, chunk)
            + [pltpu.SemaphoreType.DMA((4,))],
            compiler_params=params(),
            cost_estimate=cost(flops, 8 * rows * LAGS * chans),
            name="correlate_other",
        )(info, own_part, low_part, high_part, whitened, other_chan, before)
    else:
        gathered = lax.all_gather(picked, ("chan", "sub"), axis=0, tiled=True)
        all_parts = order(info, sources, [gathered], chans, sizes, False)
        parts = lax.all_to_all(all_parts, "tm", 0, 1, tiled=True)
        all_chans = lax.all_gather(whitened, "tm", axis=0, tiled=True)
        full = length * time_devs
        total = pl.pallas_call(
            functools.partial(whole_kernel, chunk, scale),
            out_shape=out_shape,
            in_specs=vmem(2),
            out_specs=vmem(1)[0],
            scratch_shapes=[
                pltpu.VMEM((rows, full + 2 * TILE), BF16),
                pltpu.VMEM((full + 2 * TILE, chans), BF16),
            ]
            + spare(rows, chunk),
            compiler_params=params(),
            name="correlate_whole",
        )(parts, all_chans)
    return jnp.transpose(total.reshape(LAGS, rows, chans), (1, 0, 2))


def solution(mesh):
    return jax.shard_map(
        on_device,
        mesh=mesh,
        in_specs=(
            P(("groups", "chan", "sub"), "tm"),
            P(("groups", "chan", "sub"), None),
            P("groups"),
        ),
        out_specs=P("tm", None, ("groups", "chan", "sub")),
        check_vma=False,
    )
```

time: 405 us -> 90.3 us (0.22)
  matrix products: 173 us -> 0 us
  waiting for transfers between devices: 123 us -> 22.8 us
  other arithmetic: 52.9 us -> 0 us
  Pallas kernels: 0 us -> 52.6 us
  local copies, waits for them, and re-layouts: 34.5 us -> 3.76 us
  between operations: 13.5 us -> 0.1 us
  starting transfers between devices: 6.36 us -> 10.6 us
    conv_general_dilated x8 -> x0, matrix products: 168 us -> none  [advance(): lax.conv_general_dilated(window[:, None, :], rows_here[:, None, :], (1,),...]
    reduce_scatter x1 -> x0, waiting for transfers between devices: 99.7 us -> none  [on_device(): lax.psum_scatter(jnp.transpose(summed[:, :, ::-1], (1, 2, 0)) * norm_scal...]
    pallas_call x0 -> x5, Pallas kernels: none -> 52.6 us  [the longest x1 17.1 us: on_device(): pl.pallas_call(functools.partial(split_second, chunk, scale), out_shape=o...]
    convert_element_type x1 -> x0, other arithmetic: 42.9 us -> none  [on_device(): padded = jnp.where(inside[None, :], whitened_ext, 0.0).astype(jnp.bfloat16)]
    all_gather x1 -> x0, waiting for transfers between devices: 23.5 us -> none  [on_device(): segment = lax.all_gather(slot_rows, ('chan', 'sub'), axis=0, tiled=True)]
    ppermute x2 -> x11, waiting for transfers between devices: 0.01 us -> 22.8 us  [shifted(): lax.ppermute(array, axis, [(i, (i + step) % count) for i in range(count)])]
    broadcast_in_dim x32 -> x0, local copies, waits for them, and re-layouts: 17.7 us -> none  [the longest x16 9.16 us: advance(): window[:, None, :]]
    while x1 -> x0, local copies, waits for them, and re-layouts: 9 us -> none  [correlate(): return lax.fori_loop(0, block_count, advance, start_sum)]
  transfers between devices with their start and end apart: 4 -> 11, of which waited for: 2 -> 6; matrix products, arithmetic and copies ran while one was open for 1% -> 1% of each run, Pallas kernels for 0% -> 31%
where the time goes in v1:
time: 90.3 us; the launch traced here: 89.9 us
  Pallas kernels  52.6 us (58%)
  waiting for transfers between devices  22.8 us (25%)
  starting transfers between devices  10.6 us (12%)
  local copies, waits for them, and re-layouts  3.76 us (4%)
    ppermute x11, waiting for transfers between devices, shifted(): lax.ppermute(array, axis, [(i, (i + step) % count) for i in range(count)])  22.8 us
    pallas_call x1, Pallas kernels, on_device(): pl.pallas_call(functools.partial(split_second, chunk, scale), out_shape=o...  17.1 us
    pallas_call x1, Pallas kernels, on_device(): pl.pallas_call(functools.partial(first_kernel, chunk), out_shape=out_shap...  14.5 us
    pallas_call x1, Pallas kernels, whiten(): pl.pallas_call(functools.partial(whiten_kernel, taps, 2 * TILE), out_shap...  13.2 us
    ppermute x11, starting transfers between devices, shifted(): lax.ppermute(array, axis, [(i, (i + step) % count) for i in range(count)])  10.6 us
    pallas_call x1, Pallas kernels, whiten_slots(): pl.pallas_call(functools.partial(slots_kernel, taps), out_shape=jax.Shape...  5.09 us
    pallas_call x1, Pallas kernels, order(): pl.pallas_call(functools.partial(order_kernel, chans, sizes, ring, len(pa...  2.78 us
    unnamed x22, local copies, waits for them, and re-layouts  2.25 us
  transfers between devices with their start and end apart: 11, of which 6 were waited for; matrix products, arithmetic and copies ran while one was open for 1% of the time, Pallas kernels for 31%

profile of v1, /device:TPU:0, one launch (start us, length us, event | category | flops | bytes accessed | tf_op | source)
XLA Modules:
  0.0 89.9 jit_solution(14119524163330201485)
XLA Ops:
  0.0 0.8 constant_dynamic-slice_fusion
  0.8 2.9 %collective-permute-start = (f32[128,128]{1,0:T(8,128)S(1)}, f32[128,128]{1,0:T(8,128)S(1)}, u32[]{:S(2)}, u32[]{:S(2)}) collective-permute-start(f32[128,128]{1,0:T(8,128)S(1)} %constant_dynamic-slice_fusion), channel_id=1, source_target_pairs={{0,2},{2,0},{1,3},{3,1},{4,6},{6,4},{5,7},{7,5},{8,10},{10,8},{9,1... | collective-permute-start | bytes 196616 | tf_op jit(solution)/shard_map/ppermute | solution.py:335
  3.8 0.7 stack.43.info
  4.5 1.6 %collective-permute-done.low.high = f32[128,128]{1,0:T(8,128)S(1)} collective-permute-done((f32[128,128]{1,0:T(8,128)S(1)}, f32[128,128]{1,0:T(8,128)S(1)}, u32[]{:S(2)}, u32[]{:S(2)}) %collective-permute-start) | collective-permute-done | bytes 65568 | tf_op jit(solution)/shard_map/ppermute | solution.py:335
  6.0 0.6 copy-done
  6.7 5.1 %whiten_slots.1.refs_0_ = bf16[16,4096]{1,0:T(8,128)(2,1)} custom-call(s32[128]{0:T(128)} %sources.1, s32[8]{0:T(128)} %stack.43.info, f32[128,4096]{1,0:T(8,128)} %x.3, f32[128,128]{1,0:T(8,128)} %copy-done, f32[128,128]{1,0:T(8,128)} %copy-done, f32[65,128]{1,0:T(8,128)} %bitcast.13), custom_call_target="tpu_custom_call" | custom-call | flops 8519680 | bytes 2097152 | tf_op jit(solution)/shard_map/whiten_slots/pallas_call | solution.py:96
  11.7 4.1 %collective-permute-start.3 = (bf16[16,4096]{1,0:T(8,128)(2,1)}, bf16[16,4096]{1,0:T(8,128)(2,1)S(1)}, u32[]{:S(2)}, u32[]{:S(2)}) collective-permute-start(bf16[16,4096]{1,0:T(8,128)(2,1)} %whiten_slots.1.refs_0_), channel_id=1, source_target_pairs={{0,12},{4,0},{8,4},{12,8},{1,13},{5,1},{9,5},{13,9},{2,14},{6,2},{... | collective-permute-start | bytes 393224 | tf_op jit(solution)/shard_map/ppermute | solution.py:335
  15.9 0.0 collective-permute-start.2
  15.9 1.0 %collective-permute-start.1 = (bf16[16,4096]{1,0:T(8,128)(2,1)}, bf16[16,4096]{1,0:T(8,128)(2,1)S(1)}, u32[]{:S(2)}, u32[]{:S(2)}) collective-permute-start(bf16[16,4096]{1,0:T(8,128)(2,1)} %whiten_slots.1.refs_0_), channel_id=1, source_target_pairs={{0,4},{4,8},{8,12},{12,0},{1,5},{5,9},{9,13},{13,1},{2,6},{6,10},{... | collective-permute-start | bytes 393224 | tf_op jit(solution)/shard_map/ppermute | solution.py:335
  16.9 3.2 %collective-permute-done.3.refs_3_ = bf16[16,4096]{1,0:T(8,128)(2,1)S(1)} collective-permute-done((bf16[16,4096]{1,0:T(8,128)(2,1)}, bf16[16,4096]{1,0:T(8,128)(2,1)S(1)}, u32[]{:S(2)}, u32[]{:S(2)}) %collective-permute-start.3) | collective-permute-done | bytes 131104 | tf_op jit(solution)/shard_map/ppermute | solution.py:335
  20.2 6.7 %collective-permute-done.2.refs_2_ = bf16[16,4096]{1,0:T(8,128)(2,1)S(1)} collective-permute-done((bf16[16,4096]{1,0:T(8,128)(2,1)}, bf16[16,4096]{1,0:T(8,128)(2,1)S(1)}, u32[]{:S(2)}, u32[]{:S(2)}) %collective-permute-start.2) | collective-permute-done | bytes 131104 | tf_op jit(solution)/shard_map/ppermute | solution.py:335
  26.9 0.5 collective-permute-start.5
  27.4 0.8 collective-permute-done.6.refs_6_
  28.2 0.2 collective-permute-done.5.refs_5_
  28.5 0.4 copy-done.6
  28.9 0.2 copy-done.7
  29.1 2.8 %order_partners.1 = (bf16[64,4352]{1,0:T(8,128)(2,1)}, bf16[32,4096]{1,0:T(8,128)(2,1)}) custom-call(s32[8]{0:T(128)} %stack.43.info, s32[1,128]{1,0:T(1,128)} %bitcast.15, bf16[16,4096]{1,0:T(8,128)(2,1)} %whiten_slots.1.refs_0_, bf16[16,4096]{1,0:T(8,128)(2,1)} %copy-done.3, bf16[16,4096]{1,0:T(8,128)(2,1)} %copy-done.2, bf16[16,4096]{1,0:T(8,128)(2,1)} %copy-done.1, ...), custom_call_target="tpu_custom_call" | custom-call | flops 134217728 | bytes 2097152 | tf_op jit(solution)/shard_map/order_partners/pallas_call | solution.py:213
  31.9 1.5 %collective-permute-start.8 = (bf16[32,4096]{1,0:T(8,128)(2,1)}, bf16[32,4096]{1,0:T(8,128)(2,1)S(1)}, u32[]{:S(2)}, u32[]{:S(2)}) collective-permute-start(bf16[32,4096]{1,0:T(8,128)(2,1)} %get-tuple-element.8), channel_id=1, source_target_pairs={{0,2},{2,0},{1,3},{3,1},{4,6},{6,4},{5,7},{7,5},{8,10},{10,8},{9,1... | collective-permute-start | bytes 786440 | tf_op jit(solution)/shard_map/ppermute | solution.py:335
  33.4 13.2 %whiten.1.chan_hbm.own_chan = bf16[4096,128]{1,0:T(8,128)(2,1)} custom-call(s32[8]{0:T(128)} %stack.43.info, f32[128,4096]{1,0:T(8,128)} %x.3, f32[128,128]{1,0:T(8,128)} %copy-done, f32[128,128]{1,0:T(8,128)} %copy-done, f32[65,128]{1,0:T(8,128)} %bitcast.14), custom_call_target="tpu_custom_call" | custom-call | flops 68157440 | bytes 3145728 | tf_op jit(solution)/shard_map/whiten/pallas_call | solution.py:138
  46.5 0.5 collective-permute-start.10
  47.1 14.5 %correlate_own.1.before = f32[8256,128]{1,0:T(8,128)} custom-call(s32[8]{0:T(128)} %stack.43.info, bf16[64,4352]{1,0:T(8,128)(2,1)} %get-tuple-element.7.part.own_part, bf16[4096,128]{1,0:T(8,128)(2,1)} %whiten.1.chan_hbm.own_chan), custom_call_target="tpu_custom_call" | custom-call | flops 8657043456 | bytes 8454144 | tf_op jit(solution)/shard_map/correlate_own/pallas_call | solution.py:380
  61.6 10.2 %collective-permute-done.10.chan_hbm = bf16[4096,128]{1,0:T(8,128)(2,1)S(1)} collective-permute-done((bf16[4096,128]{1,0:T(8,128)(2,1)}, bf16[4096,128]{1,0:T(8,128)(2,1)S(1)}, u32[]{:S(2)}, u32[]{:S(2)}) %collective-permute-start.10) | collective-permute-done | bytes 1048608 | tf_op jit(solution)/shard_map/ppermute | solution.py:335
  71.9 1.0 %copy-done.8 = bf16[4096,128]{1,0:T(8,128)(2,1)} copy-done((bf16[4096,128]{1,0:T(8,128)(2,1)}, bf16[4096,128]{1,0:T(8,128)(2,1)S(1)}, u32[]{:S(2)}) %copy-start.8) | copy-done | bytes 1048600
  72.8 17.1 %correlate_other.1 = f32[8256,128]{1,0:T(8,128)} custom-call(s32[8]{0:T(128)} %stack.43.info, bf16[64,4352]{1,0:T(8,128)(2,1)} %get-tuple-element.7.part.own_part, bf16[32,4096]{1,0:T(8,128)(2,1)} %copy-done.9, bf16[32,4096]{1,0:T(8,128)(2,1)} %copy-done.10, bf16[4096,128]{1,0:T(8,128)(2,1)} %whiten.1.chan_hbm.own_chan, bf16[4096,128]{1,0:T(8,128)(2,1)} %copy-done.8, ...), custom_call_target="tpu_custom_call" | custom-call | flops 8657043456 | bytes 8454144 | tf_op jit(solution)/shard_map/correlate_other/pallas_call | solution.py:392
  (27 shorter events, 0.1 us)
Async XLA Ops:
  0.8 5.2 %collective-permute-start = (f32[128,128]{1,0:T(8,128)S(1)}, f32[128,128]{1,0:T(8,128)S(1)}, u32[]{:S(2)}, u32[]{:S(2)}) collective-permute-start(f32[128,128]{1,0:T(8,128)S(1)} %constant_dynamic-slice_fusion), channel_id=1, source_target_pairs={{0,2},{2,0},{1,3},{3,1},{4,6},{6,4},{5,7},{7,5},{8,10},{10,8},{9,1... | collective-permute-start | bytes 196616 | tf_op jit(solution)/shard_map/ppermute | solution.py:335
  6.0 0.6 copy-start
  11.7 8.4 %collective-permute-start.3 = (bf16[16,4096]{1,0:T(8,128)(2,1)}, bf16[16,4096]{1,0:T(8,128)(2,1)S(1)}, u32[]{:S(2)}, u32[]{:S(2)}) collective-permute-start(bf16[16,4096]{1,0:T(8,128)(2,1)} %whiten_slots.1.refs_0_), channel_id=1, source_target_pairs={{0,12},{4,0},{8,4},{12,8},{1,13},{5,1},{9,5},{13,9},{2,14},{6,2},{... | collective-permute-start | bytes 393224 | tf_op jit(solution)/shard_map/ppermute | solution.py:335
  15.9 11.0 %collective-permute-start.2 = (bf16[16,4096]{1,0:T(8,128)(2,1)}, bf16[16,4096]{1,0:T(8,128)(2,1)S(1)}, u32[]{:S(2)}, u32[]{:S(2)}) collective-permute-start(bf16[16,4096]{1,0:T(8,128)(2,1)} %whiten_slots.1.refs_0_), channel_id=1, source_target_pairs={{0,8},{4,12},{8,0},{12,4},{1,9},{5,13},{9,1},{13,5},{2,10},{6,14},... | collective-permute-start | bytes 393224 | tf_op jit(solution)/shard_map/ppermute | solution.py:335
  15.9 11.0 %collective-permute-start.1 = (bf16[16,4096]{1,0:T(8,128)(2,1)}, bf16[16,4096]{1,0:T(8,128)(2,1)S(1)}, u32[]{:S(2)}, u32[]{:S(2)}) collective-permute-start(bf16[16,4096]{1,0:T(8,128)(2,1)} %whiten_slots.1.refs_0_), channel_id=1, source_target_pairs={{0,4},{4,8},{8,12},{12,0},{1,5},{5,9},{9,13},{13,1},{2,6},{6,10},{... | collective-permute-start | bytes 393224 | tf_op jit(solution)/shard_map/ppermute | solution.py:335
  16.9 10.5 %collective-permute-start.4 = (bf16[16,4096]{1,0:T(8,128)(2,1)}, bf16[16,4096]{1,0:T(8,128)(2,1)S(1)}, u32[]{:S(2)}, u32[]{:S(2)}) collective-permute-start(bf16[16,4096]{1,0:T(8,128)(2,1)} %whiten_slots.1.refs_0_), channel_id=1, source_target_pairs={{0,1},{1,0},{2,3},{3,2},{4,5},{5,4},{6,7},{7,6},{8,9},{9,8},{10,11... | collective-permute-start | bytes 393224 | tf_op jit(solution)/shard_map/ppermute | solution.py:335
  20.1 8.3 %copy-start.1 = (bf16[16,4096]{1,0:T(8,128)(2,1)}, bf16[16,4096]{1,0:T(8,128)(2,1)S(1)}, u32[]{:S(2)}) copy-start(bf16[16,4096]{1,0:T(8,128)(2,1)S(1)} %collective-permute-done.3.refs_3_) | copy-start | bytes 393220
  20.1 7.3 %collective-permute-start.7 = (bf16[16,4096]{1,0:T(8,128)(2,1)S(1)}, bf16[16,4096]{1,0:T(8,128)(2,1)S(1)}, u32[]{:S(2)}, u32[]{:S(2)}) collective-permute-start(bf16[16,4096]{1,0:T(8,128)(2,1)S(1)} %collective-permute-done.3.refs_3_), channel_id=1, source_target_pairs={{0,1},{1,0},{2,3},{3,2},{4,5},{5,4},{6,7},{7,6},{8,9},{9,8},{10,11... | collective-permute-start | bytes 393224 | tf_op jit(solution)/shard_map/ppermute | solution.py:335
  26.9 1.5 %copy-start.2 = (bf16[16,4096]{1,0:T(8,128)(2,1)}, bf16[16,4096]{1,0:T(8,128)(2,1)S(1)}, u32[]{:S(2)}) copy-start(bf16[16,4096]{1,0:T(8,128)(2,1)S(1)} %collective-permute-done.2.refs_2_) | copy-start | bytes 393220
  26.9 1.3 %collective-permute-start.6 = (bf16[16,4096]{1,0:T(8,128)(2,1)S(1)}, bf16[16,4096]{1,0:T(8,128)(2,1)S(1)}, u32[]{:S(2)}, u32[]{:S(2)}) collective-permute-start(bf16[16,4096]{1,0:T(8,128)(2,1)S(1)} %collective-permute-done.2.refs_2_), channel_id=1, source_target_pairs={{0,1},{1,0},{2,3},{3,2},{4,5},{5,4},{6,7},{7,6},{8,9},{9,8},{10,11... | collective-permute-start | bytes 393224 | tf_op jit(solution)/shard_map/ppermute | solution.py:335
  26.9 1.5 %copy-start.3 = (bf16[16,4096]{1,0:T(8,128)(2,1)}, bf16[16,4096]{1,0:T(8,128)(2,1)S(1)}, u32[]{:S(2)}) copy-start(bf16[16,4096]{1,0:T(8,128)(2,1)S(1)} %collective-permute-done.1.refs_1_) | copy-start | bytes 393220
  26.9 1.5 %collective-permute-start.5 = (bf16[16,4096]{1,0:T(8,128)(2,1)S(1)}, bf16[16,4096]{1,0:T(8,128)(2,1)S(1)}, u32[]{:S(2)}, u32[]{:S(2)}) collective-permute-start(bf16[16,4096]{1,0:T(8,128)(2,1)S(1)} %collective-permute-done.1.refs_1_), channel_id=1, source_target_pairs={{0,1},{1,0},{2,3},{3,2},{4,5},{5,4},{6,7},{7,6},{8,9},{9,8},{10,11... | collective-permute-start | bytes 393224 | tf_op jit(solution)/shard_map/ppermute | solution.py:335
  27.4 1.0 %copy-start.4 = (bf16[16,4096]{1,0:T(8,128)(2,1)}, bf16[16,4096]{1,0:T(8,128)(2,1)S(1)}, u32[]{:S(2)}) copy-start(bf16[16,4096]{1,0:T(8,128)(2,1)S(1)} %collective-permute-done.4.refs_4_) | copy-start | bytes 393220
  27.4 1.0 %copy-start.5 = (bf16[16,4096]{1,0:T(8,128)(2,1)}, bf16[16,4096]{1,0:T(8,128)(2,1)S(1)}, u32[]{:S(2)}) copy-start(bf16[16,4096]{1,0:T(8,128)(2,1)S(1)} %collective-permute-done.7.refs_7_) | copy-start | bytes 393220
  28.2 0.7 copy-start.6
  28.4 0.6 copy-start.7
  31.9 15.2 %collective-permute-start.8 = (bf16[32,4096]{1,0:T(8,128)(2,1)}, bf16[32,4096]{1,0:T(8,128)(2,1)S(1)}, u32[]{:S(2)}, u32[]{:S(2)}) collective-permute-start(bf16[32,4096]{1,0:T(8,128)(2,1)} %get-tuple-element.8), channel_id=1, source_target_pairs={{0,2},{2,0},{1,3},{3,1},{4,6},{6,4},{5,7},{7,5},{8,10},{10,8},{9,1... | collective-permute-start | bytes 786440 | tf_op jit(solution)/shard_map/ppermute | solution.py:335
  46.5 25.3 %collective-permute-start.10 = (bf16[4096,128]{1,0:T(8,128)(2,1)}, bf16[4096,128]{1,0:T(8,128)(2,1)S(1)}, u32[]{:S(2)}, u32[]{:S(2)}) collective-permute-start(bf16[4096,128]{1,0:T(8,128)(2,1)} %whiten.1.chan_hbm.own_chan), channel_id=1, source_target_pairs={{0,2},{2,0},{1,3},{3,1},{4,6},{6,4},{5,7},{7,5},{8,10},{10,8},{9,1... | collective-permute-start | bytes 3145736 | tf_op jit(solution)/shard_map/ppermute | solution.py:335
  47.1 14.5 %copy-start.9 = (bf16[32,4096]{1,0:T(8,128)(2,1)}, bf16[32,4096]{1,0:T(8,128)(2,1)S(1)}, u32[]{:S(2)}) copy-start(bf16[32,4096]{1,0:T(8,128)(2,1)S(1)} %collective-permute-done.8.low_part) | copy-start | bytes 786436
  47.1 14.5 %collective-permute-start.9 = (bf16[32,4096]{1,0:T(8,128)(2,1)S(1)}, bf16[32,4096]{1,0:T(8,128)(2,1)S(1)}, u32[]{:S(2)}, u32[]{:S(2)}) collective-permute-start(bf16[32,4096]{1,0:T(8,128)(2,1)S(1)} %collective-permute-done.8.low_part), channel_id=1, source_target_pairs={{0,1},{1,0},{2,3},{3,2},{4,5},{5,4},{6,7},{7,6},{8,9},{9,8},{10,11... | collective-permute-start | bytes 786440 | tf_op jit(solution)/shard_map/ppermute | solution.py:335
  61.6 10.3 %copy-start.10 = (bf16[32,4096]{1,0:T(8,128)(2,1)}, bf16[32,4096]{1,0:T(8,128)(2,1)S(1)}, u32[]{:S(2)}) copy-start(bf16[32,4096]{1,0:T(8,128)(2,1)S(1)} %collective-permute-done.9.high_part) | copy-start | bytes 786436
  71.9 1.0 %copy-start.8 = (bf16[4096,128]{1,0:T(8,128)(2,1)}, bf16[4096,128]{1,0:T(8,128)(2,1)S(1)}, u32[]{:S(2)}) copy-start(bf16[4096,128]{1,0:T(8,128)(2,1)S(1)} %collective-permute-done.10.chan_hbm) | copy-start | bytes 3145732

commit v2 on v1

v2 whole, which is shorter than its diff:
```python
import functools
import math

import jax
import jax.numpy as jnp
from jax import lax
from jax.experimental import pallas as pl
from jax.experimental.pallas import tpu as pltpu
from jax.sharding import PartitionSpec as P

LAGS = 129
MOST = 16
TILE = 128
FINE = 16
SETS = 24
F32 = jnp.float32
BF16 = jnp.bfloat16
VMEM_BYTES = 24 * 2**20


def vmem(count):
    return [pl.BlockSpec(memory_space=pltpu.VMEM)] * count


SMEM = pl.BlockSpec(memory_space=pltpu.SMEM)
ANY = pl.BlockSpec(memory_space=pl.ANY)


def params():
    return pltpu.CompilerParams(vmem_limit_bytes=VMEM_BYTES)


def light():
    return pl.CostEstimate(flops=1000, bytes_accessed=1000, transcendentals=0)


def set_sizes(taps):
    sizes = []
    for group in ((taps + 1) // 2, taps // 2, (taps + 1) // 2):
        sizes += [(group + 1) // 2, group // 2, (group + 1) // 2]
    return sizes


def split_taps(filters, sets, taps):
    def take(rows):
        return [filters[k : k + 1, :] if k < taps else None for k in rows]

    def plus(a, b):
        return [x if y is None else (y if x is None else x + y) for x, y in zip(a, b)]

    whole = 2 * ((taps + 1) // 2)
    even, odd = take(range(0, whole, 2)), take(range(1, whole, 2))
    for i, group in enumerate((even, odd, plus(even, odd))):
        group = group + [None] * (len(group) % 2)
        first, second = group[0::2], group[1::2]
        for j, rows in enumerate((first, second, plus(first, second))):
            for k, row in enumerate(rows):
                if row is not None:
                    at = SETS * (3 * i + j) + k
                    sets[at : at + 1, :] = row


def part_fir(stage, at, sets, row, count, rows):
    total = None
    for first in range(8):
        later = [j for j in range((count + 7) // 8) if first + 8 * j < count]
        window = stage[at + first : at + first + rows + 8 * later[-1], :]
        for j in later:
            k = row + first + 8 * j
            term = sets[k : k + 1, :] * window[8 * j : 8 * j + rows]
            total = term if total is None else total + term
    return total


def fir(samples, sets, stage, late, mixed, base, rows, counts):
    few = rows // 4
    extent = few + 32
    x3, x4, x5, x6 = (samples[pl.ds(base - 32 + p, extent, stride=4), :] for p in (3, 4, 5, 6))
    arrays = (x6, x4, x6 + x4, x5, x3, x5 + x3, x6 + x5, x4 + x3, (x6 + x4) + (x5 + x3))
    for i, array in enumerate(arrays):
        stage[i * extent : (i + 1) * extent, :] = array

    def halves(i, lead):
        size = few + lead
        at = 3 * i * extent
        p0 = part_fir(stage, at, sets, SETS * 3 * i, counts[3 * i], few + 8)
        p1 = part_fir(stage, at + extent + 8 - lead, sets, SETS * (3 * i + 1), counts[3 * i + 1], size)
        p2 = part_fir(stage, at + 2 * extent + 8 - lead, sets, SETS * (3 * i + 2), counts[3 * i + 2], size)
        late[8 : 16 + few, :] = p0
        return late[15 - lead : 15 - lead + size, :] + p1, p2 - p1 - late[16 - lead : 16 - lead + size, :]

    a_even, a_odd = halves(0, 8)
    b_even, b_odd = halves(1, 0)
    c_even, c_odd = halves(2, 0)
    mixed[0 : few + 8, :] = a_odd
    y0 = mixed[7 : 7 + few, :] + b_even
    y1 = c_even - a_even[8:] - b_even
    y2 = a_even[8:] + b_odd
    y3 = c_odd - a_odd[8:] - b_odd
    for p, y in enumerate((y0, y1, y2, y3)):
        mixed[pl.ds(p, few, stride=4), :] = y
    return mixed[0:rows, :]


def fir_scratch(rows, lanes):
    few = rows // 4
    return [
        pltpu.VMEM((9 * (few + 32), lanes), F32),
        pltpu.VMEM((few + 16, lanes), F32),
        pltpu.VMEM((max(rows, few + 8), lanes), F32),
    ]


def place_of(axes, sizes):
    at = 0
    for axis, size in zip(axes, sizes):
        at = at * size + lax.axis_index(axis)
    return at


def prepare_kernel(sizes, chans, ring, slots, sources, sources_row, filters, _, rows, sets, chan_taps, wanted, same):
    taps = filters.shape[0]
    first_chan = place_of(("chan", "sub"), sizes[1:]) * chans
    for s in range(slots):
        rows[s] = 0

    def find(p, count):
        local = sources[p] - first_chan
        mine = (local >= 0) & (local < chans)
        rows[jnp.where(mine, count, slots)] = local
        return count + mine.astype(jnp.int32)

    lax.fori_loop(0, sources.shape[0], find, 0, unroll=16)
    split_taps(filters, sets, taps)
    chan_taps[...] = jnp.concatenate([filters[...], jnp.zeros((TILE - taps, chans), F32)], 0).T
    partners = sources_row.shape[1]
    _, chan_devs, sub_devs = sizes
    own_row = jnp.broadcast_to(sources_row[...].astype(F32), (partners, partners))
    owner_row = jnp.floor((own_row + 0.5) * (1.0 / chans))
    owner_col = owner_row.T
    lane = lax.broadcasted_iota(jnp.int32, (partners, partners), 1)
    line = lax.broadcasted_iota(jnp.int32, (partners, partners), 0)
    earlier = (owner_row == owner_col) & (lane < line)
    rank = jnp.sum(earlier.astype(F32), axis=1, keepdims=True)
    owner = owner_col[:, 0:1]
    if ring:
        owner_chan = jnp.floor((owner + 0.5) * (1.0 / sub_devs))
        owner_sub = owner - sub_devs * owner_chan
        my_chan = lax.axis_index("chan").astype(F32)
        my_sub = lax.axis_index("sub").astype(F32)
        behind = my_chan - owner_chan
        behind = jnp.where(behind < 0, behind + chan_devs, behind)
        place = jnp.where(owner_sub == my_sub, 0.0, 1.0) * chan_devs + behind
    else:
        place = owner
    at = lax.broadcasted_iota(jnp.int32, wanted.shape, 1).astype(F32)
    wanted[...] = (place * slots + rank == at).astype(F32)


def prepare(sizes, sources, filters, traces, slots, ring):
    taps, chans = filters.shape
    partners = sources.shape[0]
    total = slots * sizes[1] * sizes[2]
    return pl.pallas_call(
        functools.partial(prepare_kernel, sizes, chans, ring, slots),
        out_shape=(
            jax.ShapeDtypeStruct((slots + 1,), jnp.int32),
            jax.ShapeDtypeStruct((9 * SETS, chans), F32),
            jax.ShapeDtypeStruct((chans, TILE), F32),
            jax.ShapeDtypeStruct((partners, total), F32),
            jax.ShapeDtypeStruct(traces.shape, F32),
        ),
        in_specs=[SMEM] + vmem(2) + [ANY],
        out_specs=(SMEM, *vmem(3), ANY),
        input_output_aliases={3: 4},
        compiler_params=params(),
        cost_estimate=light(),
        name="prepare",
    )(sources, sources.reshape(1, partners), filters, traces)


def slots_kernel(taps, sizes, rows, x, low, high, chan_taps, after, out, wide, tall, lane_taps, *work):
    chans, length = x.shape
    slots = out.shape[0]
    segs = TILE // slots
    seg_len = length // segs
    half = (taps - 1) // 2
    here = lax.axis_index("tm")
    keep_low = (here > 0).astype(F32)
    keep_high = (here < sizes[0] - 1).astype(F32)
    for s in range(slots):
        row = rows[s]
        group = pl.multiple_of((row >> 3) << 3, 8)
        turn = (s - row) & 7

        def pick(ref):
            return pltpu.roll(ref[pl.ds(group, 8), :], turn, 0)[s % 8 : s % 8 + 1, :]

        wide[s : s + 1, 0:TILE] = pick(low) * keep_low
        wide[s : s + 1, TILE : TILE + length] = pick(x)
        wide[s : s + 1, TILE + length :] = pick(high) * keep_high
        lane_taps[s : s + 1, :] = pick(chan_taps)
    picked = lane_taps[0:slots, :]
    lane_taps[...] = jnp.concatenate([picked] * segs, 0).T
    for t in range(seg_len // TILE + 2):
        cols = [wide[:, g * seg_len + t * TILE : g * seg_len + (t + 1) * TILE] for g in range(segs)]
        tall[t * TILE : (t + 1) * TILE, :] = jnp.concatenate(cols, 0).T
    split_taps(lane_taps, work[0], taps)
    counts = set_sizes(taps)
    done = fir(tall, *work, TILE - half, seg_len, counts)
    for t in range(seg_len // TILE):
        turned = done[t * TILE : (t + 1) * TILE].T
        for g in range(segs):
            start = g * seg_len + t * TILE
            out[:, start : start + TILE] = turned[g * slots : (g + 1) * slots].astype(BF16)


def whiten_slots(sizes, taps, rows, traces, low, high, chan_taps, after, slots):
    length = traces.shape[1]
    seg_len = length * slots // TILE
    return pl.pallas_call(
        functools.partial(slots_kernel, taps, sizes),
        out_shape=jax.ShapeDtypeStruct((slots, length), BF16),
        in_specs=[SMEM] + vmem(4) + [ANY],
        out_specs=vmem(1)[0],
        scratch_shapes=[
            pltpu.VMEM((slots, length + 2 * TILE), F32),
            pltpu.VMEM((seg_len + 2 * TILE, TILE), F32),
            pltpu.VMEM((TILE, TILE), F32),
        ]
        + [pltpu.VMEM((9 * SETS, TILE), F32)]
        + fir_scratch(seg_len, TILE),
        compiler_params=params(),
        cost_estimate=light(),
        name="whiten_slots",
    )(rows, traces, low, high, chan_taps, after)


def whiten_kernel(taps, rows, time_devs, x, low, high, sets, out, tall, *work):
    length = x.shape[1]
    half = (taps - 1) // 2
    here = lax.axis_index("tm")
    tall[0:TILE, :] = jnp.where(here > 0, low[...], 0.0).T
    tall[TILE + length :, :] = jnp.where(here < time_devs - 1, high[...], 0.0).T
    counts = set_sizes(taps)

    def turn(t, carry):
        start = pl.multiple_of(t * TILE, TILE)
        tall[pl.ds(start + TILE, TILE), :] = x[:, pl.ds(start, TILE)].T
        return carry

    lax.fori_loop(0, length // TILE, turn, 0)

    def block(i, carry):
        at = pl.multiple_of(i * rows, rows)
        out[pl.ds(at, rows), :] = fir(tall, sets, *work, at + TILE - half, rows, counts).astype(BF16)
        return carry

    lax.fori_loop(0, length // rows, block, 0)


def whiten(time_devs, taps, traces, low, high, sets):
    chans, length = traces.shape
    rows = 2 * TILE
    return pl.pallas_call(
        functools.partial(whiten_kernel, taps, rows, time_devs),
        out_shape=jax.ShapeDtypeStruct((length, chans), BF16),
        in_specs=vmem(4),
        out_specs=vmem(1)[0],
        scratch_shapes=[pltpu.VMEM((length + 2 * TILE, chans), F32)] + fir_scratch(rows, chans),
        compiler_params=params(),
        cost_estimate=light(),
        name="whiten",
    )(traces, low, high, sets)


def whiten_part_kernel(taps, rows, inner, x, sets, beside, _, *refs):
    outs, (tall, *work) = refs[:-4], refs[-4:]
    length, size = x.shape[1], tall.shape[0] - 2 * TILE
    half = (taps - 1) // 2
    tiles = rows // TILE
    at_start = (lax.axis_index("tm") > 0) == inner
    start = jnp.where(at_start, 0, length - size)
    near = x[:, pl.ds(pl.multiple_of(jnp.where(at_start, size, length - size - TILE), TILE), TILE)]
    outside = beside[...] if inner else jnp.zeros_like(near)
    tall[0:TILE, :] = jnp.where(at_start, outside, near).T
    tall[TILE + size :, :] = jnp.where(at_start, near, outside).T
    counts = set_sizes(taps)

    def turn(t):
        tall[pl.ds(pl.multiple_of(t * TILE + TILE, TILE), TILE), :] = x[
            :, pl.ds(pl.multiple_of(start + t * TILE, TILE), TILE)
        ].T

    for t in range(tiles + 1):
        turn(t)

    done = 0
    for out in outs:

        def block(i, carry):
            at = pl.multiple_of(i * rows, rows)
            value = fir(tall, sets, *work, at + TILE - half, rows, counts).astype(BF16)
            out[pl.ds(at - done, rows), :] = value
            for t in range(tiles):
                turn(jnp.minimum((i + 1) * tiles + 1 + t, size // TILE - 1))
            return carry

        lax.fori_loop(done // rows, (done + out.shape[0]) // rows, block, 0)
        done += out.shape[0]


def whiten_part(taps, traces, sets, beside, after, pieces, inner):
    chans = traces.shape[0]
    size = sum(pieces)
    rows = 2 * TILE
    return pl.pallas_call(
        functools.partial(whiten_part_kernel, taps, rows, inner),
        out_shape=tuple(jax.ShapeDtypeStruct((piece, chans), BF16) for piece in pieces),
        in_specs=vmem(3) + [ANY],
        out_specs=tuple(vmem(len(pieces))),
        scratch_shapes=[pltpu.VMEM((size + 2 * TILE, chans), F32)] + fir_scratch(rows, chans),
        compiler_params=params(),
        cost_estimate=light(),
        name="whiten_inner" if inner else "whiten_outer",
    )(traces, sets, beside, after)


def join_kernel(parts, count, after, *refs):
    size = refs[0].shape[0]
    each = count // parts
    for n in range(parts):
        for i in range(each):
            refs[count + n][i * size : (i + 1) * size, :] = refs[n * each + i][...]


def join(after, parts, pieces):
    size, length = parts[0].shape
    shape = jax.ShapeDtypeStruct((size * len(parts) // pieces, length), BF16)
    return pl.pallas_call(
        functools.partial(join_kernel, pieces, len(parts)),
        out_shape=(shape,) * pieces,
        in_specs=[ANY] + vmem(len(parts)),
        out_specs=tuple(vmem(pieces)),
        compiler_params=params(),
        cost_estimate=light(),
        name="join_slots",
    )(after, *parts)


def order_kernel(ring, count, choose, after, *refs):
    parts, (*outs, gathered) = refs[:count], refs[count:]
    step = parts[0].shape[0]
    for i, part in enumerate(parts):
        gathered[i * step : (i + 1) * step, :] = part[...]
    if not ring:
        outs[0][...] = jnp.dot(choose[...].astype(BF16), gathered[...], preferred_element_type=F32).astype(BF16)
        return
    own, send = outs
    half, length = send.shape
    here = lax.axis_index("tm")
    mine = choose[pl.ds(pl.multiple_of(here * half, half), half), :]
    theirs = choose[pl.ds(pl.multiple_of((1 - here) * half, half), half), :]
    wanted = jnp.concatenate([mine, theirs], 0).astype(BF16)
    got = jnp.dot(wanted, gathered[...], preferred_element_type=F32).astype(BF16)
    own[:, 0:TILE] = jnp.zeros((half, TILE), BF16)
    own[:, TILE + length :] = jnp.zeros((half, TILE), BF16)
    own[:, TILE : TILE + length] = got[:half]
    send[...] = got[half:]


def order(choose, after, parts, ring):
    partners, total = choose.shape
    length = parts[0].shape[1]
    if ring:
        half = partners // 2
        out_shape = (
            jax.ShapeDtypeStruct((half, length + 2 * TILE), BF16),
            jax.ShapeDtypeStruct((half, length), BF16),
        )
        out_specs = tuple(vmem(2))
    else:
        out_shape = jax.ShapeDtypeStruct((partners, length), BF16)
        out_specs = vmem(1)[0]
    return pl.pallas_call(
        functools.partial(order_kernel, ring, len(parts)),
        out_shape=out_shape,
        in_specs=vmem(1) + [ANY] + vmem(len(parts)),
        out_specs=out_specs,
        scratch_shapes=[pltpu.VMEM((total, length), BF16)],
        compiler_params=params(),
        cost_estimate=light(),
        name="order_partners",
    )(choose, after, *parts)


def lay_out(part, out, start, width):
    rows = part.shape[0]
    lane = lax.broadcasted_iota(jnp.int32, (rows, TILE), 1)
    tiles = [part[:, pl.ds(start + TILE * i, TILE)] for i in range(width // TILE + 1)]
    half = (LAGS - 1) // 2
    for b in range(FINE + 1):
        turned = [pltpu.roll(tile, half - b, 1) for tile in tiles]
        for i in range(width // TILE):
            piece = jnp.where(lane < half - b, turned[i], turned[i + 1])
            out[b * rows : (b + 1) * rows, TILE * i : TILE * i + TILE] = piece


def add_lags(shifted, chan, total, start, width, rows):
    chans = chan.shape[1]
    coarse = (LAGS - 1) // FINE
    pair = 2 if chans % TILE == 0 else 1
    for a in range(0, coarse, pair):
        cols = [chan[pl.ds(start + TILE - FINE * (a + i), width), :] for i in range(pair)]
        last = a + pair == coarse
        used = rows * (FINE + 1 if last else FINE)
        block = cols[0] if pair == 1 else jnp.concatenate(cols, 1)
        term = jnp.dot(shifted[:used, :], block, preferred_element_type=F32)
        for i in range(pair):
            size = used if i == pair - 1 else rows * FINE
            place = (a + i) * FINE * rows
            total[place : place + size, :] += term[:size, i * chans : (i + 1) * chans]


def correlate_all(part, chan, total, spare, start, width, chunk, rows):
    first, second, rest = spare
    whole = width // (2 * chunk) * (2 * chunk)
    lay_out(part, first, start, chunk)

    def advance(i, carry):
        now = pl.multiple_of(start + 2 * chunk * i, TILE)
        lay_out(part, second, now + chunk, chunk)
        add_lags(first, chan, total, now, chunk, rows)
        after = pl.multiple_of(jnp.minimum(now + 2 * chunk, start + whole - chunk), TILE)
        lay_out(part, first, after, chunk)
        add_lags(second, chan, total, now + chunk, chunk, rows)
        return carry

    lax.fori_loop(0, whole // (2 * chunk), advance, 0)
    if width > whole:
        lay_out(part, rest, start + whole, width - whole)
        add_lags(rest, chan, total, start + whole, width - whole, rows)


def add_pair(shifted, chan, before, total, start, width, rows, a, scale):
    chans = chan.shape[1]
    last = a + 2 == (LAGS - 1) // FINE
    used = rows * (FINE + 1 if last else FINE)
    term = None
    for copies, begin in zip(shifted, start):
        cols = [chan[pl.ds(begin + TILE - FINE * (a + i), width), :] for i in range(2)]
        piece = jnp.dot(copies[:used, :], jnp.concatenate(cols, 1), preferred_element_type=F32)
        term = piece if term is None else term + piece
    for i in range(2):
        size = used if i == 1 else rows * FINE
        place = (a + i) * FINE * rows
        mine = term[:size, i * chans : (i + 1) * chans]
        if before is not None:
            mine = before[place : place + size, :] + mine
        total[place : place + size, :] = mine if scale is None else mine * scale


def correlate_ring(part, chan, total, spare, start, width, chunk, rows, ready, before, scale, out, sems):
    pairs = range(0, (LAGS - 1) // FINE, 2)
    rest = width % chunk
    count = width // chunk
    begin = [pl.multiple_of(start + rest + i * chunk, TILE) for i in range(count)]
    if rest:
        lay_out(part, spare[3], start, rest)
    lay_out(part, spare[0], begin[0], chunk)
    for copy in ready:
        copy.wait()
    if rest:
        for a in pairs:
            add_pair([spare[3]], chan, before, total, [start], rest, rows, a, None)
        before = total
    for i in range(count - 2):
        lay_out(part, spare[(i + 1) % 3], begin[i + 1], chunk)
        if i == count - 3:
            lay_out(part, spare[(i + 2) % 3], begin[i + 2], chunk)
        for a in pairs:
            add_pair([spare[i % 3]], chan, before, total, [begin[i]], chunk, rows, a, None)
        before = total
    stores = []
    for n, a in enumerate(pairs):
        ends = (count - 2, count - 1)
        add_pair([spare[i % 3] for i in ends], chan, before, total, [begin[i] for i in ends], chunk, rows, a, scale)
        if out is not None:
            at = 2 * n * FINE * rows
            size = rows * (2 * FINE + (1 if a + 2 == (LAGS - 1) // FINE else 0))
            stores.append(pltpu.make_async_copy(total.at[pl.ds(at, size), :], out.at[pl.ds(at, size), :], sems.at[n]))
            stores[-1].start()
    for store in stores:
        store.wait()


def place_pieces(at_start, pieces, chan, length, sems):
    outer = pieces[0].shape[0]
    at = jnp.where(at_start, 0, length - outer)
    copies = []
    for n, piece in enumerate(pieces):
        size = piece.shape[0]
        to = chan.at[pl.ds(pl.multiple_of(TILE + at, TILE), size), :]
        copies.append(pltpu.make_async_copy(piece, to, sems.at[4 + n]))
        copies[-1].start()
        at = jnp.where(at_start, outer, 0) if n == 0 else at + size
    return copies


def first_kernel(chunk, count, part, *refs):
    pieces, (total, chan, a, b, c, d, sems) = refs[:count], refs[count:]
    length = part.shape[1] - 2 * TILE
    here = lax.axis_index("tm")
    ready = place_pieces(here == 0, pieces, chan, length, sems)
    edge = jnp.zeros((TILE, chan.shape[1]), BF16)
    chan[0:TILE, :] = edge
    chan[TILE + length :, :] = edge
    start = pl.multiple_of(here * TILE, TILE)
    correlate_ring(part, chan, total, (a, b, c, d), start, length, chunk, part.shape[0], ready, None, None, None, sems)


def second_kernel(chunk, scale, count, own_part, other_part, own_head, own_tail, before, *refs):
    pieces, (out, total, part, chan, a, b, c, d, sems) = refs[:count], refs[count:]
    length = part.shape[1] - 2 * TILE
    rows = part.shape[0]
    here = lax.axis_index("tm")
    ready = place_pieces(here > 0, pieces, chan, length, sems)
    later = here > 0
    part[:, TILE : TILE + length] = other_part[...]
    part[:, 0:TILE] = jnp.where(later, 0, own_part[:, length : length + TILE]).astype(BF16)
    part[:, TILE + length :] = jnp.where(later, own_part[:, TILE : 2 * TILE], 0).astype(BF16)
    chan[0:TILE, :] = jnp.where(later, 0, own_tail[own_tail.shape[0] - TILE :, :]).astype(BF16)
    chan[TILE + length :, :] = jnp.where(later, own_head[0:TILE, :], 0).astype(BF16)
    correlate_ring(part, chan, total, (a, b, c, d), 0, length + TILE, chunk, rows, ready, before, scale, out, sems)


def whole_kernel(chunk, scale, part_in, chan_in, total, part, chan, a, b, c):
    length = chan_in.shape[0]
    rows = part.shape[0]
    part[:, 0:TILE] = jnp.zeros((rows, TILE), BF16)
    part[:, TILE + length :] = jnp.zeros((rows, TILE), BF16)
    part[:, TILE : TILE + length] = part_in[...]
    edge = jnp.zeros((TILE, chan.shape[1]), BF16)
    chan[0:TILE, :] = edge
    chan[TILE + length :, :] = edge
    chan[TILE : TILE + length, :] = chan_in[...]
    total[...] = jnp.zeros_like(total)
    correlate_all(part, chan, total, (a, b, c), 0, length + TILE, chunk, rows)
    total[...] = total[...] * scale


def spare(rows, widths):
    return [pltpu.VMEM((rows * (FINE + 1), width), BF16) for width in widths]


def shifted(array, axis, step):
    count = lax.axis_size(axis)
    return lax.ppermute(array, axis, [(i, (i + step) % count) for i in range(count)])


def on_device(traces, filters, sources):
    chans, length = traces.shape
    partners = sources.shape[0]
    sizes = tuple(lax.axis_size(axis) for axis in ("tm", "chan", "sub"))
    time_devs, chan_devs, sub_devs = sizes
    slots = min(chans, MOST)
    rows = partners // time_devs
    scale = 1.0 / math.sqrt(length * time_devs)
    chunk = 4 * TILE
    taps = filters.T
    ring = time_devs == 2 and sub_devs == 2 and chan_devs <= 4 and chans % TILE == 0
    out_shape = jax.ShapeDtypeStruct((LAGS * rows, chans), F32)
    count = taps.shape[0]
    slot_rows, sets, chan_taps, choose, held = prepare(sizes, sources, taps, traces, slots, ring)
    if ring:
        here = lax.axis_index("tm")
        edge = lax.dynamic_slice_in_dim(traces, jnp.where(here == 0, length - TILE, 0), TILE, 1)
        beside = shifted(edge, "tm", 1)
        far = length // 2
        outer = whiten_part(count, held, sets, beside, beside, (length // 2,), False)
        other_outer = [shifted(piece, "tm", 1) for piece in outer]
        picked = whiten_slots(sizes, count, slot_rows, held, beside, beside, chan_taps, outer[0], slots)
        inner = whiten_part(count, held, sets, beside, picked, (length // 2,), True)
        other_inner = [shifted(piece, "tm", 1) for piece in inner]
        near = [picked] + [shifted(picked, "chan", step) for step in range(1, chan_devs)]
        mine = join(other_outer[0], near, 1)
        theirs = [shifted(part, "sub", 1) for part in mine]
        own_part, send = order(choose, other_inner[0], [*mine, *theirs], True)
        other_part = shifted(send, "tm", 1)
        pieces = len(outer) + len(inner)
        before = pl.pallas_call(
            functools.partial(first_kernel, chunk, pieces),
            out_shape=out_shape,
            in_specs=vmem(1) + [ANY] * pieces,
            out_specs=vmem(1)[0],
            scratch_shapes=[pltpu.VMEM((length + 2 * TILE, chans), BF16)]
            + spare(rows, (chunk, chunk, chunk, TILE))
            + [pltpu.SemaphoreType.DMA((4 + pieces,))],
            compiler_params=params(),
            cost_estimate=light(),
            name="correlate_own",
        )(own_part, *outer, *inner)
        total = pl.pallas_call(
            functools.partial(second_kernel, chunk, scale, pieces),
            out_shape=out_shape,
            in_specs=vmem(5) + [ANY] * pieces,
            out_specs=ANY,
            scratch_shapes=[
                pltpu.VMEM(out_shape.shape, F32),
                pltpu.VMEM((rows, length + 2 * TILE), BF16),
                pltpu.VMEM((length + 2 * TILE, chans), BF16),
            ]
            + spare(rows, (chunk, chunk, chunk, TILE))
            + [pltpu.SemaphoreType.DMA((4 + pieces,))],
            compiler_params=params(),
            cost_estimate=light(),
            name="correlate_other",
        )(own_part, other_part, inner[0], inner[-1], before, *other_outer, *other_inner)
    else:
        low = lax.ppermute(traces[:, length - TILE :], "tm", [(i, i + 1) for i in range(time_devs - 1)])
        high = lax.ppermute(traces[:, :TILE], "tm", [(i + 1, i) for i in range(time_devs - 1)])
        picked = whiten_slots(sizes, count, slot_rows, held, low, high, chan_taps, low, slots)
        whitened = whiten(time_devs, count, traces, low, high, sets)
        gathered = lax.all_gather(picked, ("chan", "sub"), axis=0, tiled=True)
        all_parts = order(choose, low, [gathered], False)
        parts = lax.all_to_all(all_parts, "tm", 0, 1, tiled=True)
        all_chans = lax.all_gather(whitened, "tm", axis=0, tiled=True)
        full = length * time_devs
        total = pl.pallas_call(
            functools.partial(whole_kernel, chunk, scale),
            out_shape=out_shape,
            in_specs=vmem(2),
            out_specs=vmem(1)[0],
            scratch_shapes=[
                pltpu.VMEM((rows, full + 2 * TILE), BF16),
                pltpu.VMEM((full + 2 * TILE, chans), BF16),
            ]
            + spare(rows, (chunk, chunk, TILE)),
            compiler_params=pltpu.CompilerParams(vmem_limit_bytes=2 * VMEM_BYTES),
            name="correlate_whole",
        )(parts, all_chans)
    return jnp.transpose(total.reshape(LAGS, rows, chans), (1, 0, 2))


def solution(mesh):
    return jax.shard_map(
        on_device,
        mesh=mesh,
        in_specs=(
            P(("groups", "chan", "sub"), "tm"),
            P(("groups", "chan", "sub"), None),
            P("groups"),
        ),
        out_specs=P("tm", None, ("groups", "chan", "sub")),
        check_vma=False,
    )
```

time: 90.3 us -> 59.1 us (0.65)
  Pallas kernels: 52.6 us -> 32.3 us
  waiting for transfers between devices: 22.8 us -> 12.6 us
  local copies, waits for them, and re-layouts: 3.76 us -> 1.61 us
  starting transfers between devices: 10.6 us -> 12.1 us
    pallas_call x5 -> x8, Pallas kernels: 52.6 us -> 32.3 us  [the longest x1 12 us: on_device(): pl.pallas_call(functools.partial(second_kernel, chunk, scale, pieces), ou...]
    ppermute x11 -> x8, waiting for transfers between devices: 22.8 us -> 12.6 us  [shifted(): lax.ppermute(array, axis, [(i, (i + step) % count) for i in range(count)])]
    ppermute x11 -> x8, starting transfers between devices: 10.6 us -> 12.1 us  [shifted(): lax.ppermute(array, axis, [(i, (i + step) % count) for i in range(count)])]
    unnamed x22 -> x5, local copies, waits for them, and re-layouts: 2.25 us -> 1.6 us
  transfers between devices with their start and end apart: 11 -> 8, of which waited for: 6 -> 4; matrix products, arithmetic and copies ran while one was open for 1% -> 0% of each run, Pallas kernels for 31% -> 28%
where the time goes in v2:
time: 59.1 us; the launch traced here: 58.9 us
  Pallas kernels  32.3 us (55%)
  waiting for transfers between devices  12.6 us (21%)
  starting transfers between devices  12.1 us (20%)
  local copies, waits for them, and re-layouts  1.61 us (3%)
    ppermute x8, waiting for transfers between devices, shifted(): lax.ppermute(array, axis, [(i, (i + step) % count) for i in range(count)])  12.6 us
    ppermute x8, starting transfers between devices, shifted(): lax.ppermute(array, axis, [(i, (i + step) % count) for i in range(count)])  12.1 us
    pallas_call x1, Pallas kernels, on_device(): pl.pallas_call(functools.partial(second_kernel, chunk, scale, pieces), ou...  12 us
    pallas_call x1, Pallas kernels, on_device(): pl.pallas_call(functools.partial(first_kernel, chunk, pieces), out_shape=...  9.78 us
    pallas_call x2, Pallas kernels, whiten_part(): pl.pallas_call(functools.partial(whiten_part_kernel, taps, rows, inner),...  6.51 us
    pallas_call x1, Pallas kernels, whiten_slots(): pl.pallas_call(functools.partial(slots_kernel, taps, sizes), out_shape=ja...  1.85 us
    pallas_call x1, Pallas kernels, prepare(): pl.pallas_call(functools.partial(prepare_kernel, sizes, chans, ring, slot...  1.74 us
    unnamed x5, local copies, waits for them, and re-layouts  1.6 us
  transfers between devices with their start and end apart: 8, of which 4 were waited for; matrix products, arithmetic and copies ran while one was open for 0% of the time, Pallas kernels for 28%

profile of v2, /device:TPU:0, one launch (start us, length us, event | category | flops | bytes accessed | tf_op | source)
XLA Modules:
  0.0 58.9 jit_solution(4489246285767014082)
XLA Ops:
  0.0 1.6 %copy.7._ = f32[128,4096]{1,0:T(8,128)S(1)} copy(f32[128,4096]{1,0:T(8,128)} %param.3) | data formatting | bytes 4194304
  1.6 3.0 %collective-permute-start = (f32[128,128]{1,0:T(8,128)S(1)}, f32[128,128]{1,0:T(8,128)S(1)}, u32[]{:S(2)}, u32[]{:S(2)}) collective-permute-start(f32[128,128]{1,0:T(8,128)S(1)} %constant_dynamic-slice_fusion), channel_id=1, source_target_pairs={{0,2},{2,0},{1,3},{3,1},{4,6},{6,4},{5,7},{7,5},{8,10},{10,8},{9,1... | collective-permute-start | bytes 196616 | tf_op jit(solution)/shard_map/ppermute | solution.py:558
  4.6 1.7 %prepare.1 = (s32[17]{0:T(128)S(1)}, f32[216,128]{1,0:T(8,128)S(1)}, f32[128,128]{1,0:T(8,128)S(1)}, f32[128,128]{1,0:T(8,128)S(1)}, f32[128,4096]{1,0:T(8,128)S(1)}) custom-call(s32[128]{0:T(128)S(1)} %copy-done.1, s32[1,128]{1,0:T(1,128)S(1)} %bitcast.6, f32[65,128]{1,0:T(8,128)S(1)} %bitcast.5, ...), custom_call_target="tpu_custom_call", output_to_operand_aliasing={{4}: (3, {})} | custom-call | flops 1000 | bytes 1000 | tf_op jit(solution)/shard_map/prepare/pallas_call | solution.py:164
  6.4 0.5 collective-permute-done.beside._.low.high
  6.9 3.3 %whiten_outer.1.after.refs_0_ = bf16[2048,128]{1,0:T(8,128)(2,1)S(1)} custom-call(f32[128,4096]{1,0:T(8,128)S(1)} %get-tuple-element.13.x, f32[216,128]{1,0:T(8,128)S(1)} %get-tuple-element.14.sets, f32[128,128]{1,0:T(8,128)S(1)} %collective-permute-done.beside._.low.high, f32[128,128]{1,0:T(8,128)S(1)} %collective-permute-done.beside._.low.high), custom_call_target="tpu_custom_call" | custom-call | flops 1000 | bytes 1000 | tf_op jit(solution)/shard_map/whiten_outer/pallas_call | solution.py:317
  10.1 2.1 %collective-permute-start.2 = (bf16[2048,128]{1,0:T(8,128)(2,1)S(1)}, bf16[2048,128]{1,0:T(8,128)(2,1)S(1)}, u32[]{:S(2)}, u32[]{:S(2)}) collective-permute-start(bf16[2048,128]{1,0:T(8,128)(2,1)S(1)} %whiten_outer.1.after.refs_0_), channel_id=1, source_target_pairs={{0,2},{2,0},{1,3},{3,1},{4,6},{6,4},{5,7},{7,5},{8,10},{10,8},{9,1... | collective-permute-start | bytes 1572872 | tf_op jit(solution)/shard_map/ppermute | solution.py:558
  12.2 1.9 %whiten_slots.1._.refs_0_ = bf16[16,4096]{1,0:T(8,128)(2,1)S(1)} custom-call(s32[17]{0:T(128)S(1)} %get-tuple-element.15.rows, f32[128,4096]{1,0:T(8,128)S(1)} %get-tuple-element.13.x, f32[128,128]{1,0:T(8,128)S(1)} %collective-permute-done.beside._.low.high, f32[128,128]{1,0:T(8,128)S(1)} %collective-permute-done.beside._.low.high, ...), custom_call_target="tpu_custom_call" | custom-call | flops 1000 | bytes 1000 | tf_op jit(solution)/shard_map/whiten_slots/pallas_call | solution.py:221
  14.1 3.7 %collective-permute-start.5 = (bf16[16,4096]{1,0:T(8,128)(2,1)S(1)}, bf16[16,4096]{1,0:T(8,128)(2,1)S(1)}, u32[]{:S(2)}, u32[]{:S(2)}) collective-permute-start(bf16[16,4096]{1,0:T(8,128)(2,1)S(1)} %whiten_slots.1._.refs_0_), channel_id=1, source_target_pairs={{0,12},{4,0},{8,4},{12,8},{1,13},{5,1},{9,5},{13,9},{2,14},{6,2},{... | collective-permute-start | bytes 393224 | tf_op jit(solution)/shard_map/ppermute | solution.py:558
  17.7 0.0 collective-permute-start.4
  17.7 1.0 %collective-permute-start.3 = (bf16[16,4096]{1,0:T(8,128)(2,1)S(1)}, bf16[16,4096]{1,0:T(8,128)(2,1)S(1)}, u32[]{:S(2)}, u32[]{:S(2)}) collective-permute-start(bf16[16,4096]{1,0:T(8,128)(2,1)S(1)} %whiten_slots.1._.refs_0_), channel_id=1, source_target_pairs={{0,4},{4,8},{8,12},{12,0},{1,5},{5,9},{9,13},{13,1},{2,6},{6,10},{... | collective-permute-start | bytes 393224 | tf_op jit(solution)/shard_map/ppermute | solution.py:558
  18.7 3.3 %whiten_inner.1.refs_1_.own_head.own_tail = bf16[2048,128]{1,0:T(8,128)(2,1)S(1)} custom-call(f32[128,4096]{1,0:T(8,128)S(1)} %get-tuple-element.13.x, f32[216,128]{1,0:T(8,128)S(1)} %get-tuple-element.14.sets, f32[128,128]{1,0:T(8,128)S(1)} %collective-permute-done.beside._.low.high, bf16[16,4096]{1,0:T(8,128)(2,1)S(1)} %whiten_slots.1._.refs_0_), custom_call_target="tpu_custom_call" | custom-call | flops 1000 | bytes 1000 | tf_op jit(solution)/shard_map/whiten_inner/pallas_call | solution.py:317
  22.0 0.6 %collective-permute-start.1 = (bf16[2048,128]{1,0:T(8,128)(2,1)S(1)}, bf16[2048,128]{1,0:T(8,128)(2,1)S(1)}, u32[]{:S(2)}, u32[]{:S(2)}) collective-permute-start(bf16[2048,128]{1,0:T(8,128)(2,1)S(1)} %whiten_inner.1.refs_1_.own_head.own_tail), channel_id=1, source_target_pairs={{0,2},{2,0},{1,3},{3,1},{4,6},{6,4},{5,7},{7,5},{8,10},{10,8},{9,1... | collective-permute-start | bytes 1572872 | tf_op jit(solution)/shard_map/ppermute | solution.py:558
  22.6 0.0 collective-permute-done.5.refs_3_
  22.6 5.8 %collective-permute-done.4.refs_2_ = bf16[16,4096]{1,0:T(8,128)(2,1)S(1)} collective-permute-done((bf16[16,4096]{1,0:T(8,128)(2,1)S(1)}, bf16[16,4096]{1,0:T(8,128)(2,1)S(1)}, u32[]{:S(2)}, u32[]{:S(2)}) %collective-permute-start.4) | collective-permute-done | bytes 131104 | tf_op jit(solution)/shard_map/ppermute | solution.py:558
  28.4 0.0 collective-permute-done.3.refs_1_
  28.4 0.0 collective-permute-done.2.after.refs_0_
  28.4 0.1 collective-permute-start.6
  28.5 5.8 %collective-permute-done.1.after.refs_1_ = bf16[2048,128]{1,0:T(8,128)(2,1)S(1)} collective-permute-done((bf16[2048,128]{1,0:T(8,128)(2,1)S(1)}, bf16[2048,128]{1,0:T(8,128)(2,1)S(1)}, u32[]{:S(2)}, u32[]{:S(2)}) %collective-permute-start.1) | collective-permute-done | bytes 524320 | tf_op jit(solution)/shard_map/ppermute | solution.py:558
  34.3 0.0 collective-permute-done.6.refs_1_
  34.3 0.4 order_partners.1
  34.8 1.7 %collective-permute-start.7 = (bf16[64,4096]{1,0:T(8,128)(2,1)S(1)}, bf16[64,4096]{1,0:T(8,128)(2,1)S(1)}, u32[]{:S(2)}, u32[]{:S(2)}) collective-permute-start(bf16[64,4096]{1,0:T(8,128)(2,1)S(1)} %get-tuple-element.18), channel_id=1, source_target_pairs={{0,2},{2,0},{1,3},{3,1},{4,6},{6,4},{5,7},{7,5},{8,10},{10,8},{9,1... | collective-permute-start | bytes 1572872 | tf_op jit(solution)/shard_map/ppermute | solution.py:558
  36.5 9.8 %correlate_own.1.before = f32[8256,128]{1,0:T(8,128)S(1)} custom-call(bf16[64,4352]{1,0:T(8,128)(2,1)S(1)} %get-tuple-element.17.part.own_part, bf16[2048,128]{1,0:T(8,128)(2,1)S(1)} %whiten_outer.1.after.refs_0_, bf16[2048,128]{1,0:T(8,128)(2,1)S(1)} %whiten_inner.1.refs_1_.own_head.own_tail), custom_call_target="tpu_custom_call" | custom-call | flops 1000 | bytes 1000 | tf_op jit(solution)/shard_map/correlate_own/pallas_call | solution.py:591
  46.2 0.5 collective-permute-done.7.other_part
  46.8 12.0 %correlate_other.1 = f32[8256,128]{1,0:T(8,128)} custom-call(bf16[64,4352]{1,0:T(8,128)(2,1)S(1)} %get-tuple-element.17.part.own_part, bf16[64,4096]{1,0:T(8,128)(2,1)S(1)} %collective-permute-done.7.other_part, bf16[2048,128]{1,0:T(8,128)(2,1)S(1)} %whiten_inner.1.refs_1_.own_head.own_tail, bf16[2048,128]{1,0:T(8,128)(2,1)S(1)} %whiten_inner.1.refs_1_.own_head.own_tail, ...), custom_call_target="tpu_custom_call" | custom-call | flops 1000 | bytes 1000 | tf_op jit(solution)/shard_map/correlate_other/pallas_call | solution.py:603
  (6 shorter events, 0.1 us)
Async XLA Ops:
  0.0 4.6 %copy-start = (f32[128,65]{0,1:T(8,128)S(1)}, f32[128,65]{0,1:T(8,128)}, u32[]{:S(2)}) copy-start(f32[128,65]{0,1:T(8,128)} %param.4) | copy-start | bytes 99844
  0.0 4.6 %copy-start.1 = (s32[128]{0:T(128)S(1)}, s32[128]{0:T(128)}, u32[]{:S(2)}) copy-start(s32[128]{0:T(128)} %sources.1) | copy-start | bytes 1540
  1.6 5.2 %collective-permute-start = (f32[128,128]{1,0:T(8,128)S(1)}, f32[128,128]{1,0:T(8,128)S(1)}, u32[]{:S(2)}, u32[]{:S(2)}) collective-permute-start(f32[128,128]{1,0:T(8,128)S(1)} %constant_dynamic-slice_fusion), channel_id=1, source_target_pairs={{0,2},{2,0},{1,3},{3,1},{4,6},{6,4},{5,7},{7,5},{8,10},{10,8},{9,1... | collective-permute-start | bytes 196616 | tf_op jit(solution)/shard_map/ppermute | solution.py:558
  10.1 18.3 %collective-permute-start.2 = (bf16[2048,128]{1,0:T(8,128)(2,1)S(1)}, bf16[2048,128]{1,0:T(8,128)(2,1)S(1)}, u32[]{:S(2)}, u32[]{:S(2)}) collective-permute-start(bf16[2048,128]{1,0:T(8,128)(2,1)S(1)} %whiten_outer.1.after.refs_0_), channel_id=1, source_target_pairs={{0,2},{2,0},{1,3},{3,1},{4,6},{6,4},{5,7},{7,5},{8,10},{10,8},{9,1... | collective-permute-start | bytes 1572872 | tf_op jit(solution)/shard_map/ppermute | solution.py:558
  14.1 8.5 %collective-permute-start.5 = (bf16[16,4096]{1,0:T(8,128)(2,1)S(1)}, bf16[16,4096]{1,0:T(8,128)(2,1)S(1)}, u32[]{:S(2)}, u32[]{:S(2)}) collective-permute-start(bf16[16,4096]{1,0:T(8,128)(2,1)S(1)} %whiten_slots.1._.refs_0_), channel_id=1, source_target_pairs={{0,12},{4,0},{8,4},{12,8},{1,13},{5,1},{9,5},{13,9},{2,14},{6,2},{... | collective-permute-start | bytes 393224 | tf_op jit(solution)/shard_map/ppermute | solution.py:558
  17.7 10.7 %collective-permute-start.4 = (bf16[16,4096]{1,0:T(8,128)(2,1)S(1)}, bf16[16,4096]{1,0:T(8,128)(2,1)S(1)}, u32[]{:S(2)}, u32[]{:S(2)}) collective-permute-start(bf16[16,4096]{1,0:T(8,128)(2,1)S(1)} %whiten_slots.1._.refs_0_), channel_id=1, source_target_pairs={{0,8},{4,12},{8,0},{12,4},{1,9},{5,13},{9,1},{13,5},{2,10},{6,14},... | collective-permute-start | bytes 393224 | tf_op jit(solution)/shard_map/ppermute | solution.py:558
  17.7 10.7 %collective-permute-start.3 = (bf16[16,4096]{1,0:T(8,128)(2,1)S(1)}, bf16[16,4096]{1,0:T(8,128)(2,1)S(1)}, u32[]{:S(2)}, u32[]{:S(2)}) collective-permute-start(bf16[16,4096]{1,0:T(8,128)(2,1)S(1)} %whiten_slots.1._.refs_0_), channel_id=1, source_target_pairs={{0,4},{4,8},{8,12},{12,0},{1,5},{5,9},{9,13},{13,1},{2,6},{6,10},{... | collective-permute-start | bytes 393224 | tf_op jit(solution)/shard_map/ppermute | solution.py:558
  22.0 12.3 %collective-permute-start.1 = (bf16[2048,128]{1,0:T(8,128)(2,1)S(1)}, bf16[2048,128]{1,0:T(8,128)(2,1)S(1)}, u32[]{:S(2)}, u32[]{:S(2)}) collective-permute-start(bf16[2048,128]{1,0:T(8,128)(2,1)S(1)} %whiten_inner.1.refs_1_.own_head.own_tail), channel_id=1, source_target_pairs={{0,2},{2,0},{1,3},{3,1},{4,6},{6,4},{5,7},{7,5},{8,10},{10,8},{9,1... | collective-permute-start | bytes 1572872 | tf_op jit(solution)/shard_map/ppermute | solution.py:558
  28.4 5.9 %collective-permute-start.6 = (bf16[64,4096]{1,0:T(8,128)(2,1)S(1)}, bf16[64,4096]{1,0:T(8,128)(2,1)S(1)}, u32[]{:S(2)}, u32[]{:S(2)}) collective-permute-start(bf16[64,4096]{1,0:T(8,128)(2,1)S(1)} %join_slots.1.refs_0_), channel_id=1, source_target_pairs={{0,1},{1,0},{2,3},{3,2},{4,5},{5,4},{6,7},{7,6},{8,9},{9,8},{10,11... | collective-permute-start | bytes 1572872 | tf_op jit(solution)/shard_map/ppermute | solution.py:558
  34.8 12.0 %collective-permute-start.7 = (bf16[64,4096]{1,0:T(8,128)(2,1)S(1)}, bf16[64,4096]{1,0:T(8,128)(2,1)S(1)}, u32[]{:S(2)}, u32[]{:S(2)}) collective-permute-start(bf16[64,4096]{1,0:T(8,128)(2,1)S(1)} %get-tuple-element.18), channel_id=1, source_target_pairs={{0,2},{2,0},{1,3},{3,1},{4,6},{6,4},{5,7},{7,5},{8,10},{10,8},{9,1... | collective-permute-start | bytes 1572872 | tf_op jit(solution)/shard_map/ppermute | solution.py:558

commit v3 on v2

--- a/solution.py
+++ b/solution.py
@@ -13,6 +13,7 @@
 TILE = 128
 FINE = 16
 SETS = 24
+ARRIVED = 2
 F32 = jnp.float32
 BF16 = jnp.bfloat16
 VMEM_BYTES = 24 * 2**20
@@ -326,28 +327,6 @@
     )(traces, sets, beside, after)
 
 
-def join_kernel(parts, count, after, *refs):
-    size = refs[0].shape[0]
-    each = count // parts
-    for n in range(parts):
-        for i in range(each):
-            refs[count + n][i * size : (i + 1) * size, :] = refs[n * each + i][...]
-
-
-def join(after, parts, pieces):
-    size, length = parts[0].shape
-    shape = jax.ShapeDtypeStruct((size * len(parts) // pieces, length), BF16)
-    return pl.pallas_call(
-        functools.partial(join_kernel, pieces, len(parts)),
-        out_shape=(shape,) * pieces,
-        in_specs=[ANY] + vmem(len(parts)),
-        out_specs=tuple(vmem(pieces)),
-        compiler_params=params(),
-        cost_estimate=light(),
-        name="join_slots",
-    )(after, *parts)
-
-
 def order_kernel(ring, count, choose, after, *refs):
     parts, (*outs, gathered) = refs[:count], refs[count:]
     step = parts[0].shape[0]
@@ -356,17 +335,21 @@
     if not ring:
         outs[0][...] = jnp.dot(choose[...].astype(BF16), gathered[...], preferred_element_type=F32).astype(BF16)
         return
-    own, send = outs
-    half, length = send.shape
+    own, *sends = outs
+    half, length = own.shape[0], sends[0].shape[1]
     here = lax.axis_index("tm")
     mine = choose[pl.ds(pl.multiple_of(here * half, half), half), :]
-    theirs = choose[pl.ds(pl.multiple_of((1 - here) * half, half), half), :]
+    few = half // 2
+    other = (1 - here) * half + lax.axis_index("sub") * few
+    theirs = choose[pl.ds(pl.multiple_of(other, few), few), :]
     wanted = jnp.concatenate([mine, theirs], 0).astype(BF16)
     got = jnp.dot(wanted, gathered[...], preferred_element_type=F32).astype(BF16)
     own[:, 0:TILE] = jnp.zeros((half, TILE), BF16)
     own[:, TILE + length :] = jnp.zeros((half, TILE), BF16)
     own[:, TILE : TILE + length] = got[:half]
-    send[...] = got[half:]
+    size = sends[0].shape[0]
+    for n, send in enumerate(sends):
+        send[...] = got[half + n * size : half + (n + 1) * size]
 
 
 def order(choose, after, parts, ring):
@@ -376,9 +359,9 @@
         half = partners // 2
         out_shape = (
             jax.ShapeDtypeStruct((half, length + 2 * TILE), BF16),
-            jax.ShapeDtypeStruct((half, length), BF16),
+            *[jax.ShapeDtypeStruct((half // ARRIVED, length), BF16)] * (ARRIVED // 2),
         )
-        out_specs = tuple(vmem(2))
+        out_specs = tuple(vmem(1 + ARRIVED // 2))
     else:
         out_shape = jax.ShapeDtypeStruct((partners, length), BF16)
         out_specs = vmem(1)[0]
@@ -449,7 +432,7 @@
     term = None
     for copies, begin in zip(shifted, start):
         cols = [chan[pl.ds(begin + TILE - FINE * (a + i), width), :] for i in range(2)]
-        piece = jnp.dot(copies[:used, :], jnp.concatenate(cols, 1), preferred_element_type=F32)
+        piece = jnp.dot(copies[:used, :width], jnp.concatenate(cols, 1), preferred_element_type=F32)
         term = piece if term is None else term + piece
     for i in range(2):
         size = used if i == 1 else rows * FINE
@@ -465,26 +448,23 @@
     rest = width % chunk
     count = width // chunk
     begin = [pl.multiple_of(start + rest + i * chunk, TILE) for i in range(count)]
-    if rest:
-        lay_out(part, spare[3], start, rest)
-    lay_out(part, spare[0], begin[0], chunk)
+    buffers = [spare[3] if rest and i == 0 else spare[i % 3] for i in range(count)]
+    widths = [chunk + rest if i == 0 else chunk for i in range(count)]
+    begin[0] = start
+    lay_out(part, buffers[0], start, widths[0])
     for copy in ready:
         copy.wait()
-    if rest:
+    for i in range(count - 2):
+        lay_out(part, buffers[i + 1], begin[i + 1], chunk)
+        if i == count - 3:
+            lay_out(part, buffers[i + 2], begin[i + 2], chunk)
         for a in pairs:
-            add_pair([spare[3]], chan, before, total, [start], rest, rows, a, None)
-        before = total
-    for i in range(count - 2):
-        lay_out(part, spare[(i + 1) % 3], begin[i + 1], chunk)
-        if i == count - 3:
-            lay_out(part, spare[(i + 2) % 3], begin[i + 2], chunk)
-        for a in pairs:
-            add_pair([spare[i % 3]], chan, before, total, [begin[i]], chunk, rows, a, None)
+            add_pair([buffers[i]], chan, before, total, [begin[i]], widths[i], rows, a, None)
         before = total
     stores = []
     for n, a in enumerate(pairs):
         ends = (count - 2, count - 1)
-        add_pair([spare[i % 3] for i in ends], chan, before, total, [begin[i] for i in ends], chunk, rows, a, scale)
+        add_pair([buffers[i] for i in ends], chan, before, total, [begin[i] for i in ends], chunk, rows, a, scale)
         if out is not None:
             at = 2 * n * FINE * rows
             size = rows * (2 * FINE + (1 if a + 2 == (LAGS - 1) // FINE else 0))
@@ -519,14 +499,20 @@
     correlate_ring(part, chan, total, (a, b, c, d), start, length, chunk, part.shape[0], ready, None, None, None, sems)
 
 
-def second_kernel(chunk, scale, count, own_part, other_part, own_head, own_tail, before, *refs):
+def second_kernel(chunk, scale, count, own_part, *refs):
+    arrived, (own_head, own_tail, before, *refs) = refs[:ARRIVED], refs[ARRIVED:]
     pieces, (out, total, part, chan, a, b, c, d, sems) = refs[:count], refs[count:]
     length = part.shape[1] - 2 * TILE
     rows = part.shape[0]
     here = lax.axis_index("tm")
     ready = place_pieces(here > 0, pieces, chan, length, sems)
     later = here > 0
-    part[:, TILE : TILE + length] = other_part[...]
+    few = arrived[0].shape[0]
+    core = lax.axis_index("sub")
+    for n, piece in enumerate(arrived):
+        n = n + core * ARRIVED // 2
+        at = jnp.where(n < ARRIVED, n, n - ARRIVED) * few
+        part[pl.ds(pl.multiple_of(at, few), few), TILE : TILE + length] = piece[...]
     part[:, 0:TILE] = jnp.where(later, 0, own_part[:, length : length + TILE]).astype(BF16)
     part[:, TILE + length :] = jnp.where(later, own_part[:, TILE : 2 * TILE], 0).astype(BF16)
     chan[0:TILE, :] = jnp.where(later, 0, own_tail[own_tail.shape[0] - TILE :, :]).astype(BF16)
@@ -577,16 +563,15 @@
         edge = lax.dynamic_slice_in_dim(traces, jnp.where(here == 0, length - TILE, 0), TILE, 1)
         beside = shifted(edge, "tm", 1)
         far = length // 2
-        outer = whiten_part(count, held, sets, beside, beside, (length // 2,), False)
+        outer = whiten_part(count, held, sets, beside, beside, (far,), False)
         other_outer = [shifted(piece, "tm", 1) for piece in outer]
         picked = whiten_slots(sizes, count, slot_rows, held, beside, beside, chan_taps, outer[0], slots)
-        inner = whiten_part(count, held, sets, beside, picked, (length // 2,), True)
+        inner = whiten_part(count, held, sets, beside, picked, (length - far,), True)
         other_inner = [shifted(piece, "tm", 1) for piece in inner]
-        near = [picked] + [shifted(picked, "chan", step) for step in range(1, chan_devs)]
-        mine = join(other_outer[0], near, 1)
+        mine = [picked] + [shifted(picked, "chan", step) for step in range(1, chan_devs)]
         theirs = [shifted(part, "sub", 1) for part in mine]
-        own_part, send = order(choose, other_inner[0], [*mine, *theirs], True)
-        other_part = shifted(send, "tm", 1)
+        own_part, *send = order(choose, other_outer[0], [*mine, *theirs], True)
+        near_rows = [shifted(part, "tm", 1) for part in send]
         pieces = len(outer) + len(inner)
         before = pl.pallas_call(
             functools.partial(first_kernel, chunk, pieces),
@@ -594,28 +579,30 @@
             in_specs=vmem(1) + [ANY] * pieces,
             out_specs=vmem(1)[0],
             scratch_shapes=[pltpu.VMEM((length + 2 * TILE, chans), BF16)]
-            + spare(rows, (chunk, chunk, chunk, TILE))
+            + spare(rows, (chunk, chunk, chunk, chunk + TILE))
             + [pltpu.SemaphoreType.DMA((4 + pieces,))],
             compiler_params=params(),
             cost_estimate=light(),
             name="correlate_own",
         )(own_part, *outer, *inner)
+        near_rows, other_inner, before = lax.optimization_barrier((near_rows, other_inner, before))
+        far_rows = [shifted(part, "sub", 1) for part in near_rows]
         total = pl.pallas_call(
             functools.partial(second_kernel, chunk, scale, pieces),
             out_shape=out_shape,
-            in_specs=vmem(5) + [ANY] * pieces,
+            in_specs=vmem(4 + 2 * len(send)) + [ANY] * pieces,
             out_specs=ANY,
             scratch_shapes=[
                 pltpu.VMEM(out_shape.shape, F32),
                 pltpu.VMEM((rows, length + 2 * TILE), BF16),
                 pltpu.VMEM((length + 2 * TILE, chans), BF16),
             ]
-            + spare(rows, (chunk, chunk, chunk, TILE))
+            + spare(rows, (chunk, chunk, chunk, chunk + TILE))
             + [pltpu.SemaphoreType.DMA((4 + pieces,))],
             compiler_params=params(),
             cost_estimate=light(),
             name="correlate_other",
-        )(own_part, other_part, inner[0], inner[-1], before, *other_outer, *other_inner)
+        )(own_part, *near_rows, *far_rows, inner[0], inner[-1], before, *other_outer, *other_inner)
     else:
         low = lax.ppermute(traces[:, length - TILE :], "tm", [(i, i + 1) for i in range(time_devs - 1)])
         high = lax.ppermute(traces[:, :TILE], "tm", [(i + 1, i) for i in range(time_devs - 1)])

time: 59.1 us -> 56.1 us (0.949)
  waiting for transfers between devices: 12.6 us -> 10.2 us
    ppermute x8 -> x12, waiting for transfers between devices: 12.6 us -> 10.2 us  [shifted(): lax.ppermute(array, axis, [(i, (i + step) % count) for i in range(count)])]
    ppermute x8 -> x12, starting transfers between devices: 12.1 us -> 11.7 us  [shifted(): lax.ppermute(array, axis, [(i, (i + step) % count) for i in range(count)])]
  transfers between devices with their start and end apart: 8 -> 12, of which waited for: 4 -> 5; matrix products, arithmetic and copies ran while one was open for 0% -> 0% of each run, Pallas kernels for 28% -> 30%
where the time goes in v3:
time: 56.1 us; the launch traced here: 55.9 us
  Pallas kernels  32.2 us (57%)
  starting transfers between devices  11.7 us (21%)
  waiting for transfers between devices  10.2 us (18%)
  local copies, waits for them, and re-layouts  1.61 us (3%)
    pallas_call x1, Pallas kernels, on_device(): pl.pallas_call(functools.partial(second_kernel, chunk, scale, pieces), ou...  12 us
    ppermute x12, starting transfers between devices, shifted(): lax.ppermute(array, axis, [(i, (i + step) % count) for i in range(count)])  11.7 us
    ppermute x12, waiting for transfers between devices, shifted(): lax.ppermute(array, axis, [(i, (i + step) % count) for i in range(count)])  10.2 us
    pallas_call x1, Pallas kernels, on_device(): pl.pallas_call(functools.partial(first_kernel, chunk, pieces), out_shape=...  9.78 us
    pallas_call x2, Pallas kernels, whiten_part(): pl.pallas_call(functools.partial(whiten_part_kernel, taps, rows, inner),...  6.51 us
    pallas_call x1, Pallas kernels, whiten_slots(): pl.pallas_call(functools.partial(slots_kernel, taps, sizes), out_shape=ja...  1.86 us
    pallas_call x1, Pallas kernels, prepare(): pl.pallas_call(functools.partial(prepare_kernel, sizes, chans, ring, slot...  1.74 us
    unnamed x5, local copies, waits for them, and re-layouts  1.6 us
  transfers between devices with their start and end apart: 12, of which 5 were waited for; matrix products, arithmetic and copies ran while one was open for 0% of the time, Pallas kernels for 30%

profile of v3, /device:TPU:0, one launch (start us, length us, event | category | flops | bytes accessed | tf_op | source)
XLA Modules:
  0.0 55.9 jit_solution(15097487988765900634)
XLA Ops:
  0.0 1.6 %copy.7._ = f32[128,4096]{1,0:T(8,128)S(1)} copy(f32[128,4096]{1,0:T(8,128)} %param.3) | data formatting | bytes 4194304
  1.6 3.0 %collective-permute-start = (f32[128,128]{1,0:T(8,128)S(1)}, f32[128,128]{1,0:T(8,128)S(1)}, u32[]{:S(2)}, u32[]{:S(2)}) collective-permute-start(f32[128,128]{1,0:T(8,128)S(1)} %constant_dynamic-slice_fusion), channel_id=1, source_target_pairs={{0,2},{2,0},{1,3},{3,1},{4,6},{6,4},{5,7},{7,5},{8,10},{10,8},{9,1... | collective-permute-start | bytes 196616 | tf_op jit(solution)/shard_map/ppermute | solution.py:544
  4.6 1.7 %prepare.1 = (s32[17]{0:T(128)S(1)}, f32[216,128]{1,0:T(8,128)S(1)}, f32[128,128]{1,0:T(8,128)S(1)}, f32[128,128]{1,0:T(8,128)S(1)}, f32[128,4096]{1,0:T(8,128)S(1)}) custom-call(s32[128]{0:T(128)S(1)} %copy-done.1, s32[1,128]{1,0:T(1,128)S(1)} %bitcast.6, f32[65,128]{1,0:T(8,128)S(1)} %bitcast.5, ...), custom_call_target="tpu_custom_call", output_to_operand_aliasing={{4}: (3, {})} | custom-call | flops 1000 | bytes 1000 | tf_op jit(solution)/shard_map/prepare/pallas_call | solution.py:165
  6.4 0.5 collective-permute-done.beside._.low.high
  6.9 3.3 %whiten_outer.1.after.refs_0_ = bf16[2048,128]{1,0:T(8,128)(2,1)S(1)} custom-call(f32[128,4096]{1,0:T(8,128)S(1)} %get-tuple-element.16.x, f32[216,128]{1,0:T(8,128)S(1)} %get-tuple-element.17.sets, f32[128,128]{1,0:T(8,128)S(1)} %collective-permute-done.beside._.low.high, f32[128,128]{1,0:T(8,128)S(1)} %collective-permute-done.beside._.low.high), custom_call_target="tpu_custom_call" | custom-call | flops 1000 | bytes 1000 | tf_op jit(solution)/shard_map/whiten_outer/pallas_call | solution.py:318
  10.1 2.1 %collective-permute-start.1 = (bf16[2048,128]{1,0:T(8,128)(2,1)S(1)}, bf16[2048,128]{1,0:T(8,128)(2,1)S(1)}, u32[]{:S(2)}, u32[]{:S(2)}) collective-permute-start(bf16[2048,128]{1,0:T(8,128)(2,1)S(1)} %whiten_outer.1.after.refs_0_), channel_id=1, source_target_pairs={{0,2},{2,0},{1,3},{3,1},{4,6},{6,4},{5,7},{7,5},{8,10},{10,8},{9,1... | collective-permute-start | bytes 1572872 | tf_op jit(solution)/shard_map/ppermute | solution.py:544
  12.2 1.9 %whiten_slots.1.refs_0_._ = bf16[16,4096]{1,0:T(8,128)(2,1)S(1)} custom-call(s32[17]{0:T(128)S(1)} %get-tuple-element.18.rows, f32[128,4096]{1,0:T(8,128)S(1)} %get-tuple-element.16.x, f32[128,128]{1,0:T(8,128)S(1)} %collective-permute-done.beside._.low.high, f32[128,128]{1,0:T(8,128)S(1)} %collective-permute-done.beside._.low.high, ...), custom_call_target="tpu_custom_call" | custom-call | flops 1000 | bytes 1000 | tf_op jit(solution)/shard_map/whiten_slots/pallas_call | solution.py:222
  14.1 0.1 collective-permute-start.5
  14.2 3.7 %collective-permute-start.4 = (bf16[16,4096]{1,0:T(8,128)(2,1)S(1)}, bf16[16,4096]{1,0:T(8,128)(2,1)S(1)}, u32[]{:S(2)}, u32[]{:S(2)}) collective-permute-start(bf16[16,4096]{1,0:T(8,128)(2,1)S(1)} %whiten_slots.1.refs_0_._), channel_id=1, source_target_pairs={{0,12},{4,0},{8,4},{12,8},{1,13},{5,1},{9,5},{13,9},{2,14},{6,2},{... | collective-permute-start | bytes 393224 | tf_op jit(solution)/shard_map/ppermute | solution.py:544
  17.8 1.0 %collective-permute-start.2 = (bf16[16,4096]{1,0:T(8,128)(2,1)S(1)}, bf16[16,4096]{1,0:T(8,128)(2,1)S(1)}, u32[]{:S(2)}, u32[]{:S(2)}) collective-permute-start(bf16[16,4096]{1,0:T(8,128)(2,1)S(1)} %whiten_slots.1.refs_0_._), channel_id=1, source_target_pairs={{0,4},{4,8},{8,12},{12,0},{1,5},{5,9},{9,13},{13,1},{2,6},{6,10},{... | collective-permute-start | bytes 393224 | tf_op jit(solution)/shard_map/ppermute | solution.py:544
  18.8 3.3 %whiten_inner.1.refs_1_.refs_2_.refs_3_ = bf16[2048,128]{1,0:T(8,128)(2,1)S(1)} custom-call(f32[128,4096]{1,0:T(8,128)S(1)} %get-tuple-element.16.x, f32[216,128]{1,0:T(8,128)S(1)} %get-tuple-element.17.sets, f32[128,128]{1,0:T(8,128)S(1)} %collective-permute-done.beside._.low.high, bf16[16,4096]{1,0:T(8,128)(2,1)S(1)} %whiten_slots.1.refs_0_._), custom_call_target="tpu_custom_call" | custom-call | flops 1000 | bytes 1000 | tf_op jit(solution)/shard_map/whiten_inner/pallas_call | solution.py:318
  22.1 0.0 collective-permute-done.5.refs_4_
  22.1 0.6 %collective-permute-start.10 = (bf16[2048,128]{1,0:T(8,128)(2,1)S(1)}, bf16[2048,128]{1,0:T(8,128)(2,1)S(1)}, u32[]{:S(2)}, u32[]{:S(2)}) collective-permute-start(bf16[2048,128]{1,0:T(8,128)(2,1)S(1)} %whiten_inner.1.refs_1_.refs_2_.refs_3_), channel_id=1, source_target_pairs={{0,2},{2,0},{1,3},{3,1},{4,6},{6,4},{5,7},{7,5},{8,10},{10,8},{9,1... | collective-permute-start | bytes 1572872 | tf_op jit(solution)/shard_map/ppermute | solution.py:544
  22.7 0.0 collective-permute-start.8
  22.7 7.2 %collective-permute-done.3.refs_2_ = bf16[16,4096]{1,0:T(8,128)(2,1)S(1)} collective-permute-done((bf16[16,4096]{1,0:T(8,128)(2,1)S(1)}, bf16[16,4096]{1,0:T(8,128)(2,1)S(1)}, u32[]{:S(2)}, u32[]{:S(2)}) %collective-permute-start.3) | collective-permute-done | bytes 131104 | tf_op jit(solution)/shard_map/ppermute | solution.py:544
  29.9 0.5 collective-permute-start.6
  30.4 0.8 %collective-permute-done.7.refs_6_ = bf16[16,4096]{1,0:T(8,128)(2,1)S(1)} collective-permute-done((bf16[16,4096]{1,0:T(8,128)(2,1)S(1)}, bf16[16,4096]{1,0:T(8,128)(2,1)S(1)}, u32[]{:S(2)}, u32[]{:S(2)}) %collective-permute-start.7) | collective-permute-done | bytes 131104 | tf_op jit(solution)/shard_map/ppermute | solution.py:544
  31.2 0.2 collective-permute-done.6.refs_5_
  31.4 0.4 order_partners.1
  31.8 0.6 %collective-permute-start.9 = (bf16[32,4096]{1,0:T(8,128)(2,1)S(1)}, bf16[32,4096]{1,0:T(8,128)(2,1)S(1)}, u32[]{:S(2)}, u32[]{:S(2)}) collective-permute-start(bf16[32,4096]{1,0:T(8,128)(2,1)S(1)} %get-tuple-element.21), channel_id=1, source_target_pairs={{0,2},{2,0},{1,3},{3,1},{4,6},{6,4},{5,7},{7,5},{8,10},{10,8},{9,1... | collective-permute-start | bytes 786440 | tf_op jit(solution)/shard_map/ppermute | solution.py:544
  32.4 9.8 %correlate_own.1.refs_4_ = f32[8256,128]{1,0:T(8,128)S(1)} custom-call(bf16[64,4352]{1,0:T(8,128)(2,1)S(1)} %get-tuple-element.20.part.own_part, bf16[2048,128]{1,0:T(8,128)(2,1)S(1)} %whiten_outer.1.after.refs_0_, bf16[2048,128]{1,0:T(8,128)(2,1)S(1)} %whiten_inner.1.refs_1_.refs_2_.refs_3_), custom_call_target="tpu_custom_call" | custom-call | flops 1000 | bytes 1000 | tf_op jit(solution)/shard_map/correlate_own/pallas_call | solution.py:576
  42.2 0.1 collective-permute-start.11
  42.3 1.5 %collective-permute-done.11.refs_1_ = bf16[32,4096]{1,0:T(8,128)(2,1)S(1)} collective-permute-done((bf16[32,4096]{1,0:T(8,128)(2,1)S(1)}, bf16[32,4096]{1,0:T(8,128)(2,1)S(1)}, u32[]{:S(2)}, u32[]{:S(2)}) %collective-permute-start.11) | collective-permute-done | bytes 262176 | tf_op jit(solution)/shard_map/ppermute | solution.py:544
  43.8 12.0 %correlate_other.1 = f32[8256,128]{1,0:T(8,128)} custom-call(bf16[64,4352]{1,0:T(8,128)(2,1)S(1)} %get-tuple-element.20.part.own_part, bf16[32,4096]{1,0:T(8,128)(2,1)S(1)} %collective-permute-done.9.refs_0_, bf16[32,4096]{1,0:T(8,128)(2,1)S(1)} %collective-permute-done.11.refs_1_, bf16[2048,128]{1,0:T(8,128)(2,1)S(1)} %whiten_inner.1.refs_1_.refs_2_.refs_3_, ...), custom_call_target="tpu_custom_call" | custom-call | flops 1000 | bytes 1000 | tf_op jit(solution)/shard_map/correlate_other/pallas_call | solution.py:590
  (13 shorter events, 0.0 us)
Async XLA Ops:
  0.0 4.6 %copy-start = (f32[128,65]{0,1:T(8,128)S(1)}, f32[128,65]{0,1:T(8,128)}, u32[]{:S(2)}) copy-start(f32[128,65]{0,1:T(8,128)} %param.4) | copy-start | bytes 99844
  0.0 4.6 %copy-start.1 = (s32[128]{0:T(128)S(1)}, s32[128]{0:T(128)}, u32[]{:S(2)}) copy-start(s32[128]{0:T(128)} %sources.1) | copy-start | bytes 1540
  1.6 5.2 %collective-permute-start = (f32[128,128]{1,0:T(8,128)S(1)}, f32[128,128]{1,0:T(8,128)S(1)}, u32[]{:S(2)}, u32[]{:S(2)}) collective-permute-start(f32[128,128]{1,0:T(8,128)S(1)} %constant_dynamic-slice_fusion), channel_id=1, source_target_pairs={{0,2},{2,0},{1,3},{3,1},{4,6},{6,4},{5,7},{7,5},{8,10},{10,8},{9,1... | collective-permute-start | bytes 196616 | tf_op jit(solution)/shard_map/ppermute | solution.py:544
  10.1 21.3 %collective-permute-start.1 = (bf16[2048,128]{1,0:T(8,128)(2,1)S(1)}, bf16[2048,128]{1,0:T(8,128)(2,1)S(1)}, u32[]{:S(2)}, u32[]{:S(2)}) collective-permute-start(bf16[2048,128]{1,0:T(8,128)(2,1)S(1)} %whiten_outer.1.after.refs_0_), channel_id=1, source_target_pairs={{0,2},{2,0},{1,3},{3,1},{4,6},{6,4},{5,7},{7,5},{8,10},{10,8},{9,1... | collective-permute-start | bytes 1572872 | tf_op jit(solution)/shard_map/ppermute | solution.py:544
  14.1 8.0 %collective-permute-start.5 = (bf16[16,4096]{1,0:T(8,128)(2,1)S(1)}, bf16[16,4096]{1,0:T(8,128)(2,1)S(1)}, u32[]{:S(2)}, u32[]{:S(2)}) collective-permute-start(bf16[16,4096]{1,0:T(8,128)(2,1)S(1)} %whiten_slots.1.refs_0_._), channel_id=1, source_target_pairs={{0,1},{1,0},{2,3},{3,2},{4,5},{5,4},{6,7},{7,6},{8,9},{9,8},{10,11... | collective-permute-start | bytes 393224 | tf_op jit(solution)/shard_map/ppermute | solution.py:544
  14.2 8.5 %collective-permute-start.4 = (bf16[16,4096]{1,0:T(8,128)(2,1)S(1)}, bf16[16,4096]{1,0:T(8,128)(2,1)S(1)}, u32[]{:S(2)}, u32[]{:S(2)}) collective-permute-start(bf16[16,4096]{1,0:T(8,128)(2,1)S(1)} %whiten_slots.1.refs_0_._), channel_id=1, source_target_pairs={{0,12},{4,0},{8,4},{12,8},{1,13},{5,1},{9,5},{13,9},{2,14},{6,2},{... | collective-permute-start | bytes 393224 | tf_op jit(solution)/shard_map/ppermute | solution.py:544
  17.8 12.1 %collective-permute-start.3 = (bf16[16,4096]{1,0:T(8,128)(2,1)S(1)}, bf16[16,4096]{1,0:T(8,128)(2,1)S(1)}, u32[]{:S(2)}, u32[]{:S(2)}) collective-permute-start(bf16[16,4096]{1,0:T(8,128)(2,1)S(1)} %whiten_slots.1.refs_0_._), channel_id=1, source_target_pairs={{0,8},{4,12},{8,0},{12,4},{1,9},{5,13},{9,1},{13,5},{2,10},{6,14},... | collective-permute-start | bytes 393224 | tf_op jit(solution)/shard_map/ppermute | solution.py:544
  17.8 12.1 %collective-permute-start.2 = (bf16[16,4096]{1,0:T(8,128)(2,1)S(1)}, bf16[16,4096]{1,0:T(8,128)(2,1)S(1)}, u32[]{:S(2)}, u32[]{:S(2)}) collective-permute-start(bf16[16,4096]{1,0:T(8,128)(2,1)S(1)} %whiten_slots.1.refs_0_._), channel_id=1, source_target_pairs={{0,4},{4,8},{8,12},{12,0},{1,5},{5,9},{9,13},{13,1},{2,6},{6,10},{... | collective-permute-start | bytes 393224 | tf_op jit(solution)/shard_map/ppermute | solution.py:544
  22.1 20.1 %collective-permute-start.10 = (bf16[2048,128]{1,0:T(8,128)(2,1)S(1)}, bf16[2048,128]{1,0:T(8,128)(2,1)S(1)}, u32[]{:S(2)}, u32[]{:S(2)}) collective-permute-start(bf16[2048,128]{1,0:T(8,128)(2,1)S(1)} %whiten_inner.1.refs_1_.refs_2_.refs_3_), channel_id=1, source_target_pairs={{0,2},{2,0},{1,3},{3,1},{4,6},{6,4},{5,7},{7,5},{8,10},{10,8},{9,1... | collective-permute-start | bytes 1572872 | tf_op jit(solution)/shard_map/ppermute | solution.py:544
  22.7 7.7 %collective-permute-start.8 = (bf16[16,4096]{1,0:T(8,128)(2,1)S(1)}, bf16[16,4096]{1,0:T(8,128)(2,1)S(1)}, u32[]{:S(2)}, u32[]{:S(2)}) collective-permute-start(bf16[16,4096]{1,0:T(8,128)(2,1)S(1)} %collective-permute-done.4.refs_3_), channel_id=1, source_target_pairs={{0,1},{1,0},{2,3},{3,2},{4,5},{5,4},{6,7},{7,6},{8,9},{9,8},{10,11... | collective-permute-start | bytes 393224 | tf_op jit(solution)/shard_map/ppermute | solution.py:544
  29.9 1.3 %collective-permute-start.7 = (bf16[16,4096]{1,0:T(8,128)(2,1)S(1)}, bf16[16,4096]{1,0:T(8,128)(2,1)S(1)}, u32[]{:S(2)}, u32[]{:S(2)}) collective-permute-start(bf16[16,4096]{1,0:T(8,128)(2,1)S(1)} %collective-permute-done.3.refs_2_), channel_id=1, source_target_pairs={{0,1},{1,0},{2,3},{3,2},{4,5},{5,4},{6,7},{7,6},{8,9},{9,8},{10,11... | collective-permute-start | bytes 393224 | tf_op jit(solution)/shard_map/ppermute | solution.py:544
  29.9 1.5 %collective-permute-start.6 = (bf16[16,4096]{1,0:T(8,128)(2,1)S(1)}, bf16[16,4096]{1,0:T(8,128)(2,1)S(1)}, u32[]{:S(2)}, u32[]{:S(2)}) collective-permute-start(bf16[16,4096]{1,0:T(8,128)(2,1)S(1)} %collective-permute-done.2.refs_1_), channel_id=1, source_target_pairs={{0,1},{1,0},{2,3},{3,2},{4,5},{5,4},{6,7},{7,6},{8,9},{9,8},{10,11... | collective-permute-start | bytes 393224 | tf_op jit(solution)/shard_map/ppermute | solution.py:544
  31.8 10.4 %collective-permute-start.9 = (bf16[32,4096]{1,0:T(8,128)(2,1)S(1)}, bf16[32,4096]{1,0:T(8,128)(2,1)S(1)}, u32[]{:S(2)}, u32[]{:S(2)}) collective-permute-start(bf16[32,4096]{1,0:T(8,128)(2,1)S(1)} %get-tuple-element.21), channel_id=1, source_target_pairs={{0,2},{2,0},{1,3},{3,1},{4,6},{6,4},{5,7},{7,5},{8,10},{10,8},{9,1... | collective-permute-start | bytes 786440 | tf_op jit(solution)/shard_map/ppermute | solution.py:544
  42.2 1.6 %collective-permute-start.11 = (bf16[32,4096]{1,0:T(8,128)(2,1)S(1)}, bf16[32,4096]{1,0:T(8,128)(2,1)S(1)}, u32[]{:S(2)}, u32[]{:S(2)}) collective-permute-start(bf16[32,4096]{1,0:T(8,128)(2,1)S(1)} %collective-permute-done.9.refs_0_), channel_id=1, source_target_pairs={{0,1},{1,0},{2,3},{3,2},{4,5},{5,4},{6,7},{7,6},{8,9},{9,8},{10,11... | collective-permute-start | bytes 786440 | tf_op jit(solution)/shard_map/ppermute | solution.py:544

commit v4 on v3

--- a/solution.py
+++ b/solution.py
@@ -563,7 +563,8 @@
         edge = lax.dynamic_slice_in_dim(traces, jnp.where(here == 0, length - TILE, 0), TILE, 1)
         beside = shifted(edge, "tm", 1)
         far = length // 2
-        outer = whiten_part(count, held, sets, beside, beside, (far,), False)
+        outer = whiten_part(count, held, sets, edge, edge, (far,), False)
+        beside, *outer = lax.optimization_barrier((beside, *outer))
         other_outer = [shifted(piece, "tm", 1) for piece in outer]
         picked = whiten_slots(sizes, count, slot_rows, held, beside, beside, chan_taps, outer[0], slots)
         inner = whiten_part(count, held, sets, beside, picked, (length - far,), True)

time: 56.1 us -> 55.1 us (0.982)
  waiting for transfers between devices: 10.2 us -> 8.76 us
    ppermute x12, waiting for transfers between devices: 10.2 us -> 8.76 us  [shifted(): lax.ppermute(array, axis, [(i, (i + step) % count) for i in range(count)])]
  transfers between devices with their start and end apart: 12 -> 12, of which waited for: 5 -> 4; matrix products, arithmetic and copies ran while one was open for 0% -> 0% of each run, Pallas kernels for 30% -> 37%
where the time goes in v4:
time: 55.1 us; the launch traced here: 55 us
  Pallas kernels  32.2 us (58%)
  starting transfers between devices  12.1 us (22%)
  waiting for transfers between devices  8.76 us (16%)
  local copies, waits for them, and re-layouts  1.61 us (3%)
    ppermute x12, starting transfers between devices, shifted(): lax.ppermute(array, axis, [(i, (i + step) % count) for i in range(count)])  12.1 us
    pallas_call x1, Pallas kernels, on_device(): pl.pallas_call(functools.partial(second_kernel, chunk, scale, pieces), ou...  12 us
    pallas_call x1, Pallas kernels, on_device(): pl.pallas_call(functools.partial(first_kernel, chunk, pieces), out_shape=...  9.78 us
    ppermute x12, waiting for transfers between devices, shifted(): lax.ppermute(array, axis, [(i, (i + step) % count) for i in range(count)])  8.76 us
    pallas_call x2, Pallas kernels, whiten_part(): pl.pallas_call(functools.partial(whiten_part_kernel, taps, rows, inner),...  6.53 us
    pallas_call x1, Pallas kernels, whiten_slots(): pl.pallas_call(functools.partial(slots_kernel, taps, sizes), out_shape=ja...  1.85 us
    pallas_call x1, Pallas kernels, prepare(): pl.pallas_call(functools.partial(prepare_kernel, sizes, chans, ring, slot...  1.74 us
    unnamed x5, local copies, waits for them, and re-layouts  1.6 us
  transfers between devices with their start and end apart: 12, of which 4 were waited for; matrix products, arithmetic and copies ran while one was open for 0% of the time, Pallas kernels for 37%

profile of v4, /device:TPU:0, one launch (start us, length us, event | category | flops | bytes accessed | tf_op | source)
XLA Modules:
  0.0 55.0 jit_solution(11552150561636193888)
XLA Ops:
  0.0 1.6 %copy.7._ = f32[128,4096]{1,0:T(8,128)S(1)} copy(f32[128,4096]{1,0:T(8,128)} %param.3) | data formatting | bytes 4194304
  1.6 3.0 %collective-permute-start = (f32[128,128]{1,0:T(8,128)S(1)}, f32[128,128]{1,0:T(8,128)S(1)}, u32[]{:S(2)}, u32[]{:S(2)}) collective-permute-start(f32[128,128]{1,0:T(8,128)S(1)} %constant_dynamic-slice_fusion.beside._), channel_id=1, source_target_pairs={{0,2},{2,0},{1,3},{3,1},{4,6},{6,4},{5,7},{7,5},{8,10},{10,8},{9,1... | collective-permute-start | bytes 196616 | tf_op jit(solution)/shard_map/ppermute | solution.py:544
  4.6 1.7 %prepare.1 = (s32[17]{0:T(128)S(1)}, f32[216,128]{1,0:T(8,128)S(1)}, f32[128,128]{1,0:T(8,128)S(1)}, f32[128,128]{1,0:T(8,128)S(1)}, f32[128,4096]{1,0:T(8,128)S(1)}) custom-call(s32[128]{0:T(128)S(1)} %copy-done.1, s32[1,128]{1,0:T(1,128)S(1)} %bitcast.6, f32[65,128]{1,0:T(8,128)S(1)} %bitcast.5, ...), custom_call_target="tpu_custom_call", output_to_operand_aliasing={{4}: (3, {})} | custom-call | flops 1000 | bytes 1000 | tf_op jit(solution)/shard_map/prepare/pallas_call | solution.py:165
  6.4 3.3 %whiten_outer.1.after.refs_0_ = bf16[2048,128]{1,0:T(8,128)(2,1)S(1)} custom-call(f32[128,4096]{1,0:T(8,128)S(1)} %get-tuple-element.18.x, f32[216,128]{1,0:T(8,128)S(1)} %get-tuple-element.19.sets, f32[128,128]{1,0:T(8,128)S(1)} %constant_dynamic-slice_fusion.beside._, f32[128,128]{1,0:T(8,128)S(1)} %constant_dynamic-slice_fusion.beside._), custom_call_target="tpu_custom_call" | custom-call | flops 1000 | bytes 1000 | tf_op jit(solution)/shard_map/whiten_outer/pallas_call | solution.py:318
  9.7 0.1 collective-permute-start.1
  9.7 1.9 %whiten_slots.1.refs_0_._ = bf16[16,4096]{1,0:T(8,128)(2,1)S(1)} custom-call(s32[17]{0:T(128)S(1)} %get-tuple-element.21.rows, f32[128,4096]{1,0:T(8,128)S(1)} %get-tuple-element.18.x, f32[128,128]{1,0:T(8,128)S(1)} %collective-permute-done.low.high.beside, f32[128,128]{1,0:T(8,128)S(1)} %collective-permute-done.low.high.beside, ...), custom_call_target="tpu_custom_call" | custom-call | flops 1000 | bytes 1000 | tf_op jit(solution)/shard_map/whiten_slots/pallas_call | solution.py:222
  11.6 0.1 collective-permute-start.5
  11.7 4.2 %collective-permute-start.4 = (bf16[16,4096]{1,0:T(8,128)(2,1)S(1)}, bf16[16,4096]{1,0:T(8,128)(2,1)S(1)}, u32[]{:S(2)}, u32[]{:S(2)}) collective-permute-start(bf16[16,4096]{1,0:T(8,128)(2,1)S(1)} %whiten_slots.1.refs_0_._), channel_id=1, source_target_pairs={{0,12},{4,0},{8,4},{12,8},{1,13},{5,1},{9,5},{13,9},{2,14},{6,2},{... | collective-permute-start | bytes 393224 | tf_op jit(solution)/shard_map/ppermute | solution.py:544
  15.8 0.0 collective-permute-start.3
  15.9 1.0 %collective-permute-start.2 = (bf16[16,4096]{1,0:T(8,128)(2,1)S(1)}, bf16[16,4096]{1,0:T(8,128)(2,1)S(1)}, u32[]{:S(2)}, u32[]{:S(2)}) collective-permute-start(bf16[16,4096]{1,0:T(8,128)(2,1)S(1)} %whiten_slots.1.refs_0_._), channel_id=1, source_target_pairs={{0,4},{4,8},{8,12},{12,0},{1,5},{5,9},{9,13},{13,1},{2,6},{6,10},{... | collective-permute-start | bytes 393224 | tf_op jit(solution)/shard_map/ppermute | solution.py:544
  16.9 3.3 %whiten_inner.1.refs_1_.refs_2_.refs_3_ = bf16[2048,128]{1,0:T(8,128)(2,1)S(1)} custom-call(f32[128,4096]{1,0:T(8,128)S(1)} %get-tuple-element.18.x, f32[216,128]{1,0:T(8,128)S(1)} %get-tuple-element.19.sets, f32[128,128]{1,0:T(8,128)S(1)} %collective-permute-done.low.high.beside, bf16[16,4096]{1,0:T(8,128)(2,1)S(1)} %whiten_slots.1.refs_0_._), custom_call_target="tpu_custom_call" | custom-call | flops 1000 | bytes 1000 | tf_op jit(solution)/shard_map/whiten_inner/pallas_call | solution.py:318
  20.1 0.0 collective-permute-done.5.refs_4_
  20.1 1.6 %collective-permute-start.10 = (bf16[2048,128]{1,0:T(8,128)(2,1)S(1)}, bf16[2048,128]{1,0:T(8,128)(2,1)S(1)}, u32[]{:S(2)}, u32[]{:S(2)}) collective-permute-start(bf16[2048,128]{1,0:T(8,128)(2,1)S(1)} %whiten_inner.1.refs_1_.refs_2_.refs_3_), channel_id=1, source_target_pairs={{0,2},{2,0},{1,3},{3,1},{4,6},{6,4},{5,7},{7,5},{8,10},{10,8},{9,1... | collective-permute-start | bytes 1572872 | tf_op jit(solution)/shard_map/ppermute | solution.py:544
  21.7 6.2 %collective-permute-done.3.refs_2_ = bf16[16,4096]{1,0:T(8,128)(2,1)S(1)} collective-permute-done((bf16[16,4096]{1,0:T(8,128)(2,1)S(1)}, bf16[16,4096]{1,0:T(8,128)(2,1)S(1)}, u32[]{:S(2)}, u32[]{:S(2)}) %collective-permute-start.3) | collective-permute-done | bytes 131104 | tf_op jit(solution)/shard_map/ppermute | solution.py:544
  27.9 0.0 collective-permute-done.2.refs_1_
  27.9 0.5 collective-permute-start.6
  28.5 0.8 %collective-permute-done.7.refs_6_ = bf16[16,4096]{1,0:T(8,128)(2,1)S(1)} collective-permute-done((bf16[16,4096]{1,0:T(8,128)(2,1)S(1)}, bf16[16,4096]{1,0:T(8,128)(2,1)S(1)}, u32[]{:S(2)}, u32[]{:S(2)}) %collective-permute-start.7) | collective-permute-done | bytes 131104 | tf_op jit(solution)/shard_map/ppermute | solution.py:544
  29.3 0.2 collective-permute-done.6.refs_5_
  29.5 0.4 order_partners.1
  29.8 1.6 %collective-permute-start.9 = (bf16[32,4096]{1,0:T(8,128)(2,1)S(1)}, bf16[32,4096]{1,0:T(8,128)(2,1)S(1)}, u32[]{:S(2)}, u32[]{:S(2)}) collective-permute-start(bf16[32,4096]{1,0:T(8,128)(2,1)S(1)} %get-tuple-element.25), channel_id=1, source_target_pairs={{0,2},{2,0},{1,3},{3,1},{4,6},{6,4},{5,7},{7,5},{8,10},{10,8},{9,1... | collective-permute-start | bytes 786440 | tf_op jit(solution)/shard_map/ppermute | solution.py:544
  31.4 9.8 %correlate_own.1.refs_4_ = f32[8256,128]{1,0:T(8,128)S(1)} custom-call(bf16[64,4352]{1,0:T(8,128)(2,1)S(1)} %get-tuple-element.24.part.own_part, bf16[2048,128]{1,0:T(8,128)(2,1)S(1)} %whiten_outer.1.after.refs_0_, bf16[2048,128]{1,0:T(8,128)(2,1)S(1)} %whiten_inner.1.refs_1_.refs_2_.refs_3_), custom_call_target="tpu_custom_call" | custom-call | flops 1000 | bytes 1000 | tf_op jit(solution)/shard_map/correlate_own/pallas_call | solution.py:577
  41.2 0.1 collective-permute-start.11
  41.3 1.5 %collective-permute-done.11.refs_1_ = bf16[32,4096]{1,0:T(8,128)(2,1)S(1)} collective-permute-done((bf16[32,4096]{1,0:T(8,128)(2,1)S(1)}, bf16[32,4096]{1,0:T(8,128)(2,1)S(1)}, u32[]{:S(2)}, u32[]{:S(2)}) %collective-permute-start.11) | collective-permute-done | bytes 262176 | tf_op jit(solution)/shard_map/ppermute | solution.py:544
  42.8 12.0 %correlate_other.1 = f32[8256,128]{1,0:T(8,128)} custom-call(bf16[64,4352]{1,0:T(8,128)(2,1)S(1)} %get-tuple-element.24.part.own_part, bf16[32,4096]{1,0:T(8,128)(2,1)S(1)} %collective-permute-done.9.refs_0_, bf16[32,4096]{1,0:T(8,128)(2,1)S(1)} %collective-permute-done.11.refs_1_, bf16[2048,128]{1,0:T(8,128)(2,1)S(1)} %whiten_inner.1.refs_1_.refs_2_.refs_3_, ...), custom_call_target="tpu_custom_call" | custom-call | flops 1000 | bytes 1000 | tf_op jit(solution)/shard_map/correlate_other/pallas_call | solution.py:591
  (13 shorter events, 0.0 us)
Async XLA Ops:
  0.0 4.6 %copy-start = (f32[128,65]{0,1:T(8,128)S(1)}, f32[128,65]{0,1:T(8,128)}, u32[]{:S(2)}) copy-start(f32[128,65]{0,1:T(8,128)} %param.4) | copy-start | bytes 99844
  0.0 4.6 %copy-start.1 = (s32[128]{0:T(128)S(1)}, s32[128]{0:T(128)}, u32[]{:S(2)}) copy-start(s32[128]{0:T(128)} %sources.1) | copy-start | bytes 1540
  1.6 8.0 %collective-permute-start = (f32[128,128]{1,0:T(8,128)S(1)}, f32[128,128]{1,0:T(8,128)S(1)}, u32[]{:S(2)}, u32[]{:S(2)}) collective-permute-start(f32[128,128]{1,0:T(8,128)S(1)} %constant_dynamic-slice_fusion.beside._), channel_id=1, source_target_pairs={{0,2},{2,0},{1,3},{3,1},{4,6},{6,4},{5,7},{7,5},{8,10},{10,8},{9,1... | collective-permute-start | bytes 196616 | tf_op jit(solution)/shard_map/ppermute | solution.py:544
  9.7 19.8 %collective-permute-start.1 = (bf16[2048,128]{1,0:T(8,128)(2,1)S(1)}, bf16[2048,128]{1,0:T(8,128)(2,1)S(1)}, u32[]{:S(2)}, u32[]{:S(2)}) collective-permute-start(bf16[2048,128]{1,0:T(8,128)(2,1)S(1)} %whiten_outer.1.after.refs_0_), channel_id=1, source_target_pairs={{0,2},{2,0},{1,3},{3,1},{4,6},{6,4},{5,7},{7,5},{8,10},{10,8},{9,1... | collective-permute-start | bytes 1572872 | tf_op jit(solution)/shard_map/ppermute | solution.py:544
  11.6 8.5 %collective-permute-start.5 = (bf16[16,4096]{1,0:T(8,128)(2,1)S(1)}, bf16[16,4096]{1,0:T(8,128)(2,1)S(1)}, u32[]{:S(2)}, u32[]{:S(2)}) collective-permute-start(bf16[16,4096]{1,0:T(8,128)(2,1)S(1)} %whiten_slots.1.refs_0_._), channel_id=1, source_target_pairs={{0,1},{1,0},{2,3},{3,2},{4,5},{5,4},{6,7},{7,6},{8,9},{9,8},{10,11... | collective-permute-start | bytes 393224 | tf_op jit(solution)/shard_map/ppermute | solution.py:544
  11.7 10.0 %collective-permute-start.4 = (bf16[16,4096]{1,0:T(8,128)(2,1)S(1)}, bf16[16,4096]{1,0:T(8,128)(2,1)S(1)}, u32[]{:S(2)}, u32[]{:S(2)}) collective-permute-start(bf16[16,4096]{1,0:T(8,128)(2,1)S(1)} %whiten_slots.1.refs_0_._), channel_id=1, source_target_pairs={{0,12},{4,0},{8,4},{12,8},{1,13},{5,1},{9,5},{13,9},{2,14},{6,2},{... | collective-permute-start | bytes 393224 | tf_op jit(solution)/shard_map/ppermute | solution.py:544
  15.8 12.1 %collective-permute-start.3 = (bf16[16,4096]{1,0:T(8,128)(2,1)S(1)}, bf16[16,4096]{1,0:T(8,128)(2,1)S(1)}, u32[]{:S(2)}, u32[]{:S(2)}) collective-permute-start(bf16[16,4096]{1,0:T(8,128)(2,1)S(1)} %whiten_slots.1.refs_0_._), channel_id=1, source_target_pairs={{0,8},{4,12},{8,0},{12,4},{1,9},{5,13},{9,1},{13,5},{2,10},{6,14},... | collective-permute-start | bytes 393224 | tf_op jit(solution)/shard_map/ppermute | solution.py:544
  15.9 12.1 %collective-permute-start.2 = (bf16[16,4096]{1,0:T(8,128)(2,1)S(1)}, bf16[16,4096]{1,0:T(8,128)(2,1)S(1)}, u32[]{:S(2)}, u32[]{:S(2)}) collective-permute-start(bf16[16,4096]{1,0:T(8,128)(2,1)S(1)} %whiten_slots.1.refs_0_._), channel_id=1, source_target_pairs={{0,4},{4,8},{8,12},{12,0},{1,5},{5,9},{9,13},{13,1},{2,6},{6,10},{... | collective-permute-start | bytes 393224 | tf_op jit(solution)/shard_map/ppermute | solution.py:544
  20.1 21.1 %collective-permute-start.10 = (bf16[2048,128]{1,0:T(8,128)(2,1)S(1)}, bf16[2048,128]{1,0:T(8,128)(2,1)S(1)}, u32[]{:S(2)}, u32[]{:S(2)}) collective-permute-start(bf16[2048,128]{1,0:T(8,128)(2,1)S(1)} %whiten_inner.1.refs_1_.refs_2_.refs_3_), channel_id=1, source_target_pairs={{0,2},{2,0},{1,3},{3,1},{4,6},{6,4},{5,7},{7,5},{8,10},{10,8},{9,1... | collective-permute-start | bytes 1572872 | tf_op jit(solution)/shard_map/ppermute | solution.py:544
  21.7 6.8 %collective-permute-start.8 = (bf16[16,4096]{1,0:T(8,128)(2,1)S(1)}, bf16[16,4096]{1,0:T(8,128)(2,1)S(1)}, u32[]{:S(2)}, u32[]{:S(2)}) collective-permute-start(bf16[16,4096]{1,0:T(8,128)(2,1)S(1)} %collective-permute-done.4.refs_3_), channel_id=1, source_target_pairs={{0,1},{1,0},{2,3},{3,2},{4,5},{5,4},{6,7},{7,6},{8,9},{9,8},{10,11... | collective-permute-start | bytes 393224 | tf_op jit(solution)/shard_map/ppermute | solution.py:544
  27.9 1.3 %collective-permute-start.7 = (bf16[16,4096]{1,0:T(8,128)(2,1)S(1)}, bf16[16,4096]{1,0:T(8,128)(2,1)S(1)}, u32[]{:S(2)}, u32[]{:S(2)}) collective-permute-start(bf16[16,4096]{1,0:T(8,128)(2,1)S(1)} %collective-permute-done.3.refs_2_), channel_id=1, source_target_pairs={{0,1},{1,0},{2,3},{3,2},{4,5},{5,4},{6,7},{7,6},{8,9},{9,8},{10,11... | collective-permute-start | bytes 393224 | tf_op jit(solution)/shard_map/ppermute | solution.py:544
  27.9 1.5 %collective-permute-start.6 = (bf16[16,4096]{1,0:T(8,128)(2,1)S(1)}, bf16[16,4096]{1,0:T(8,128)(2,1)S(1)}, u32[]{:S(2)}, u32[]{:S(2)}) collective-permute-start(bf16[16,4096]{1,0:T(8,128)(2,1)S(1)} %collective-permute-done.2.refs_1_), channel_id=1, source_target_pairs={{0,1},{1,0},{2,3},{3,2},{4,5},{5,4},{6,7},{7,6},{8,9},{9,8},{10,11... | collective-permute-start | bytes 393224 | tf_op jit(solution)/shard_map/ppermute | solution.py:544
  29.8 11.4 %collective-permute-start.9 = (bf16[32,4096]{1,0:T(8,128)(2,1)S(1)}, bf16[32,4096]{1,0:T(8,128)(2,1)S(1)}, u32[]{:S(2)}, u32[]{:S(2)}) collective-permute-start(bf16[32,4096]{1,0:T(8,128)(2,1)S(1)} %get-tuple-element.25), channel_id=1, source_target_pairs={{0,2},{2,0},{1,3},{3,1},{4,6},{6,4},{5,7},{7,5},{8,10},{10,8},{9,1... | collective-permute-start | bytes 786440 | tf_op jit(solution)/shard_map/ppermute | solution.py:544
  41.2 1.6 %collective-permute-start.11 = (bf16[32,4096]{1,0:T(8,128)(2,1)S(1)}, bf16[32,4096]{1,0:T(8,128)(2,1)S(1)}, u32[]{:S(2)}, u32[]{:S(2)}) collective-permute-start(bf16[32,4096]{1,0:T(8,128)(2,1)S(1)} %collective-permute-done.9.refs_0_), channel_id=1, source_target_pairs={{0,1},{1,0},{2,3},{3,2},{4,5},{5,4},{6,7},{7,6},{8,9},{9,8},{10,11... | collective-permute-start | bytes 786440 | tf_op jit(solution)/shard_map/ppermute | solution.py:544

commit v5 on v4

--- a/solution.py
+++ b/solution.py
@@ -119,21 +119,7 @@
     return at
 
 
-def prepare_kernel(sizes, chans, ring, slots, sources, sources_row, filters, _, rows, sets, chan_taps, wanted, same):
-    taps = filters.shape[0]
-    first_chan = place_of(("chan", "sub"), sizes[1:]) * chans
-    for s in range(slots):
-        rows[s] = 0
-
-    def find(p, count):
-        local = sources[p] - first_chan
-        mine = (local >= 0) & (local < chans)
-        rows[jnp.where(mine, count, slots)] = local
-        return count + mine.astype(jnp.int32)
-
-    lax.fori_loop(0, sources.shape[0], find, 0, unroll=16)
-    split_taps(filters, sets, taps)
-    chan_taps[...] = jnp.concatenate([filters[...], jnp.zeros((TILE - taps, chans), F32)], 0).T
+def choose_rows(sizes, chans, ring, slots, sources_row, wanted):
     partners = sources_row.shape[1]
     _, chan_devs, sub_devs = sizes
     own_row = jnp.broadcast_to(sources_row[...].astype(F32), (partners, partners))
@@ -158,6 +144,25 @@
     wanted[...] = (place * slots + rank == at).astype(F32)
 
 
+def prepare_kernel(sizes, chans, ring, slots, sources, sources_row, filters, _, rows, sets, chan_taps, same, *wanted):
+    taps = filters.shape[0]
+    first_chan = place_of(("chan", "sub"), sizes[1:]) * chans
+    for s in range(slots):
+        rows[s] = 0
+
+    def find(p, count):
+        local = sources[p] - first_chan
+        mine = (local >= 0) & (local < chans)
+        rows[jnp.where(mine, count, slots)] = local
+        return count + mine.astype(jnp.int32)
+
+    lax.fori_loop(0, sources.shape[0], find, 0, unroll=16)
+    split_taps(filters, sets, taps)
+    chan_taps[...] = jnp.concatenate([filters[...], jnp.zeros((TILE - taps, chans), F32)], 0).T
+    if not ring:
+        choose_rows(sizes, chans, ring, slots, sources_row, wanted[0])
+
+
 def prepare(sizes, sources, filters, traces, slots, ring):
     taps, chans = filters.shape
     partners = sources.shape[0]
@@ -168,12 +173,12 @@
             jax.ShapeDtypeStruct((slots + 1,), jnp.int32),
             jax.ShapeDtypeStruct((9 * SETS, chans), F32),
             jax.ShapeDtypeStruct((chans, TILE), F32),
-            jax.ShapeDtypeStruct((partners, total), F32),
             jax.ShapeDtypeStruct(traces.shape, F32),
+            *[jax.ShapeDtypeStruct((partners, total), F32)] * (not ring),
         ),
         in_specs=[SMEM] + vmem(2) + [ANY],
-        out_specs=(SMEM, *vmem(3), ANY),
-        input_output_aliases={3: 4},
+        out_specs=(SMEM, *vmem(2), ANY, *vmem(not ring)),
+        input_output_aliases={3: 3},
         compiler_params=params(),
         cost_estimate=light(),
         name="prepare",
@@ -275,8 +280,11 @@
     )(traces, low, high, sets)
 
 
-def whiten_part_kernel(taps, rows, inner, x, sets, beside, _, *refs):
+def whiten_part_kernel(taps, rows, inner, sizes, x, sets, beside, _, *refs):
     outs, (tall, *work) = refs[:-4], refs[-4:]
+    if inner:
+        other, sources_row, *outs, full, wanted = outs
+        choose_rows(sizes, x.shape[0], True, MOST, sources_row, wanted)
     length, size = x.shape[1], tall.shape[0] - 2 * TILE
     half = (taps - 1) // 2
     tiles = rows // TILE
@@ -296,6 +304,12 @@
     for t in range(tiles + 1):
         turn(t)
 
+    if inner:
+        edge = jnp.zeros((TILE, tall.shape[1]), BF16)
+        full[0:TILE, :] = edge
+        full[TILE + length :, :] = edge
+        place = pl.multiple_of(TILE + jnp.where(at_start, size, 0), TILE)
+        full[pl.ds(place, length - size), :] = other[...]
     done = 0
     for out in outs:
 
@@ -303,6 +317,8 @@
             at = pl.multiple_of(i * rows, rows)
             value = fir(tall, sets, *work, at + TILE - half, rows, counts).astype(BF16)
             out[pl.ds(at - done, rows), :] = value
+            if inner:
+                full[pl.ds(pl.multiple_of(TILE + start + at, TILE), rows), :] = value
             for t in range(tiles):
                 turn(jnp.minimum((i + 1) * tiles + 1 + t, size // TILE - 1))
             return carry
@@ -311,20 +327,25 @@
         done += out.shape[0]
 
 
-def whiten_part(taps, traces, sets, beside, after, pieces, inner):
+def whiten_part(taps, traces, sets, beside, after, pieces, inner, sizes, other=()):
     chans = traces.shape[0]
     size = sum(pieces)
+    full = [traces.shape[1] + 2 * TILE] if inner else []
+    extra = ()
+    if inner:
+        partners = other[1].shape[1]
+        extra = (jax.ShapeDtypeStruct((partners, MOST * sizes[1] * sizes[2]), F32),)
     rows = 2 * TILE
     return pl.pallas_call(
-        functools.partial(whiten_part_kernel, taps, rows, inner),
-        out_shape=tuple(jax.ShapeDtypeStruct((piece, chans), BF16) for piece in pieces),
-        in_specs=vmem(3) + [ANY],
-        out_specs=tuple(vmem(len(pieces))),
+        functools.partial(whiten_part_kernel, taps, rows, inner, sizes),
+        out_shape=tuple(jax.ShapeDtypeStruct((piece, chans), BF16) for piece in (*pieces, *full)) + extra,
+        in_specs=vmem(3) + [ANY] + vmem(len(other)),
+        out_specs=tuple(vmem(len(pieces) + len(full) + len(extra))),
         scratch_shapes=[pltpu.VMEM((size + 2 * TILE, chans), F32)] + fir_scratch(rows, chans),
         compiler_params=params(),
         cost_estimate=light(),
         name="whiten_inner" if inner else "whiten_outer",
-    )(traces, sets, beside, after)
+    )(traces, sets, beside, after, *other)
 
 
 def order_kernel(ring, count, choose, after, *refs):
@@ -487,16 +508,10 @@
     return copies
 
 
-def first_kernel(chunk, count, part, *refs):
-    pieces, (total, chan, a, b, c, d, sems) = refs[:count], refs[count:]
+def first_kernel(chunk, part, chan, total, a, b, c, d):
     length = part.shape[1] - 2 * TILE
-    here = lax.axis_index("tm")
-    ready = place_pieces(here == 0, pieces, chan, length, sems)
-    edge = jnp.zeros((TILE, chan.shape[1]), BF16)
-    chan[0:TILE, :] = edge
-    chan[TILE + length :, :] = edge
-    start = pl.multiple_of(here * TILE, TILE)
-    correlate_ring(part, chan, total, (a, b, c, d), start, length, chunk, part.shape[0], ready, None, None, None, sems)
+    start = pl.multiple_of(lax.axis_index("tm") * TILE, TILE)
+    correlate_ring(part, chan, total, (a, b, c, d), start, length, chunk, part.shape[0], (), None, None, None, None)
 
 
 def second_kernel(chunk, scale, count, own_part, *refs):
@@ -554,20 +569,20 @@
     scale = 1.0 / math.sqrt(length * time_devs)
     chunk = 4 * TILE
     taps = filters.T
-    ring = time_devs == 2 and sub_devs == 2 and chan_devs <= 4 and chans % TILE == 0
+    ring = time_devs == 2 and sub_devs == 2 and chan_devs <= 4 and slots == MOST and chans % TILE == 0
     out_shape = jax.ShapeDtypeStruct((LAGS * rows, chans), F32)
     count = taps.shape[0]
-    slot_rows, sets, chan_taps, choose, held = prepare(sizes, sources, taps, traces, slots, ring)
+    slot_rows, sets, chan_taps, held, *choose = prepare(sizes, sources, taps, traces, slots, ring)
     if ring:
         here = lax.axis_index("tm")
         edge = lax.dynamic_slice_in_dim(traces, jnp.where(here == 0, length - TILE, 0), TILE, 1)
         beside = shifted(edge, "tm", 1)
         far = length // 2
-        outer = whiten_part(count, held, sets, edge, edge, (far,), False)
+        outer = whiten_part(count, held, sets, edge, edge, (far,), False, sizes)
         beside, *outer = lax.optimization_barrier((beside, *outer))
         other_outer = [shifted(piece, "tm", 1) for piece in outer]
         picked = whiten_slots(sizes, count, slot_rows, held, beside, beside, chan_taps, outer[0], slots)
-        inner = whiten_part(count, held, sets, beside, picked, (length - far,), True)
+        *inner, own_chan, choose = whiten_part(count, held, sets, beside, picked, (length - far,), True, sizes, (*outer, sources.reshape(1, partners)))
         other_inner = [shifted(piece, "tm", 1) for piece in inner]
         mine = [picked] + [shifted(picked, "chan", step) for step in range(1, chan_devs)]
         theirs = [shifted(part, "sub", 1) for part in mine]
@@ -575,17 +590,15 @@
         near_rows = [shifted(part, "tm", 1) for part in send]
         pieces = len(outer) + len(inner)
         before = pl.pallas_call(
-            functools.partial(first_kernel, chunk, pieces),
+            functools.partial(first_kernel, chunk),
             out_shape=out_shape,
-            in_specs=vmem(1) + [ANY] * pieces,
+            in_specs=vmem(2),
             out_specs=vmem(1)[0],
-            scratch_shapes=[pltpu.VMEM((length + 2 * TILE, chans), BF16)]
-            + spare(rows, (chunk, chunk, chunk, chunk + TILE))
-            + [pltpu.SemaphoreType.DMA((4 + pieces,))],
+            scratch_shapes=spare(rows, (chunk, chunk, chunk, chunk + TILE)),
             compiler_params=params(),
             cost_estimate=light(),
             name="correlate_own",
-        )(own_part, *outer, *inner)
+        )(own_part, own_chan)
         near_rows, other_inner, before = lax.optimization_barrier((near_rows, other_inner, before))
         far_rows = [shifted(part, "sub", 1) for part in near_rows]
         total = pl.pallas_call(
@@ -610,7 +623,7 @@
         picked = whiten_slots(sizes, count, slot_rows, held, low, high, chan_taps, low, slots)
         whitened = whiten(time_devs, count, traces, low, high, sets)
         gathered = lax.all_gather(picked, ("chan", "sub"), axis=0, tiled=True)
-        all_parts = order(choose, low, [gathered], False)
+        all_parts = order(choose[0], low, [gathered], False)
         parts = lax.all_to_all(all_parts, "tm", 0, 1, tiled=True)
         all_chans = lax.all_gather(whitened, "tm", axis=0, tiled=True)
         full = length * time_devs

time: 55.1 us -> 54.7 us (level)
  no operation moved by 1% of the time
where the time goes in v5:
time: 54.7 us; the launch traced here: 54.6 us
  Pallas kernels  32.2 us (59%)
  starting transfers between devices  12.1 us (22%)
  waiting for transfers between devices  8.43 us (15%)
  local copies, waits for them, and re-layouts  1.61 us (3%)
    ppermute x12, starting transfers between devices, shifted(): lax.ppermute(array, axis, [(i, (i + step) % count) for i in range(count)])  12.1 us
    pallas_call x1, Pallas kernels, on_device(): pl.pallas_call(functools.partial(second_kernel, chunk, scale, pieces), ou...  12 us
    pallas_call x1, Pallas kernels, on_device(): pl.pallas_call(functools.partial(first_kernel, chunk), out_shape=out_shap...  9.39 us
    ppermute x12, waiting for transfers between devices, shifted(): lax.ppermute(array, axis, [(i, (i + step) % count) for i in range(count)])  8.43 us
    pallas_call x2, Pallas kernels, whiten_part(): pl.pallas_call(functools.partial(whiten_part_kernel, taps, rows, inner, s...  6.98 us
    pallas_call x1, Pallas kernels, whiten_slots(): pl.pallas_call(functools.partial(slots_kernel, taps, sizes), out_shape=ja...  1.85 us
    pallas_call x1, Pallas kernels, prepare(): pl.pallas_call(functools.partial(prepare_kernel, sizes, chans, ring, slot...  1.65 us
    unnamed x5, local copies, waits for them, and re-layouts  1.6 us
  transfers between devices with their start and end apart: 12, of which 4 were waited for; matrix products, arithmetic and copies ran while one was open for 0% of the time, Pallas kernels for 37%

profile of v5, /device:TPU:0, one launch (start us, length us, event | category | flops | bytes accessed | tf_op | source)
XLA Modules:
  0.0 54.6 jit_solution(343375173842240276)
XLA Ops:
  0.0 1.6 %copy.7._ = f32[128,4096]{1,0:T(8,128)S(1)} copy(f32[128,4096]{1,0:T(8,128)} %param.3) | data formatting | bytes 4194304
  1.6 3.0 %collective-permute-start = (f32[128,128]{1,0:T(8,128)S(1)}, f32[128,128]{1,0:T(8,128)S(1)}, u32[]{:S(2)}, u32[]{:S(2)}) collective-permute-start(f32[128,128]{1,0:T(8,128)S(1)} %constant_dynamic-slice_fusion.beside._), channel_id=1, source_target_pairs={{0,2},{2,0},{1,3},{3,1},{4,6},{6,4},{5,7},{7,5},{8,10},{10,8},{9,1... | collective-permute-start | bytes 196616 | tf_op jit(solution)/shard_map/ppermute | solution.py:559
  4.6 1.7 %prepare.1 = (s32[17]{0:T(128)S(1)}, f32[216,128]{1,0:T(8,128)S(1)}, f32[128,128]{1,0:T(8,128)S(1)}, f32[128,4096]{1,0:T(8,128)S(1)}) custom-call(s32[128]{0:T(128)S(1)} %copy-done.1, s32[1,128]{1,0:T(1,128)S(1)} %bitcast.6, f32[65,128]{1,0:T(8,128)S(1)} %bitcast.5, f32[128,4096]{1,0:T(8,128)S(1)} %copy.7._), custom_call_target="tpu_custom_call", output_to_operand_aliasing={{3}: (3, {})} | custom-call | flops 1000 | bytes 1000 | tf_op jit(solution)/shard_map/prepare/pallas_call | solution.py:170
  6.3 3.4 %whiten_outer.1.after.refs_0_ = bf16[2048,128]{1,0:T(8,128)(2,1)S(1)} custom-call(f32[128,4096]{1,0:T(8,128)S(1)} %get-tuple-element.19.x, f32[216,128]{1,0:T(8,128)S(1)} %get-tuple-element.20.sets, f32[128,128]{1,0:T(8,128)S(1)} %constant_dynamic-slice_fusion.beside._, f32[128,128]{1,0:T(8,128)S(1)} %constant_dynamic-slice_fusion.beside._), custom_call_target="tpu_custom_call" | custom-call | flops 1000 | bytes 1000 | tf_op jit(solution)/shard_map/whiten_outer/pallas_call | solution.py:339
  9.7 0.0 collective-permute-done.low.high.beside
  9.7 0.1 collective-permute-start.1
  9.8 1.9 %whiten_slots.1._.refs_0_ = bf16[16,4096]{1,0:T(8,128)(2,1)S(1)} custom-call(s32[17]{0:T(128)S(1)} %get-tuple-element.22.rows, f32[128,4096]{1,0:T(8,128)S(1)} %get-tuple-element.19.x, f32[128,128]{1,0:T(8,128)S(1)} %collective-permute-done.low.high.beside, f32[128,128]{1,0:T(8,128)S(1)} %collective-permute-done.low.high.beside, ...), custom_call_target="tpu_custom_call" | custom-call | flops 1000 | bytes 1000 | tf_op jit(solution)/shard_map/whiten_slots/pallas_call | solution.py:227
  11.6 0.1 collective-permute-start.5
  11.7 4.2 %collective-permute-start.4 = (bf16[16,4096]{1,0:T(8,128)(2,1)S(1)}, bf16[16,4096]{1,0:T(8,128)(2,1)S(1)}, u32[]{:S(2)}, u32[]{:S(2)}) collective-permute-start(bf16[16,4096]{1,0:T(8,128)(2,1)S(1)} %whiten_slots.1._.refs_0_), channel_id=1, source_target_pairs={{0,12},{4,0},{8,4},{12,8},{1,13},{5,1},{9,5},{13,9},{2,14},{6,2},{... | collective-permute-start | bytes 393224 | tf_op jit(solution)/shard_map/ppermute | solution.py:559
  15.9 0.0 collective-permute-start.3
  15.9 1.0 %collective-permute-start.2 = (bf16[16,4096]{1,0:T(8,128)(2,1)S(1)}, bf16[16,4096]{1,0:T(8,128)(2,1)S(1)}, u32[]{:S(2)}, u32[]{:S(2)}) collective-permute-start(bf16[16,4096]{1,0:T(8,128)(2,1)S(1)} %whiten_slots.1._.refs_0_), channel_id=1, source_target_pairs={{0,4},{4,8},{8,12},{12,0},{1,5},{5,9},{9,13},{13,1},{2,6},{6,10},{... | collective-permute-start | bytes 393224 | tf_op jit(solution)/shard_map/ppermute | solution.py:559
  16.9 3.6 %whiten_inner.1 = (bf16[2048,128]{1,0:T(8,128)(2,1)S(1)}, bf16[4352,128]{1,0:T(8,128)(2,1)S(1)}, f32[128,128]{1,0:T(8,128)S(1)}) custom-call(f32[128,4096]{1,0:T(8,128)S(1)} %get-tuple-element.19.x, f32[216,128]{1,0:T(8,128)S(1)} %get-tuple-element.20.sets, f32[128,128]{1,0:T(8,128)S(1)} %collective-permute-done.low.high.beside, ...), custom_call_target="tpu_custom_call" | custom-call | flops 1000 | bytes 1000 | tf_op jit(solution)/shard_map/whiten_inner/pallas_call | solution.py:339
  20.5 0.0 collective-permute-done.5.refs_4_
  20.5 1.6 %collective-permute-start.10 = (bf16[2048,128]{1,0:T(8,128)(2,1)S(1)}, bf16[2048,128]{1,0:T(8,128)(2,1)S(1)}, u32[]{:S(2)}, u32[]{:S(2)}) collective-permute-start(bf16[2048,128]{1,0:T(8,128)(2,1)S(1)} %get-tuple-element.28.refs_2_.refs_3_), channel_id=1, source_target_pairs={{0,2},{2,0},{1,3},{3,1},{4,6},{6,4},{5,7},{7,5},{8,10},{10,8},{9,1... | collective-permute-start | bytes 1572872 | tf_op jit(solution)/shard_map/ppermute | solution.py:559
  22.1 5.9 %collective-permute-done.3.refs_2_ = bf16[16,4096]{1,0:T(8,128)(2,1)S(1)} collective-permute-done((bf16[16,4096]{1,0:T(8,128)(2,1)S(1)}, bf16[16,4096]{1,0:T(8,128)(2,1)S(1)}, u32[]{:S(2)}, u32[]{:S(2)}) %collective-permute-start.3) | collective-permute-done | bytes 131104 | tf_op jit(solution)/shard_map/ppermute | solution.py:559
  28.0 0.5 collective-permute-start.6
  28.5 0.8 %collective-permute-done.7.refs_6_ = bf16[16,4096]{1,0:T(8,128)(2,1)S(1)} collective-permute-done((bf16[16,4096]{1,0:T(8,128)(2,1)S(1)}, bf16[16,4096]{1,0:T(8,128)(2,1)S(1)}, u32[]{:S(2)}, u32[]{:S(2)}) %collective-permute-start.7) | collective-permute-done | bytes 131104 | tf_op jit(solution)/shard_map/ppermute | solution.py:559
  29.3 0.2 collective-permute-done.6.refs_5_
  29.5 0.4 order_partners.1
  29.9 1.6 %collective-permute-start.9 = (bf16[32,4096]{1,0:T(8,128)(2,1)S(1)}, bf16[32,4096]{1,0:T(8,128)(2,1)S(1)}, u32[]{:S(2)}, u32[]{:S(2)}) collective-permute-start(bf16[32,4096]{1,0:T(8,128)(2,1)S(1)} %get-tuple-element.27), channel_id=1, source_target_pairs={{0,2},{2,0},{1,3},{3,1},{4,6},{6,4},{5,7},{7,5},{8,10},{10,8},{9,1... | collective-permute-start | bytes 786440 | tf_op jit(solution)/shard_map/ppermute | solution.py:559
  31.4 9.4 %correlate_own.1.refs_4_ = f32[8256,128]{1,0:T(8,128)S(1)} custom-call(bf16[64,4352]{1,0:T(8,128)(2,1)S(1)} %get-tuple-element.26.part.own_part, bf16[4352,128]{1,0:T(8,128)(2,1)S(1)} %get-tuple-element.29.chan), custom_call_target="tpu_custom_call" | custom-call | flops 1000 | bytes 1000 | tf_op jit(solution)/shard_map/correlate_own/pallas_call | solution.py:592
  40.9 0.1 collective-permute-start.11
  41.0 1.5 %collective-permute-done.11.refs_1_ = bf16[32,4096]{1,0:T(8,128)(2,1)S(1)} collective-permute-done((bf16[32,4096]{1,0:T(8,128)(2,1)S(1)}, bf16[32,4096]{1,0:T(8,128)(2,1)S(1)}, u32[]{:S(2)}, u32[]{:S(2)}) %collective-permute-start.11) | collective-permute-done | bytes 262176 | tf_op jit(solution)/shard_map/ppermute | solution.py:559
  42.5 12.0 %correlate_other.1 = f32[8256,128]{1,0:T(8,128)} custom-call(bf16[64,4352]{1,0:T(8,128)(2,1)S(1)} %get-tuple-element.26.part.own_part, bf16[32,4096]{1,0:T(8,128)(2,1)S(1)} %collective-permute-done.9.refs_0_, bf16[32,4096]{1,0:T(8,128)(2,1)S(1)} %collective-permute-done.11.refs_1_, bf16[2048,128]{1,0:T(8,128)(2,1)S(1)} %get-tuple-element.28.refs_2_.refs_3_, ...), custom_call_target="tpu_custom_call" | custom-call | flops 1000 | bytes 1000 | tf_op jit(solution)/shard_map/correlate_other/pallas_call | solution.py:604
  (13 shorter events, 0.0 us)
Async XLA Ops:
  0.0 4.6 %copy-start = (f32[128,65]{0,1:T(8,128)S(1)}, f32[128,65]{0,1:T(8,128)}, u32[]{:S(2)}) copy-start(f32[128,65]{0,1:T(8,128)} %param.4) | copy-start | bytes 99844
  0.0 4.6 %copy-start.1 = (s32[128]{0:T(128)S(1)}, s32[128]{0:T(128)}, u32[]{:S(2)}) copy-start(s32[128]{0:T(128)} %sources.1) | copy-start | bytes 1540
  1.6 8.1 %collective-permute-start = (f32[128,128]{1,0:T(8,128)S(1)}, f32[128,128]{1,0:T(8,128)S(1)}, u32[]{:S(2)}, u32[]{:S(2)}) collective-permute-start(f32[128,128]{1,0:T(8,128)S(1)} %constant_dynamic-slice_fusion.beside._), channel_id=1, source_target_pairs={{0,2},{2,0},{1,3},{3,1},{4,6},{6,4},{5,7},{7,5},{8,10},{10,8},{9,1... | collective-permute-start | bytes 196616 | tf_op jit(solution)/shard_map/ppermute | solution.py:559
  9.7 19.8 %collective-permute-start.1 = (bf16[2048,128]{1,0:T(8,128)(2,1)S(1)}, bf16[2048,128]{1,0:T(8,128)(2,1)S(1)}, u32[]{:S(2)}, u32[]{:S(2)}) collective-permute-start(bf16[2048,128]{1,0:T(8,128)(2,1)S(1)} %whiten_outer.1.after.refs_0_), channel_id=1, source_target_pairs={{0,2},{2,0},{1,3},{3,1},{4,6},{6,4},{5,7},{7,5},{8,10},{10,8},{9,1... | collective-permute-start | bytes 1572872 | tf_op jit(solution)/shard_map/ppermute | solution.py:559
  11.6 8.9 %collective-permute-start.5 = (bf16[16,4096]{1,0:T(8,128)(2,1)S(1)}, bf16[16,4096]{1,0:T(8,128)(2,1)S(1)}, u32[]{:S(2)}, u32[]{:S(2)}) collective-permute-start(bf16[16,4096]{1,0:T(8,128)(2,1)S(1)} %whiten_slots.1._.refs_0_), channel_id=1, source_target_pairs={{0,1},{1,0},{2,3},{3,2},{4,5},{5,4},{6,7},{7,6},{8,9},{9,8},{10,11... | collective-permute-start | bytes 393224 | tf_op jit(solution)/shard_map/ppermute | solution.py:559
  11.7 10.3 %collective-permute-start.4 = (bf16[16,4096]{1,0:T(8,128)(2,1)S(1)}, bf16[16,4096]{1,0:T(8,128)(2,1)S(1)}, u32[]{:S(2)}, u32[]{:S(2)}) collective-permute-start(bf16[16,4096]{1,0:T(8,128)(2,1)S(1)} %whiten_slots.1._.refs_0_), channel_id=1, source_target_pairs={{0,12},{4,0},{8,4},{12,8},{1,13},{5,1},{9,5},{13,9},{2,14},{6,2},{... | collective-permute-start | bytes 393224 | tf_op jit(solution)/shard_map/ppermute | solution.py:559
  15.9 12.1 %collective-permute-start.3 = (bf16[16,4096]{1,0:T(8,128)(2,1)S(1)}, bf16[16,4096]{1,0:T(8,128)(2,1)S(1)}, u32[]{:S(2)}, u32[]{:S(2)}) collective-permute-start(bf16[16,4096]{1,0:T(8,128)(2,1)S(1)} %whiten_slots.1._.refs_0_), channel_id=1, source_target_pairs={{0,8},{4,12},{8,0},{12,4},{1,9},{5,13},{9,1},{13,5},{2,10},{6,14},... | collective-permute-start | bytes 393224 | tf_op jit(solution)/shard_map/ppermute | solution.py:559
  15.9 12.1 %collective-permute-start.2 = (bf16[16,4096]{1,0:T(8,128)(2,1)S(1)}, bf16[16,4096]{1,0:T(8,128)(2,1)S(1)}, u32[]{:S(2)}, u32[]{:S(2)}) collective-permute-start(bf16[16,4096]{1,0:T(8,128)(2,1)S(1)} %whiten_slots.1._.refs_0_), channel_id=1, source_target_pairs={{0,4},{4,8},{8,12},{12,0},{1,5},{5,9},{9,13},{13,1},{2,6},{6,10},{... | collective-permute-start | bytes 393224 | tf_op jit(solution)/shard_map/ppermute | solution.py:559
  20.5 20.3 %collective-permute-start.10 = (bf16[2048,128]{1,0:T(8,128)(2,1)S(1)}, bf16[2048,128]{1,0:T(8,128)(2,1)S(1)}, u32[]{:S(2)}, u32[]{:S(2)}) collective-permute-start(bf16[2048,128]{1,0:T(8,128)(2,1)S(1)} %get-tuple-element.28.refs_2_.refs_3_), channel_id=1, source_target_pairs={{0,2},{2,0},{1,3},{3,1},{4,6},{6,4},{5,7},{7,5},{8,10},{10,8},{9,1... | collective-permute-start | bytes 1572872 | tf_op jit(solution)/shard_map/ppermute | solution.py:559
  22.1 6.4 %collective-permute-start.8 = (bf16[16,4096]{1,0:T(8,128)(2,1)S(1)}, bf16[16,4096]{1,0:T(8,128)(2,1)S(1)}, u32[]{:S(2)}, u32[]{:S(2)}) collective-permute-start(bf16[16,4096]{1,0:T(8,128)(2,1)S(1)} %collective-permute-done.4.refs_3_), channel_id=1, source_target_pairs={{0,1},{1,0},{2,3},{3,2},{4,5},{5,4},{6,7},{7,6},{8,9},{9,8},{10,11... | collective-permute-start | bytes 393224 | tf_op jit(solution)/shard_map/ppermute | solution.py:559
  28.0 1.3 %collective-permute-start.7 = (bf16[16,4096]{1,0:T(8,128)(2,1)S(1)}, bf16[16,4096]{1,0:T(8,128)(2,1)S(1)}, u32[]{:S(2)}, u32[]{:S(2)}) collective-permute-start(bf16[16,4096]{1,0:T(8,128)(2,1)S(1)} %collective-permute-done.3.refs_2_), channel_id=1, source_target_pairs={{0,1},{1,0},{2,3},{3,2},{4,5},{5,4},{6,7},{7,6},{8,9},{9,8},{10,11... | collective-permute-start | bytes 393224 | tf_op jit(solution)/shard_map/ppermute | solution.py:559
  28.0 1.5 %collective-permute-start.6 = (bf16[16,4096]{1,0:T(8,128)(2,1)S(1)}, bf16[16,4096]{1,0:T(8,128)(2,1)S(1)}, u32[]{:S(2)}, u32[]{:S(2)}) collective-permute-start(bf16[16,4096]{1,0:T(8,128)(2,1)S(1)} %collective-permute-done.2.refs_1_), channel_id=1, source_target_pairs={{0,1},{1,0},{2,3},{3,2},{4,5},{5,4},{6,7},{7,6},{8,9},{9,8},{10,11... | collective-permute-start | bytes 393224 | tf_op jit(solution)/shard_map/ppermute | solution.py:559
  29.9 11.0 %collective-permute-start.9 = (bf16[32,4096]{1,0:T(8,128)(2,1)S(1)}, bf16[32,4096]{1,0:T(8,128)(2,1)S(1)}, u32[]{:S(2)}, u32[]{:S(2)}) collective-permute-start(bf16[32,4096]{1,0:T(8,128)(2,1)S(1)} %get-tuple-element.27), channel_id=1, source_target_pairs={{0,2},{2,0},{1,3},{3,1},{4,6},{6,4},{5,7},{7,5},{8,10},{10,8},{9,1... | collective-permute-start | bytes 786440 | tf_op jit(solution)/shard_map/ppermute | solution.py:559
  40.9 1.6 %collective-permute-start.11 = (bf16[32,4096]{1,0:T(8,128)(2,1)S(1)}, bf16[32,4096]{1,0:T(8,128)(2,1)S(1)}, u32[]{:S(2)}, u32[]{:S(2)}) collective-permute-start(bf16[32,4096]{1,0:T(8,128)(2,1)S(1)} %collective-permute-done.9.refs_0_), channel_id=1, source_target_pairs={{0,1},{1,0},{2,3},{3,2},{4,5},{5,4},{6,7},{7,6},{8,9},{9,8},{10,11... | collective-permute-start | bytes 786440 | tf_op jit(solution)/shard_map/ppermute | solution.py:559

commit v6 on v5

--- a/solution.py
+++ b/solution.py
@@ -144,19 +144,8 @@
     wanted[...] = (place * slots + rank == at).astype(F32)
 
 
-def prepare_kernel(sizes, chans, ring, slots, sources, sources_row, filters, _, rows, sets, chan_taps, same, *wanted):
+def prepare_kernel(sizes, chans, ring, slots, sources_row, filters, _, sets, chan_taps, same, *wanted):
     taps = filters.shape[0]
-    first_chan = place_of(("chan", "sub"), sizes[1:]) * chans
-    for s in range(slots):
-        rows[s] = 0
-
-    def find(p, count):
-        local = sources[p] - first_chan
-        mine = (local >= 0) & (local < chans)
-        rows[jnp.where(mine, count, slots)] = local
-        return count + mine.astype(jnp.int32)
-
-    lax.fori_loop(0, sources.shape[0], find, 0, unroll=16)
     split_taps(filters, sets, taps)
     chan_taps[...] = jnp.concatenate([filters[...], jnp.zeros((TILE - taps, chans), F32)], 0).T
     if not ring:
@@ -170,27 +159,37 @@
     return pl.pallas_call(
         functools.partial(prepare_kernel, sizes, chans, ring, slots),
         out_shape=(
-            jax.ShapeDtypeStruct((slots + 1,), jnp.int32),
             jax.ShapeDtypeStruct((9 * SETS, chans), F32),
             jax.ShapeDtypeStruct((chans, TILE), F32),
             jax.ShapeDtypeStruct(traces.shape, F32),
             *[jax.ShapeDtypeStruct((partners, total), F32)] * (not ring),
         ),
-        in_specs=[SMEM] + vmem(2) + [ANY],
-        out_specs=(SMEM, *vmem(2), ANY, *vmem(not ring)),
-        input_output_aliases={3: 3},
+        in_specs=vmem(2) + [ANY],
+        out_specs=(*vmem(2), ANY, *vmem(not ring)),
+        input_output_aliases={2: 2},
         compiler_params=params(),
         cost_estimate=light(),
         name="prepare",
-    )(sources, sources.reshape(1, partners), filters, traces)
-
-
-def slots_kernel(taps, sizes, rows, x, low, high, chan_taps, after, out, wide, tall, lane_taps, *work):
+    )(sources.reshape(1, partners), filters, traces)
+
+
+def slots_kernel(taps, sizes, sources, x, low, high, chan_taps, after, out, rows, wide, tall, lane_taps, *work):
     chans, length = x.shape
     slots = out.shape[0]
     segs = TILE // slots
     seg_len = length // segs
     half = (taps - 1) // 2
+    first_chan = place_of(("chan", "sub"), sizes[1:]) * chans
+    for s in range(slots):
+        rows[s] = 0
+
+    def find(p, count):
+        local = sources[p] - first_chan
+        mine = (local >= 0) & (local < chans)
+        rows[jnp.where(mine, count, slots)] = local
+        return count + mine.astype(jnp.int32)
+
+    lax.fori_loop(0, sources.shape[0], find, 0, unroll=16)
     here = lax.axis_index("tm")
     keep_low = (here > 0).astype(F32)
     keep_high = (here < sizes[0] - 1).astype(F32)
@@ -230,6 +229,7 @@
         in_specs=[SMEM] + vmem(4) + [ANY],
         out_specs=vmem(1)[0],
         scratch_shapes=[
+            pltpu.SMEM((slots + 1,), jnp.int32),
             pltpu.VMEM((slots, length + 2 * TILE), F32),
             pltpu.VMEM((seg_len + 2 * TILE, TILE), F32),
             pltpu.VMEM((TILE, TILE), F32),
@@ -572,7 +572,7 @@
     ring = time_devs == 2 and sub_devs == 2 and chan_devs <= 4 and slots == MOST and chans % TILE == 0
     out_shape = jax.ShapeDtypeStruct((LAGS * rows, chans), F32)
     count = taps.shape[0]
-    slot_rows, sets, chan_taps, held, *choose = prepare(sizes, sources, taps, traces, slots, ring)
+    sets, chan_taps, held, *choose = prepare(sizes, sources, taps, traces, slots, ring)
     if ring:
         here = lax.axis_index("tm")
         edge = lax.dynamic_slice_in_dim(traces, jnp.where(here == 0, length - TILE, 0), TILE, 1)
@@ -581,7 +581,7 @@
         outer = whiten_part(count, held, sets, edge, edge, (far,), False, sizes)
         beside, *outer = lax.optimization_barrier((beside, *outer))
         other_outer = [shifted(piece, "tm", 1) for piece in outer]
-        picked = whiten_slots(sizes, count, slot_rows, held, beside, beside, chan_taps, outer[0], slots)
+        picked = whiten_slots(sizes, count, sources, held, beside, beside, chan_taps, outer[0], slots)
         *inner, own_chan, choose = whiten_part(count, held, sets, beside, picked, (length - far,), True, sizes, (*outer, sources.reshape(1, partners)))
         other_inner = [shifted(piece, "tm", 1) for piece in inner]
         mine = [picked] + [shifted(picked, "chan", step) for step in range(1, chan_devs)]
@@ -620,7 +620,7 @@
     else:
         low = lax.ppermute(traces[:, length - TILE :], "tm", [(i, i + 1) for i in range(time_devs - 1)])
         high = lax.ppermute(traces[:, :TILE], "tm", [(i + 1, i) for i in range(time_devs - 1)])
-        picked = whiten_slots(sizes, count, slot_rows, held, low, high, chan_taps, low, slots)
+        picked = whiten_slots(sizes, count, sources, held, low, high, chan_taps, low, slots)
         whitened = whiten(time_devs, count, traces, low, high, sets)
         gathered = lax.all_gather(picked, ("chan", "sub"), axis=0, tiled=True)
         all_parts = order(choose[0], low, [gathered], False)

time: 54.7 us -> 53.7 us (0.982)
  Pallas kernels: 32.2 us -> 31.3 us
    pallas_call x1, Pallas kernels: 1.65 us -> 0.13 us  [prepare(): pl.pallas_call(functools.partial(prepare_kernel, sizes, chans, ring, slot...]
  transfers between devices with their start and end apart: 12 -> 12, of which waited for: 4 -> 4; matrix products, arithmetic and copies ran while one was open for 0% -> 0% of each run, Pallas kernels for 37% -> 36%
where the time goes in v6:
time: 53.7 us; the launch traced here: 53.6 us
  Pallas kernels  31.3 us (58%)
  starting transfers between devices  12 us (22%)
  waiting for transfers between devices  8.48 us (16%)
  local copies, waits for them, and re-layouts  1.61 us (3%)
    ppermute x12, starting transfers between devices, shifted(): lax.ppermute(array, axis, [(i, (i + step) % count) for i in range(count)])  12 us
    pallas_call x1, Pallas kernels, on_device(): pl.pallas_call(functools.partial(second_kernel, chunk, scale, pieces), ou...  12 us
    pallas_call x1, Pallas kernels, on_device(): pl.pallas_call(functools.partial(first_kernel, chunk), out_shape=out_shap...  9.39 us
    ppermute x12, waiting for transfers between devices, shifted(): lax.ppermute(array, axis, [(i, (i + step) % count) for i in range(count)])  8.48 us
    pallas_call x2, Pallas kernels, whiten_part(): pl.pallas_call(functools.partial(whiten_part_kernel, taps, rows, inner, s...  7.05 us
    pallas_call x1, Pallas kernels, whiten_slots(): pl.pallas_call(functools.partial(slots_kernel, taps, sizes), out_shape=ja...  2.37 us
    unnamed x5, local copies, waits for them, and re-layouts  1.6 us
  transfers between devices with their start and end apart: 12, of which 4 were waited for; matrix products, arithmetic and copies ran while one was open for 0% of the time, Pallas kernels for 36%

profile of v6, /device:TPU:0, one launch (start us, length us, event | category | flops | bytes accessed | tf_op | source)
XLA Modules:
  0.0 53.6 jit_solution(4692277436333810944)
XLA Ops:
  0.0 1.6 %copy.7._ = f32[128,4096]{1,0:T(8,128)S(1)} copy(f32[128,4096]{1,0:T(8,128)} %param.3) | data formatting | bytes 4194304
  1.6 3.0 %collective-permute-start = (f32[128,128]{1,0:T(8,128)S(1)}, f32[128,128]{1,0:T(8,128)S(1)}, u32[]{:S(2)}, u32[]{:S(2)}) collective-permute-start(f32[128,128]{1,0:T(8,128)S(1)} %constant_dynamic-slice_fusion.beside._), channel_id=1, source_target_pairs={{0,2},{2,0},{1,3},{3,1},{4,6},{6,4},{5,7},{7,5},{8,10},{10,8},{9,1... | collective-permute-start | bytes 196616 | tf_op jit(solution)/shard_map/ppermute | solution.py:559
  4.6 0.1 prepare.1
  4.8 3.4 %whiten_outer.1.after.refs_0_ = bf16[2048,128]{1,0:T(8,128)(2,1)S(1)} custom-call(f32[128,4096]{1,0:T(8,128)S(1)} %get-tuple-element.18.x, f32[216,128]{1,0:T(8,128)S(1)} %get-tuple-element.19.sets, f32[128,128]{1,0:T(8,128)S(1)} %constant_dynamic-slice_fusion.beside._, f32[128,128]{1,0:T(8,128)S(1)} %constant_dynamic-slice_fusion.beside._), custom_call_target="tpu_custom_call" | custom-call | flops 1000 | bytes 1000 | tf_op jit(solution)/shard_map/whiten_outer/pallas_call | solution.py:339
  8.2 0.0 collective-permute-done.low.high.beside
  8.2 0.7 %collective-permute-start.1 = (bf16[2048,128]{1,0:T(8,128)(2,1)S(1)}, bf16[2048,128]{1,0:T(8,128)(2,1)S(1)}, u32[]{:S(2)}, u32[]{:S(2)}) collective-permute-start(bf16[2048,128]{1,0:T(8,128)(2,1)S(1)} %whiten_outer.1.after.refs_0_), channel_id=1, source_target_pairs={{0,2},{2,0},{1,3},{3,1},{4,6},{6,4},{5,7},{7,5},{8,10},{10,8},{9,1... | collective-permute-start | bytes 1572872 | tf_op jit(solution)/shard_map/ppermute | solution.py:559
  8.9 2.4 %whiten_slots.1._.refs_0_ = bf16[16,4096]{1,0:T(8,128)(2,1)S(1)} custom-call(s32[128]{0:T(128)S(1)} %copy-done.1, f32[128,4096]{1,0:T(8,128)S(1)} %get-tuple-element.18.x, f32[128,128]{1,0:T(8,128)S(1)} %collective-permute-done.low.high.beside, f32[128,128]{1,0:T(8,128)S(1)} %collective-permute-done.low.high.beside, ...), custom_call_target="tpu_custom_call" | custom-call | flops 1000 | bytes 1000 | tf_op jit(solution)/shard_map/whiten_slots/pallas_call | solution.py:226
  11.3 0.1 collective-permute-start.5
  11.3 3.7 %collective-permute-start.4 = (bf16[16,4096]{1,0:T(8,128)(2,1)S(1)}, bf16[16,4096]{1,0:T(8,128)(2,1)S(1)}, u32[]{:S(2)}, u32[]{:S(2)}) collective-permute-start(bf16[16,4096]{1,0:T(8,128)(2,1)S(1)} %whiten_slots.1._.refs_0_), channel_id=1, source_target_pairs={{0,12},{4,0},{8,4},{12,8},{1,13},{5,1},{9,5},{13,9},{2,14},{6,2},{... | collective-permute-start | bytes 393224 | tf_op jit(solution)/shard_map/ppermute | solution.py:559
  15.0 0.0 collective-permute-start.3
  15.0 1.0 %collective-permute-start.2 = (bf16[16,4096]{1,0:T(8,128)(2,1)S(1)}, bf16[16,4096]{1,0:T(8,128)(2,1)S(1)}, u32[]{:S(2)}, u32[]{:S(2)}) collective-permute-start(bf16[16,4096]{1,0:T(8,128)(2,1)S(1)} %whiten_slots.1._.refs_0_), channel_id=1, source_target_pairs={{0,4},{4,8},{8,12},{12,0},{1,5},{5,9},{9,13},{13,1},{2,6},{6,10},{... | collective-permute-start | bytes 393224 | tf_op jit(solution)/shard_map/ppermute | solution.py:559
  16.0 3.6 %whiten_inner.1 = (bf16[2048,128]{1,0:T(8,128)(2,1)S(1)}, bf16[4352,128]{1,0:T(8,128)(2,1)S(1)}, f32[128,128]{1,0:T(8,128)S(1)}) custom-call(f32[128,4096]{1,0:T(8,128)S(1)} %get-tuple-element.18.x, f32[216,128]{1,0:T(8,128)S(1)} %get-tuple-element.19.sets, f32[128,128]{1,0:T(8,128)S(1)} %collective-permute-done.low.high.beside, ...), custom_call_target="tpu_custom_call" | custom-call | flops 1000 | bytes 1000 | tf_op jit(solution)/shard_map/whiten_inner/pallas_call | solution.py:339
  19.7 1.4 %collective-permute-start.10 = (bf16[2048,128]{1,0:T(8,128)(2,1)S(1)}, bf16[2048,128]{1,0:T(8,128)(2,1)S(1)}, u32[]{:S(2)}, u32[]{:S(2)}) collective-permute-start(bf16[2048,128]{1,0:T(8,128)(2,1)S(1)} %get-tuple-element.26.refs_2_.refs_3_), channel_id=1, source_target_pairs={{0,2},{2,0},{1,3},{3,1},{4,6},{6,4},{5,7},{7,5},{8,10},{10,8},{9,1... | collective-permute-start | bytes 1572872 | tf_op jit(solution)/shard_map/ppermute | solution.py:559
  21.1 6.0 %collective-permute-done.3.refs_2_ = bf16[16,4096]{1,0:T(8,128)(2,1)S(1)} collective-permute-done((bf16[16,4096]{1,0:T(8,128)(2,1)S(1)}, bf16[16,4096]{1,0:T(8,128)(2,1)S(1)}, u32[]{:S(2)}, u32[]{:S(2)}) %collective-permute-start.3) | collective-permute-done | bytes 131104 | tf_op jit(solution)/shard_map/ppermute | solution.py:559
  27.1 0.0 collective-permute-done.2.refs_1_
  27.1 0.5 collective-permute-start.6
  27.6 0.8 %collective-permute-done.7.refs_6_ = bf16[16,4096]{1,0:T(8,128)(2,1)S(1)} collective-permute-done((bf16[16,4096]{1,0:T(8,128)(2,1)S(1)}, bf16[16,4096]{1,0:T(8,128)(2,1)S(1)}, u32[]{:S(2)}, u32[]{:S(2)}) %collective-permute-start.7) | collective-permute-done | bytes 131104 | tf_op jit(solution)/shard_map/ppermute | solution.py:559
  28.4 0.2 collective-permute-done.6.refs_5_
  28.6 0.4 order_partners.1
  29.0 1.4 %collective-permute-start.9 = (bf16[32,4096]{1,0:T(8,128)(2,1)S(1)}, bf16[32,4096]{1,0:T(8,128)(2,1)S(1)}, u32[]{:S(2)}, u32[]{:S(2)}) collective-permute-start(bf16[32,4096]{1,0:T(8,128)(2,1)S(1)} %get-tuple-element.25), channel_id=1, source_target_pairs={{0,2},{2,0},{1,3},{3,1},{4,6},{6,4},{5,7},{7,5},{8,10},{10,8},{9,1... | collective-permute-start | bytes 786440 | tf_op jit(solution)/shard_map/ppermute | solution.py:559
  30.4 9.4 %correlate_own.1.refs_4_ = f32[8256,128]{1,0:T(8,128)S(1)} custom-call(bf16[64,4352]{1,0:T(8,128)(2,1)S(1)} %get-tuple-element.24.part.own_part, bf16[4352,128]{1,0:T(8,128)(2,1)S(1)} %get-tuple-element.27.chan), custom_call_target="tpu_custom_call" | custom-call | flops 1000 | bytes 1000 | tf_op jit(solution)/shard_map/correlate_own/pallas_call | solution.py:592
  39.8 0.1 collective-permute-start.11
  40.0 1.5 %collective-permute-done.11.refs_1_ = bf16[32,4096]{1,0:T(8,128)(2,1)S(1)} collective-permute-done((bf16[32,4096]{1,0:T(8,128)(2,1)S(1)}, bf16[32,4096]{1,0:T(8,128)(2,1)S(1)}, u32[]{:S(2)}, u32[]{:S(2)}) %collective-permute-start.11) | collective-permute-done | bytes 262176 | tf_op jit(solution)/shard_map/ppermute | solution.py:559
  41.4 12.0 %correlate_other.1 = f32[8256,128]{1,0:T(8,128)} custom-call(bf16[64,4352]{1,0:T(8,128)(2,1)S(1)} %get-tuple-element.24.part.own_part, bf16[32,4096]{1,0:T(8,128)(2,1)S(1)} %collective-permute-done.9.refs_0_, bf16[32,4096]{1,0:T(8,128)(2,1)S(1)} %collective-permute-done.11.refs_1_, bf16[2048,128]{1,0:T(8,128)(2,1)S(1)} %get-tuple-element.26.refs_2_.refs_3_, ...), custom_call_target="tpu_custom_call" | custom-call | flops 1000 | bytes 1000 | tf_op jit(solution)/shard_map/correlate_other/pallas_call | solution.py:604
  (13 shorter events, 0.0 us)
Async XLA Ops:
  0.0 4.6 %copy-start = (f32[128,65]{0,1:T(8,128)S(1)}, f32[128,65]{0,1:T(8,128)}, u32[]{:S(2)}) copy-start(f32[128,65]{0,1:T(8,128)} %param.4) | copy-start | bytes 99844
  0.0 4.6 %copy-start.1 = (s32[128]{0:T(128)S(1)}, s32[128]{0:T(128)}, u32[]{:S(2)}) copy-start(s32[128]{0:T(128)} %sources.1) | copy-start | bytes 1540
  1.6 6.5 %collective-permute-start = (f32[128,128]{1,0:T(8,128)S(1)}, f32[128,128]{1,0:T(8,128)S(1)}, u32[]{:S(2)}, u32[]{:S(2)}) collective-permute-start(f32[128,128]{1,0:T(8,128)S(1)} %constant_dynamic-slice_fusion.beside._), channel_id=1, source_target_pairs={{0,2},{2,0},{1,3},{3,1},{4,6},{6,4},{5,7},{7,5},{8,10},{10,8},{9,1... | collective-permute-start | bytes 196616 | tf_op jit(solution)/shard_map/ppermute | solution.py:559
  8.2 20.4 %collective-permute-start.1 = (bf16[2048,128]{1,0:T(8,128)(2,1)S(1)}, bf16[2048,128]{1,0:T(8,128)(2,1)S(1)}, u32[]{:S(2)}, u32[]{:S(2)}) collective-permute-start(bf16[2048,128]{1,0:T(8,128)(2,1)S(1)} %whiten_outer.1.after.refs_0_), channel_id=1, source_target_pairs={{0,2},{2,0},{1,3},{3,1},{4,6},{6,4},{5,7},{7,5},{8,10},{10,8},{9,1... | collective-permute-start | bytes 1572872 | tf_op jit(solution)/shard_map/ppermute | solution.py:559
  11.3 8.4 %collective-permute-start.5 = (bf16[16,4096]{1,0:T(8,128)(2,1)S(1)}, bf16[16,4096]{1,0:T(8,128)(2,1)S(1)}, u32[]{:S(2)}, u32[]{:S(2)}) collective-permute-start(bf16[16,4096]{1,0:T(8,128)(2,1)S(1)} %whiten_slots.1._.refs_0_), channel_id=1, source_target_pairs={{0,1},{1,0},{2,3},{3,2},{4,5},{5,4},{6,7},{7,6},{8,9},{9,8},{10,11... | collective-permute-start | bytes 393224 | tf_op jit(solution)/shard_map/ppermute | solution.py:559
  11.3 9.8 %collective-permute-start.4 = (bf16[16,4096]{1,0:T(8,128)(2,1)S(1)}, bf16[16,4096]{1,0:T(8,128)(2,1)S(1)}, u32[]{:S(2)}, u32[]{:S(2)}) collective-permute-start(bf16[16,4096]{1,0:T(8,128)(2,1)S(1)} %whiten_slots.1._.refs_0_), channel_id=1, source_target_pairs={{0,12},{4,0},{8,4},{12,8},{1,13},{5,1},{9,5},{13,9},{2,14},{6,2},{... | collective-permute-start | bytes 393224 | tf_op jit(solution)/shard_map/ppermute | solution.py:559
  15.0 12.1 %collective-permute-start.3 = (bf16[16,4096]{1,0:T(8,128)(2,1)S(1)}, bf16[16,4096]{1,0:T(8,128)(2,1)S(1)}, u32[]{:S(2)}, u32[]{:S(2)}) collective-permute-start(bf16[16,4096]{1,0:T(8,128)(2,1)S(1)} %whiten_slots.1._.refs_0_), channel_id=1, source_target_pairs={{0,8},{4,12},{8,0},{12,4},{1,9},{5,13},{9,1},{13,5},{2,10},{6,14},... | collective-permute-start | bytes 393224 | tf_op jit(solution)/shard_map/ppermute | solution.py:559
  15.0 12.1 %collective-permute-start.2 = (bf16[16,4096]{1,0:T(8,128)(2,1)S(1)}, bf16[16,4096]{1,0:T(8,128)(2,1)S(1)}, u32[]{:S(2)}, u32[]{:S(2)}) collective-permute-start(bf16[16,4096]{1,0:T(8,128)(2,1)S(1)} %whiten_slots.1._.refs_0_), channel_id=1, source_target_pairs={{0,4},{4,8},{8,12},{12,0},{1,5},{5,9},{9,13},{13,1},{2,6},{6,10},{... | collective-permute-start | bytes 393224 | tf_op jit(solution)/shard_map/ppermute | solution.py:559
  19.7 20.2 %collective-permute-start.10 = (bf16[2048,128]{1,0:T(8,128)(2,1)S(1)}, bf16[2048,128]{1,0:T(8,128)(2,1)S(1)}, u32[]{:S(2)}, u32[]{:S(2)}) collective-permute-start(bf16[2048,128]{1,0:T(8,128)(2,1)S(1)} %get-tuple-element.26.refs_2_.refs_3_), channel_id=1, source_target_pairs={{0,2},{2,0},{1,3},{3,1},{4,6},{6,4},{5,7},{7,5},{8,10},{10,8},{9,1... | collective-permute-start | bytes 1572872 | tf_op jit(solution)/shard_map/ppermute | solution.py:559
  21.1 6.5 %collective-permute-start.8 = (bf16[16,4096]{1,0:T(8,128)(2,1)S(1)}, bf16[16,4096]{1,0:T(8,128)(2,1)S(1)}, u32[]{:S(2)}, u32[]{:S(2)}) collective-permute-start(bf16[16,4096]{1,0:T(8,128)(2,1)S(1)} %collective-permute-done.4.refs_3_), channel_id=1, source_target_pairs={{0,1},{1,0},{2,3},{3,2},{4,5},{5,4},{6,7},{7,6},{8,9},{9,8},{10,11... | collective-permute-start | bytes 393224 | tf_op jit(solution)/shard_map/ppermute | solution.py:559
  27.1 1.3 %collective-permute-start.7 = (bf16[16,4096]{1,0:T(8,128)(2,1)S(1)}, bf16[16,4096]{1,0:T(8,128)(2,1)S(1)}, u32[]{:S(2)}, u32[]{:S(2)}) collective-permute-start(bf16[16,4096]{1,0:T(8,128)(2,1)S(1)} %collective-permute-done.3.refs_2_), channel_id=1, source_target_pairs={{0,1},{1,0},{2,3},{3,2},{4,5},{5,4},{6,7},{7,6},{8,9},{9,8},{10,11... | collective-permute-start | bytes 393224 | tf_op jit(solution)/shard_map/ppermute | solution.py:559
  27.1 1.5 %collective-permute-start.6 = (bf16[16,4096]{1,0:T(8,128)(2,1)S(1)}, bf16[16,4096]{1,0:T(8,128)(2,1)S(1)}, u32[]{:S(2)}, u32[]{:S(2)}) collective-permute-start(bf16[16,4096]{1,0:T(8,128)(2,1)S(1)} %collective-permute-done.2.refs_1_), channel_id=1, source_target_pairs={{0,1},{1,0},{2,3},{3,2},{4,5},{5,4},{6,7},{7,6},{8,9},{9,8},{10,11... | collective-permute-start | bytes 393224 | tf_op jit(solution)/shard_map/ppermute | solution.py:559
  29.0 10.8 %collective-permute-start.9 = (bf16[32,4096]{1,0:T(8,128)(2,1)S(1)}, bf16[32,4096]{1,0:T(8,128)(2,1)S(1)}, u32[]{:S(2)}, u32[]{:S(2)}) collective-permute-start(bf16[32,4096]{1,0:T(8,128)(2,1)S(1)} %get-tuple-element.25), channel_id=1, source_target_pairs={{0,2},{2,0},{1,3},{3,1},{4,6},{6,4},{5,7},{7,5},{8,10},{10,8},{9,1... | collective-permute-start | bytes 786440 | tf_op jit(solution)/shard_map/ppermute | solution.py:559
  39.8 1.6 %collective-permute-start.11 = (bf16[32,4096]{1,0:T(8,128)(2,1)S(1)}, bf16[32,4096]{1,0:T(8,128)(2,1)S(1)}, u32[]{:S(2)}, u32[]{:S(2)}) collective-permute-start(bf16[32,4096]{1,0:T(8,128)(2,1)S(1)} %collective-permute-done.9.refs_0_), channel_id=1, source_target_pairs={{0,1},{1,0},{2,3},{3,2},{4,5},{5,4},{6,7},{7,6},{8,9},{9,8},{10,11... | collective-permute-start | bytes 786440 | tf_op jit(solution)/shard_map/ppermute | solution.py:559
